TPU v7x, 32 devices: a whole 2x2x4 slice. The times are simulated.
32 devices in a mesh: dp: 8 (over z, y), ffn: 4 (over x, core).
Axes of the slice: x: 2, y: 2, z: 4, core: 2. Of those that a mesh axis runs over, the one named last changes fastest.
Arguments:
- item_owner: int32 [8192, 2], P('dp'), may hold values from 0 to 31, all different within a row; in each aligned block of 1024 rows (0 to 1023, 1024 to 2047, ...) at most 128 rows name the same one
- item_row: int32 [8192, 2], P('dp'), may hold values from 0 to 783
- lengths: int32 [16], P('dp'), may hold values from 1 to 512, as said below
- log_count: int32 [25088], P(('dp', 'ffn')), may hold values from 0 to 4
- item_table: float32 [25088, 256], P(('dp', 'ffn'))
- table_mom: float32 [25088, 256], P(('dp', 'ffn')), may hold values from -0.00024414062 to 0.00024414062
- table_sec: float32 [25088, 256], P(('dp', 'ffn')), may hold values from 1.7028116e-10 to 2.7244986e-09
- qkv_weight: float32 [256, 768], replicated, may hold values from -0.375 to 0.375
- qkv_mom: float32 [256, 768], replicated, may hold values from -0.00024414062 to 0.00024414062
- qkv_sec: float32 [256, 768], replicated, may hold values from 1.7028116e-10 to 2.7244986e-09
- out_weight: float32 [256, 256], replicated, may hold values from -2 to 2
- out_mom: float32 [256, 256], replicated, may hold values from -0.00024414062 to 0.00024414062
- out_sec: float32 [256, 256], replicated, may hold values from 1.7028116e-10 to 2.7244986e-09
- ffn_in: float32 [256, 1024], P(None, 'ffn'), may hold values from -0.375 to 0.375
- ffn_in_mom: float32 [256, 1024], P(None, 'ffn'), may hold values from -0.00024414062 to 0.00024414062
- ffn_in_sec: float32 [256, 1024], P(None, 'ffn'), may hold values from 1.7028116e-10 to 2.7244986e-09
- ffn_back: float32 [1024, 256], P('ffn'), may hold values from -0.1875 to 0.1875
- ffn_back_mom: float32 [1024, 256], P('ffn'), may hold values from -0.00024414062 to 0.00024414062
- ffn_back_sec: float32 [1024, 256], P('ffn'), may hold values from 1.7028116e-10 to 2.7244986e-09
- norm_gains: float32 [3, 256], replicated, may hold values from 0.5 to 1.5
- gains_mom: float32 [3, 256], replicated, may hold values from -0.0009765625 to 0.0009765625
- gains_sec: float32 [3, 256], replicated, may hold values from 2.7244986e-09 to 4.3591978e-08
- positions: float32 [512, 256], replicated, may hold values from -1.5 to 1.5
- positions_mom: float32 [512, 256], replicated, may hold values from -0.00024414062 to 0.00024414062
- positions_sec: float32 [512, 256], replicated, may hold values from 1.7028116e-10 to 2.7244986e-09
Outputs:
- loss_parts: float32 [2], replicated
- stream_rms: float32 [3], replicated
- clip_norm: float32 [1], replicated
- new_table: float32 [25088, 256], P(('dp', 'ffn'))
- new_table_mom: float32 [25088, 256], P(('dp', 'ffn'))
- new_table_sec: float32 [25088, 256], P(('dp', 'ffn'))
- new_qkv: float32 [256, 768], replicated
- new_qkv_mom: float32 [256, 768], replicated
- new_qkv_sec: float32 [256, 768], replicated
- new_out: float32 [256, 256], replicated
- new_out_mom: float32 [256, 256], replicated
- new_out_sec: float32 [256, 256], replicated
- new_ffn_in: float32 [256, 1024], P(None, 'ffn')
- new_ffn_in_mom: float32 [256, 1024], P(None, 'ffn')
- new_ffn_in_sec: float32 [256, 1024], P(None, 'ffn')
- new_ffn_back: float32 [1024, 256], P('ffn')
- new_ffn_back_mom: float32 [1024, 256], P('ffn')
- new_ffn_back_sec: float32 [1024, 256], P('ffn')
- new_gains: float32 [3, 256], replicated
- new_gains_mom: float32 [3, 256], replicated
- new_gains_sec: float32 [3, 256], replicated
- new_positions: float32 [512, 256], replicated
- new_positions_mom: float32 [512, 256], replicated
- new_positions_sec: float32 [512, 256], replicated
Inputs may be any that keep to these rules, and one draw needn't show every extreme that they name: `item_owner`: column 0 and column 1 of a slot name different owners. Within the rows of one device no owner is named more than 128 times over both columns, and on some device one owner is named exactly 128 times. An item's owner is device index dp * (devices of ffn) + ffn. `lengths`: A history's valid events are its first slots; some history is full.
All inputs are finite; a program needn't handle non-finite values.
Results may differ from a plain program's by a relative error of at most 0.012.
Values may be sent and summed in bfloat16 or wider, within the bound.
A program may use at most 128 MiB of HBM per device.

v0:
```python
import math

import jax
import jax.numpy as jnp
from jax import lax
from jax.sharding import PartitionSpec as P

D = 256
H = 8
STEP = 5
HD = 32


EPS = 1e-06
NEG = -1e30
LEARN = 0.05
GAIN_LEARN = 0.4
BETA_ONE = 0.5
BETA_TWO = 0.5
DECAY = 0.01
ADAM_EPS = 1e-08
CLIP = 0.05


def combined_all(part, axis, combine):
    gathered = jax.tree.map(lambda a: lax.all_gather(a, axis), part)

    def take(source):
        return jax.tree.map(lambda a: lax.dynamic_index_in_dim(a, source, 0, False), gathered)

    return lax.fori_loop(
        1, lax.axis_size(axis), lambda source, state: combine(state, take(source)), take(0)
    )


def lowered(value):
    return value.astype(jnp.bfloat16)


def against(left, right):
    return lax.dot_general(
        left, right, (((1,), (1,)), ((), ())), preferred_element_type=jnp.float32
    )


def across(left, right):
    return lax.dot_general(
        left, right, (((0,), (0,)), ((), ())), preferred_element_type=jnp.float32
    )


def matmul(left, right):
    return jnp.dot(left, right, preferred_element_type=jnp.float32)


def rms_norm(hidden, gain):
    return hidden * lax.rsqrt(jnp.mean(hidden * hidden, -1, keepdims=True) + EPS) * gain


def rms_back(hidden, gain, upstream):
    factor = lax.rsqrt(jnp.mean(hidden * hidden, -1, keepdims=True) + EPS)
    scaled = upstream * gain
    inner = jnp.mean(scaled * hidden, -1, keepdims=True)
    grad_hidden = factor * scaled - hidden * factor * factor * factor * inner
    grad_gain = jnp.sum(upstream * hidden * factor, 0)
    return (grad_hidden, grad_gain)


def head_split(block):
    return block.reshape(block.shape[0], H, HD)


def score_block(united_seq, length):
    queries = head_split(united_seq[:, :D])
    key_rows = head_split(united_seq[:, D : 2 * D])
    scores = jnp.einsum(
        "qhd,khd->hqk", queries, key_rows, preferred_element_type=jnp.float32
    ) * HD ** (-0.5)
    places = jnp.arange(united_seq.shape[0])
    allowed = (places[None, :] <= places[:, None]) & (places[None, :] < length)
    return (jnp.where(allowed[None], scores, NEG), queries, key_rows)


def attend(pair):
    united_seq, length = pair
    scores, queries, key_rows = score_block(united_seq, length)
    values = head_split(united_seq[:, 2 * D :])
    top = jnp.max(scores, -1, keepdims=True)
    expo = jnp.exp(scores - top)
    total = jnp.sum(expo, -1, keepdims=True)
    probs = expo / total
    mixed = jnp.einsum("hqk,khd->qhd", lowered(probs), values, preferred_element_type=jnp.float32)
    return (mixed.reshape(united_seq.shape[0], D), (top + jnp.log(total))[:, :, 0])


def attend_back(quad):
    united_seq, length, log_total, grad_mixed = quad
    scores, queries, key_rows = score_block(united_seq, length)
    values = head_split(united_seq[:, 2 * D :])
    probs = jnp.exp(scores - log_total[:, :, None])
    grad_heads = head_split(grad_mixed)
    grad_probs = jnp.einsum("qhd,khd->hqk", grad_heads, values, preferred_element_type=jnp.float32)
    grad_values = jnp.einsum(
        "hqk,qhd->khd", lowered(probs), grad_heads, preferred_element_type=jnp.float32
    )
    grad_scores = lowered(probs * (grad_probs - jnp.sum(probs * grad_probs, -1, keepdims=True)))
    grad_queries = jnp.einsum(
        "hqk,khd->qhd", grad_scores, key_rows, preferred_element_type=jnp.float32
    ) * HD ** (-0.5)
    grad_keys = jnp.einsum(
        "hqk,qhd->khd", grad_scores, queries, preferred_element_type=jnp.float32
    ) * HD ** (-0.5)
    width = united_seq.shape[0]
    return jnp.concatenate(
        [
            grad_queries.reshape(width, D),
            grad_keys.reshape(width, D),
            grad_values.reshape(width, D),
        ],
        1,
    )


def combine_totals(first, second):
    top = jnp.maximum(first[0], second[0])
    return (top, first[1] * jnp.exp(first[0] - top) + second[1] * jnp.exp(second[0] - top))


def adam(weight, moment, second, grad, factor, learn_rate):
    clipped = grad * factor
    new_mom = BETA_ONE * moment + (1.0 - BETA_ONE) * clipped
    new_sec = BETA_TWO * second + (1.0 - BETA_TWO) * clipped * clipped
    corr_one = 1.0 - BETA_ONE**STEP
    corr_two = 1.0 - BETA_TWO**STEP
    new_weight = weight - learn_rate * (
        new_mom / corr_one / (jnp.sqrt(new_sec / corr_two) + ADAM_EPS) + DECAY * weight
    )
    return (new_weight, new_mom, new_sec)


def squared(value):
    return jnp.sum(value * value)


def shards(
    item_owner,
    item_row,
    lengths,
    log_count,
    item_table,
    table_mom,
    table_sec,
    qkv_weight,
    qkv_mom,
    qkv_sec,
    out_weight,
    out_mom,
    out_sec,
    ffn_in,
    ffn_in_mom,
    ffn_in_sec,
    ffn_back,
    ffn_back_mom,
    ffn_back_sec,
    norm_gains,
    gains_mom,
    gains_sec,
    positions,
    positions_mom,
    positions_sec,
):
    n_dp = lax.axis_size("dp")
    n_ffn = lax.axis_size("ffn")
    ffn_place = lax.axis_index("ffn")
    dp_place = lax.axis_index("dp")
    tokens = item_owner.shape[0]
    rows_dev = item_table.shape[0]
    width = item_table.shape[1]
    seqs = lengths.shape[0]
    span = tokens // seqs
    capacity = max(2, 4 * tokens // (n_dp * n_ffn))
    quarter = tokens // n_ffn
    flat_owner = item_owner.reshape(-1)
    flat_row = item_row.reshape(-1)
    dest = flat_owner // n_ffn
    mine = flat_owner % n_ffn == ffn_place
    onehot = ((dest[:, None] == jnp.arange(n_dp)[None, :]) & mine[:, None]).astype(jnp.int32)
    slots = jnp.sum((jnp.cumsum(onehot, 0) - onehot) * onehot, 1)
    slots = jnp.where(mine, slots, capacity)
    requests = (
        jnp.full((n_dp, capacity), rows_dev, jnp.int32).at[dest, slots].set(flat_row, mode="drop")
    )
    table_low = lowered(item_table)
    count_low = log_count.astype(jnp.bfloat16)
    asked = lax.all_to_all(requests, "dp", split_axis=0, concat_axis=0, tiled=True)
    safe = jnp.clip(asked, 0, rows_dev - 1)
    found = lax.all_to_all(table_low[safe], "dp", split_axis=0, concat_axis=0, tiled=True)
    found_bias = lax.all_to_all(count_low[safe], "dp", split_axis=0, concat_axis=0, tiled=True)
    picked = jnp.clip(slots, 0, capacity - 1)
    token_rows = jnp.where(mine[:, None], found[dest, picked], 0).astype(jnp.float32)
    token_bias = jnp.where(mine, found_bias[dest, picked], 0).astype(jnp.float32)
    joined_rows, joined_bias = (
        lax.psum(token_rows.reshape(tokens, 2, width).astype(jnp.bfloat16), "ffn").astype(
            jnp.float32
        ),
        lax.psum(token_bias.reshape(tokens, 2).astype(jnp.bfloat16), "ffn").astype(jnp.float32),
    )
    valid = (jnp.arange(span)[None, :] < lengths[:, None]).astype(jnp.float32).reshape(-1)
    target_rows = joined_rows[:, 1]
    target_bias = joined_bias[:, 1]
    hidden0 = (joined_rows[:, 0].reshape(seqs, span, width) + positions[None]).reshape(
        tokens, width
    )
    normed1 = lowered(rms_norm(hidden0, norm_gains[0]))
    qkv_low = lowered(qkv_weight)
    united = lowered(matmul(normed1, qkv_low))
    united_seqs = united.reshape(seqs, span, 3 * width)
    mixed, attn_totals = lax.map(attend, (united_seqs, lengths))
    attn_mid = lowered(mixed.reshape(tokens, width))
    out_low = lowered(out_weight)
    attn_branch = matmul(attn_mid, out_low)
    hidden1 = hidden0 + attn_branch
    normed2 = lowered(rms_norm(hidden1, norm_gains[1]))
    in_low = lowered(ffn_in)
    back_low = lowered(ffn_back)
    pre_act = matmul(normed2, in_low)
    activated = lowered(jax.nn.gelu(pre_act, approximate=True))
    ffn_branch = lax.psum(matmul(activated, back_low), "ffn")
    hidden2 = hidden1 + ffn_branch
    final = lowered(rms_norm(hidden2, norm_gains[2]))
    begin = ffn_place * quarter
    mine_rows = lax.dynamic_slice_in_dim(target_rows, begin, quarter, 0)
    mine_valid = lax.dynamic_slice_in_dim(valid, begin, quarter, 0)
    mine_bias = lax.dynamic_slice_in_dim(target_bias, begin, quarter, 0)
    mine_final = lax.dynamic_slice_in_dim(final, begin, quarter, 0)
    cand_rows = lowered(mine_rows)
    cand_bias = lowered(jnp.where(mine_valid > 0, -mine_bias, NEG))
    all_rows, all_bias = (
        lax.all_gather(cand_rows, "dp", axis=0, tiled=True),
        lax.all_gather(cand_bias, "dp", axis=0, tiled=True),
    )
    total_cands = all_rows.shape[0]
    block = math.gcd(total_cands, 2048)
    row_blocks = all_rows.reshape(total_cands // block, block, width)
    bias_blocks = all_bias.astype(jnp.float32).reshape(total_cands // block, block)

    def total_step(carry, pieces):
        run_max, run_sum = carry
        logits = against(final, pieces[0]) + pieces[1][None, :]
        top = jnp.maximum(run_max, jnp.max(logits, 1))
        run_sum = run_sum * jnp.exp(run_max - top) + jnp.sum(jnp.exp(logits - top[:, None]), 1)
        return ((top, run_sum), None)

    start_max = jnp.full((tokens,), NEG, jnp.float32)
    (part_max, part_sum), unused = lax.scan(
        total_step, (start_max, jnp.zeros((tokens,), jnp.float32)), (row_blocks, bias_blocks)
    )
    glob_max, glob_sum = combined_all((part_max, part_sum), "ffn", combine_totals)
    log_total = glob_max + jnp.log(glob_sum)
    positive = jnp.sum(final.astype(jnp.float32) * target_rows, 1) - target_bias
    stats_local = jnp.stack(
        [
            jnp.sum(valid * (log_total - positive)),
            jnp.sum(valid),
            jnp.sum(valid * jnp.sum(hidden2 * hidden2, 1)),
            jnp.sum(valid * jnp.sum(attn_branch * attn_branch, 1)),
            jnp.sum(valid * jnp.sum(ffn_branch * ffn_branch, 1)),
        ]
    )
    stats = lax.psum(stats_local, "dp")

    def grad_step(carry, pieces):
        logits = against(final, pieces[0]) + pieces[1][None, :]
        weights = lowered(jnp.exp(logits - log_total[:, None]) * valid[:, None])
        return (carry + matmul(weights, pieces[0]), None)

    grad_part, unused = lax.scan(
        grad_step, jnp.zeros((tokens, width), jnp.float32), (row_blocks, bias_blocks)
    )
    grad_final = lax.psum(grad_part, "ffn") - valid[:, None] * target_rows
    inner = math.gcd(quarter * lax.axis_size("dp"), 2048)

    def one_block(number):
        rows_blk = lax.dynamic_slice_in_dim(all_rows, number * inner, inner, 0)
        bias_blk = lax.dynamic_slice_in_dim(all_bias, number * inner, inner, 0).astype(jnp.float32)
        weights = lowered(
            jnp.exp(against(final, rows_blk) + bias_blk[None, :] - log_total[:, None])
            * valid[:, None]
        )
        return across(weights, final)

    cand_grad = lax.psum_scatter(
        lax.map(one_block, jnp.arange(quarter * lax.axis_size("dp") // inner)).reshape(
            quarter * lax.axis_size("dp"), width
        ),
        "dp",
        scatter_dimension=0,
        tiled=True,
    )
    quarter_grad = cand_grad - mine_valid[:, None] * mine_final.astype(jnp.float32)
    target_grad = lax.all_gather(lowered(quarter_grad), "ffn", axis=0, tiled=True)
    grad_h2, grad_gain3 = rms_back(hidden2, norm_gains[2], grad_final)
    ffn_up = lowered(grad_h2)
    grad_ffn_back = across(activated, ffn_up)
    grad_act = against(ffn_up, back_low)
    unused_val, gelu_pull = jax.vjp(
        lambda inner_act: jax.nn.gelu(inner_act, approximate=True), pre_act
    )
    grad_pre = lowered(gelu_pull(grad_act)[0])
    grad_ffn_in = across(normed2, grad_pre)
    grad_normed2 = lax.psum(against(grad_pre, in_low), "ffn")
    grad_h1_norm, grad_gain2 = rms_back(hidden1, norm_gains[1], grad_normed2)
    grad_h1 = grad_h2 + grad_h1_norm
    attn_up = lowered(grad_h1)
    grad_out = across(attn_mid, attn_up)
    grad_mixed = lowered(against(attn_up, out_low))
    grad_united = lax.map(
        attend_back, (united_seqs, lengths, attn_totals, grad_mixed.reshape(seqs, span, width))
    )
    grad_united = lowered(grad_united.reshape(tokens, 3 * width))
    grad_qkv = across(normed1, grad_united)
    grad_h0_norm, grad_gain1 = rms_back(hidden0, norm_gains[0], against(grad_united, qkv_low))
    grad_h0 = grad_h1 + grad_h0_norm
    grad_positions = jnp.sum(grad_h0.reshape(seqs, span, width), 0)
    grad_gains = jnp.stack([grad_gain1, grad_gain2, grad_gain3])
    row_grads = jnp.stack([lowered(grad_h0), target_grad], 1).reshape(2 * tokens, width)
    outgoing = (
        jnp.zeros((n_dp, capacity, width), jnp.bfloat16).at[dest, slots].set(row_grads, mode="drop")
    )
    incoming = lax.all_to_all(outgoing, "dp", split_axis=0, concat_axis=0, tiled=True)
    table_grad = (
        jnp.zeros(item_table.shape, jnp.float32)
        .at[asked.reshape(-1)]
        .add(incoming.reshape(-1, width).astype(jnp.float32), mode="drop")
    )
    grad_qkv, grad_out, grad_ffn_in, grad_ffn_back, grad_gains, grad_positions = lax.psum(
        (grad_qkv, grad_out, grad_ffn_in, grad_ffn_back, grad_gains, grad_positions), "dp"
    )
    first_dp = (dp_place == 0).astype(jnp.float32)
    first_ffn = (ffn_place == 0).astype(jnp.float32)
    shared_sq = (
        squared(grad_qkv) + squared(grad_out) + squared(grad_gains) + squared(grad_positions)
    )
    norm_local = squared(table_grad) + first_dp * (
        squared(grad_ffn_in) + squared(grad_ffn_back) + first_ffn * shared_sq
    )
    norm_sq = lax.psum(norm_local, ("dp", "ffn"))
    norm = jnp.sqrt(norm_sq)
    factor = CLIP / jnp.maximum(norm, CLIP)
    table_new = adam(item_table, table_mom, table_sec, table_grad, factor, LEARN)
    qkv_new = adam(qkv_weight, qkv_mom, qkv_sec, grad_qkv, factor, LEARN)
    out_new = adam(out_weight, out_mom, out_sec, grad_out, factor, LEARN)
    in_new = adam(ffn_in, ffn_in_mom, ffn_in_sec, grad_ffn_in, factor, LEARN)
    back_new = adam(ffn_back, ffn_back_mom, ffn_back_sec, grad_ffn_back, factor, LEARN)
    gains_new = adam(norm_gains, gains_mom, gains_sec, grad_gains, factor, GAIN_LEARN)
    pos_new = adam(positions, positions_mom, positions_sec, grad_positions, factor, LEARN)
    loss_parts = stats[:2]
    stream_rms = jnp.sqrt(stats[2:] / (stats[1] * width))
    return (
        loss_parts,
        stream_rms,
        norm.reshape(1),
        table_new[0],
        table_new[1],
        table_new[2],
        qkv_new[0],
        qkv_new[1],
        qkv_new[2],
        out_new[0],
        out_new[1],
        out_new[2],
        in_new[0],
        in_new[1],
        in_new[2],
        back_new[0],
        back_new[1],
        back_new[2],
        gains_new[0],
        gains_new[1],
        gains_new[2],
        pos_new[0],
        pos_new[1],
        pos_new[2],
    )


def solution(mesh):
    placed = (
        P("dp", None),
        P("dp", None),
        P("dp"),
        P(("dp", "ffn")),
        P(("dp", "ffn"), None),
        P(("dp", "ffn"), None),
        P(("dp", "ffn"), None),
        P(),
        P(),
        P(),
        P(),
        P(),
        P(),
        P(None, "ffn"),
        P(None, "ffn"),
        P(None, "ffn"),
        P("ffn", None),
        P("ffn", None),
        P("ffn", None),
        P(),
        P(),
        P(),
        P(),
        P(),
        P(),
    )
    return jax.shard_map(
        shards,
        mesh=mesh,
        in_specs=placed,
        out_specs=(
            P(),
            P(),
            P(),
            P(("dp", "ffn"), None),
            P(("dp", "ffn"), None),
            P(("dp", "ffn"), None),
            P(),
            P(),
            P(),
            P(),
            P(),
            P(),
            P(None, "ffn"),
            P(None, "ffn"),
            P(None, "ffn"),
            P("ffn", None),
            P("ffn", None),
            P("ffn", None),
            P(),
            P(),
            P(),
            P(),
            P(),
            P(),
        ),
        check_vma=False,
    )
```

profile of v0, /device:TPU:0, one launch (start us, length us, event | category | flops | bytes accessed | tf_op | source)
XLA Modules:
  0.0 620.9 jit_solution(5075063267746156349)
XLA Ops:
  9.1 2.3 reduce-window.6
  14.9 8.6 %scatter_custom_fusion.1 = s32[1024]{0:T(1024)} fusion(s32[2048]{0:T(1024)S(1)} %broadcast_select_fusion.1, s32[2048]{0:T(1024)S(1)} %reshape.670, s32[]{:T(128)} %constant.241.clone.1), kind=kCustom, calls=%fused_computation.229 | custom fusion | bytes 4100
  23.5 7.3 %all-to-all-start = ((s32[8,1,128]{2,1,0:T(1,128)}), s32[8,1,128]{2,1,0:T(1,128)S(1)}, u32[]{:S(2)}, u32[]{:S(2)}) async-start(s32[8,1,128]{2,1,0:T(1,128)} %bitcast.26), calls=%async_computation | async-start | bytes 8192 | tf_op jit(solution)/shard_map/all_to_all | solution.py:195
  31.5 5.7 all-to-all-done
  37.2 6.8 %gather_fusion.2 = bf16[1024]{0:T(1024)(128)(2,1)S(1)} fusion(bf16[784]{0:T(1024)(128)(2,1)S(1)} %convert_element_type.165, s32[1024]{0:T(1024)S(1)} %fusion.86), kind=kCustom, calls=%fused_computation.2 | custom fusion | bytes 8192 | tf_op jit(solution)/shard_map/gather | solution.py:198
  44.6 3.3 all-to-all-start.2
  49.1 5.0 gather_fusion
  54.3 5.8 all-to-all-start.1
  60.4 16.2 %gather_fusion.3 = bf16[2048]{0:T(1024)(128)(2,1)S(1)} fusion(bf16[8,128]{1,0:T(8,128)(2,1)S(1)} %bitcast.219, s32[2048]{0:T(1024)S(1)} %bitcast.220), kind=kCustom, calls=%fused_computation.3 | custom fusion | bytes 24576 | tf_op jit(solution)/shard_map/gather | solution.py:201
  78.4 11.1 %gather_fusion.1 = bf16[2048,256]{1,0:T(8,128)(2,1)S(1)} fusion(bf16[8,128,256]{2,1,0:T(8,128)(2,1)S(1)} %all-to-all-done.1, s32[2048]{0:T(1024)S(1)} %bitcast.221), kind=kCustom, calls=%fused_computation.1 | custom fusion | bytes 2113536 | tf_op jit(solution)/shard_map/gather | solution.py:200
  90.8 2.4 copy_select_fusion
  93.4 37.4 %all-reduce.8.cloned.1.call-done = bf16[1024,2,256]{2,0,1:T(8,128)(2,1)} async-done(((bf16[1024,2,256]{2,0,1:T(8,128)(2,1)}), bf16[1024,2,256]{2,0,1:T(8,128)(2,1)}) %all-reduce.8.cloned.1.call-update) | async-done | bytes 1048592 | tf_op jit(solution)/shard_map/psum | solution.py:203
  135.5 16.5 %while.10 = (s32[]{:T(128)}, bf16[2,512,256]{2,1,0:T(8,128)(2,1)}, f32[2,8,512]{2,1,0:T(8,128)S(1)}, bf16[2,512,768]{1,2,0:T(8,128)(2,1)S(1)}, s32[2]{0:T(128)S(1)}, /*index=5*/s32[]{:T(128)}) while((s32[]{:T(128)}, bf16[2,512,256]{2,1,0:T(8,128)(2,1)}, f32[2,8,512]{2,1,0:T(8,128)S(1)}, bf16[2,512,768]{1,2,0:T(8,128)(2,1)S(1)}, ...), condition=%wide.region_9.10_spmd, body=%wide.region_6.9_spmd.sunk | while | flops 294121984 | bytes 35783840 | solution.py:218
  140.4 2.4 fusion.156
  148.7 2.4 fusion.156
  152.1 2.1 multiply_reduce_fusion.10
  155.5 2.5 fusion.63
  158.9 18.0 %psum.93 = bf16[1024,2]{1,0:T(8,128)(2,1)S(1)} all-reduce(bf16[1024,2]{1,0:T(8,128)(2,1)} %get-tuple-element.417), channel_id=1, replica_groups=mesh['dp'=8,'ffn'=4] {'ffn'}, use_global_device_ids=true, to_apply=%region_13.14 | all-reduce | flops 2048 | bytes 8192 | tf_op jit(solution)/shard_map/psum | solution.py:206
  177.3 20.5 %all-gather.2 = bf16[8,1,256]{2,1,0:T(2,128)(2,1)S(1)} all-gather(bf16[1,1,256]{2,1,0:T(2,128)(2,1)S(1)} %reshape.693), channel_id=1, replica_groups=mesh['dp'=8,'ffn'=4] {'dp'}, dimensions={0}, use_global_device_ids=true | all-gather | bytes 4608 | tf_op jit(solution)/shard_map/all_gather | solution.py:240
  202.3 37.4 %all-gather.6.cloned.1.call-done = bf16[2048,1,256]{2,0,1:T(8,128)(2,1)} async-done(((bf16[256,1,256]{2,0,1:T(8,128)(2,1)}), bf16[2048,1,256]{2,0,1:T(8,128)(2,1)}) %all-gather.6.cloned.1.call-update) | async-done | bytes 1048592 | tf_op jit(solution)/shard_map/all_gather | solution.py:239
  239.7 2.6 add_reduce_fusion
  242.3 3.2 copy-done
  245.5 1.9 exponential_reduce_fusion
  247.4 5.2 all-gather.3
  252.6 5.6 all-gather.1
  259.0 4.3 multiply_convert_fusion.1
  263.3 1.9 copy-done.13
  265.3 2.3 fusion.27
  267.6 34.9 %all-reduce.12.cloned.1.call-done = f32[1024,256]{1,0:T(8,128)} async-done(((f32[1024,256]{1,0:T(8,128)}), f32[1024,256]{1,0:T(8,128)}) %all-reduce.12.cloned.1.call-update) | async-done | bytes 1048592 | tf_op jit(solution)/shard_map/psum | solution.py:280
  302.5 2.4 multiply_reduce_fusion.1
  307.5 2.2 fusion.19
  311.9 2.2 fusion.24
  314.1 4.9 fusion.104
  319.1 2.8 fusion.49
  321.9 2.3 fusion.90
  324.2 24.2 %all-reduce.14.cloned.1.call-done = f32[1024,256]{1,0:T(8,128)} async-done(((f32[1024,256]{1,0:T(8,128)}), f32[1024,256]{1,0:T(8,128)}) %all-reduce.14.cloned.1.call-update) | async-done | bytes 1048592 | tf_op jit(solution)/shard_map/psum | solution.py:311
  350.1 1.9 subtract_add_fusion.1
  354.2 30.5 %while.12 = (s32[]{:T(128)}, bf16[2,512,768]{2,1,0:T(8,128)(2,1)}, bf16[2,512,768]{1,2,0:T(8,128)(2,1)S(1)}, s32[2]{0:T(128)S(1)}, f32[2,8,512]{2,1,0:T(8,128)S(1)}, /*index=5*/bf16[2,512,256]{2,1,0:T(8,128)(2,1)}, s32[]{:T(128)}) while((s32[]{:T(128)}, bf16[2,512,768]{2,1,0:T(8,128)(2,1)}, bf16[2,512,768]{1,2,0:T(8,128)(2,1)S(1)}, ...), condition=%wide.region_33.34_spmd, body=%wide.region_31.33_spmd.sunk | while | flops 705950208 | bytes 75613296 | solution.py:317
  358.1 2.3 fusion.170
  360.5 3.0 multiply_reduce_fusion.21
  363.5 2.7 multiply_convert_fusion.13
  373.4 2.3 fusion.170
  375.7 3.0 multiply_reduce_fusion.21
  378.7 2.7 multiply_convert_fusion.13
  384.7 2.8 multiply_reduce_fusion.3
  387.6 3.1 convert_bitcast_fusion
  390.6 2.2 reduce_sum.309
  393.8 2.5 fusion.36
  397.1 3.3 stack.44
  400.4 19.5 %reduce-scatter.2.cloned.1.call-done = f32[256,256]{1,0:T(8,128)} async-done(((f32[2048,256]{1,0:T(8,128)}), f32[256,256]{1,0:T(8,128)}) %reduce-scatter.2.cloned.1.call-update) | async-done | bytes 262160 | tf_op jit(solution)/shard_map/reduce_scatter | solution.py:292
  421.0 7.3 %all_gather.21 = bf16[1024,256]{1,0:T(8,128)(2,1)S(1)} all-gather(bf16[256,256]{1,0:T(8,128)(2,1)S(1)} %subtract_convert_fusion), channel_id=1, replica_groups=mesh['dp'=8,'ffn'=4] {'ffn'}, dimensions={0}, use_global_device_ids=true | all-gather | bytes 655360 | tf_op jit(solution)/shard_map/all_gather | solution.py:301
  431.9 10.4 %scatter_custom_fusion.2 = bf16[1024,256]{1,0:T(8,128)(2,1)} fusion(s32[2048]{0:T(1024)} %copy-done.32, bf16[2048,256]{1,0:T(8,128)(2,1)} %reshape.676, bf16[]{:T(256)} %constant.249.clone.1), kind=kCustom, calls=%fused_computation.127 | custom fusion | bytes 524800
  442.3 3.6 all-to-all-start.3
  445.9 30.4 %all-reduce = (f32[5]{0:T(128)S(1)}, f32[3,256]{1,0:T(4,128)S(1)}) all-reduce(f32[5]{0:T(128)S(1)} %stack.44, f32[3,256]{1,0:T(4,128)S(1)} %pad_maximum_fusion.1), channel_id=1, replica_groups=mesh['dp'=8,'ffn'=4] {'dp'}, use_global_device_ids=true, to_apply=%region_26.27 | all-reduce | flops 773 | bytes 6184 | tf_op jit(solution)/shard_map/psum | solution.py:270
  478.1 59.4 %all-reduce.16.cloned.1.call-done = (f32[256,256]{1,0:T(8,128)}, f32[256,256]{1,0:T(8,128)}, f32[256,768]{1,0:T(8,128)}, f32[256,256]{1,0:T(8,128)}, f32[512,256]{1,0:T(8,128)}) async-done(((f32[256,256]{1,0:T(8,128)}, f32[256,256]{1,0:T(8,128)}, f32[256,768]{1,0:T(8,128)}, f32[256,256]{1,0:T(8,128)}, f32[512,256]{1,0:T(8,128)}), (f32[256,256]{1,0:T(8,128)}, f32[256,256]{1,0:T(8,128)}, ...) | async-done | bytes 2097168 | tf_op jit(solution)/shard_map/psum | solution.py:336
  539.1 1.9 multiply_reduce_fusion.13
  543.0 1.8 multiply_reduce_fusion.14
  550.8 6.1 scatter_custom_fusion
  559.0 39.1 %psum.103 = f32[]{:T(128)} all-reduce(f32[]{:T(128)S(6)} %add.469), channel_id=1, replica_groups=mesh['dp'=8,'ffn'=4] {'dp','ffn'}, use_global_device_ids=true, to_apply=%region_55.56 | all-reduce | flops 1 | bytes 8 | tf_op jit(solution)/shard_map/psum | solution.py:347
  599.6 2.2 multiply_subtract_fusion.6
  601.8 2.8 multiply_subtract_fusion.3
  604.5 3.4 multiply_subtract_fusion.2
  608.0 1.9 multiply_subtract_fusion.1
  609.9 2.8 multiply_subtract_fusion.4
  (237 shorter events, 74.1 us)
Async XLA Ops:
  7.2 52.9 %copy-start.29 = (s32[1024,2]{0,1:T(2,128)S(1)}, s32[1024,2]{0,1:T(2,128)}, u32[]{:S(2)}) copy-start(s32[1024,2]{0,1:T(2,128)} %param.31) | copy-start | bytes 24580
  14.9 8.6 %copy-start.32 = (s32[2048]{0:T(1024)}, s32[2048]{0:T(1024)S(1)}, u32[]{:S(2)}) copy-start(s32[2048]{0:T(1024)S(1)} %broadcast_select_fusion.1) | copy-start | bytes 24580
  23.5 13.7 %all-to-all-start = ((s32[8,1,128]{2,1,0:T(1,128)}), s32[8,1,128]{2,1,0:T(1,128)S(1)}, u32[]{:S(2)}, u32[]{:S(2)}) async-start(s32[8,1,128]{2,1,0:T(1,128)} %bitcast.26), calls=%async_computation | async-start | bytes 8192 | tf_op jit(solution)/shard_map/all_to_all | solution.py:195
  37.2 7.4 %copy-start.27 = (s32[8,1,128]{2,1,0:T(1,128)}, s32[8,1,128]{2,1,0:T(1,128)S(1)}, u32[]{:S(2)}) copy-start(s32[8,1,128]{2,1,0:T(1,128)S(1)} %all-to-all-done) | copy-start | bytes 12292
  44.6 9.6 %all-to-all-start.2 = ((bf16[8,1,128]{2,1,0:T(2,128)(2,1)}), bf16[8,1,128]{2,1,0:T(2,128)(2,1)S(1)}, u32[]{:S(2)}, u32[]{:S(2)}) async-start(bf16[8,1,128]{2,1,0:T(2,128)(2,1)} %copy.137), calls=%async_computation.2 | async-start | bytes 8192 | tf_op jit(solution)/shard_map/all_to_all | solution.py:198
  54.3 24.2 %all-to-all-start.1 = ((bf16[8,128,256]{2,1,0:T(8,128)(2,1)}), bf16[8,128,256]{2,1,0:T(8,128)(2,1)S(1)}, u32[]{:S(2)}, u32[]{:S(2)}) async-start(bf16[8,128,256]{2,1,0:T(8,128)(2,1)} %bitcast.29), calls=%async_computation.1 | async-start | bytes 1048576 | tf_op jit(solution)/shard_map/all_to_all | solution.py:197
  60.0 70.8 %all-reduce.8.cloned.1.call-start = ((), (), s32[]{:S(2)}) async-start(), calls=%async_computation.5 | async-start | bytes 2097152 | tf_op jit(solution)/shard_map/psum | solution.py:203
  77.2 16.2 %copy-start.30 = (f32[3,256]{1,0:T(4,128)S(1)}, f32[3,256]{1,0:T(4,128)}, u32[]{:S(2)}) copy-start(f32[3,256]{1,0:T(4,128)} %param.50) | copy-start | bytes 9220
  78.4 55.2 %copy-start.9 = (f32[512,256]{1,0:T(8,128)S(1)}, f32[512,256]{1,0:T(8,128)}, u32[]{:S(2)}) copy-start(f32[512,256]{1,0:T(8,128)} %param.53) | copy-start | bytes 1572868
  78.4 55.4 %copy-start.6 = (f32[256,768]{1,0:T(8,128)S(1)}, f32[256,768]{1,0:T(8,128)}, u32[]{:S(2)}) copy-start(f32[256,768]{1,0:T(8,128)} %param.38) | copy-start | bytes 2359300
  89.5 46.0 %copy-start.35 = (s32[2]{0:T(128)S(1)}, s32[2]{0:T(128)}, u32[]{:S(2)}) copy-start(s32[2]{0:T(128)} %param.33) | copy-start | bytes 28
  93.2 104.9 %all-reduce.10.cloned.1.call-start = ((), (), s32[]{:S(2)}) async-start(), calls=%async_computation.6 | async-start | bytes 2097152 | tf_op jit(solution)/shard_map/psum | solution.py:228
  132.2 1.4 copy-start.2
  133.8 1.0 copy-start.1
  135.5 18.6 %copy-start.16 = (f32[256,256]{1,0:T(8,128)S(1)}, f32[256,256]{1,0:T(8,128)}, u32[]{:S(2)}) copy-start(f32[256,256]{1,0:T(8,128)} %param.44) | copy-start | bytes 786436
  140.4 2.6 copy-start.20
  143.0 0.8 copy-start.21
  148.7 2.6 copy-start.20
  151.3 0.8 copy-start.21
  152.1 5.9 slice-start
  154.5 1.0 copy-start.24
  158.0 81.7 %all-gather.6.cloned.1.call-start = ((), (), s32[]{:S(2)}) async-start(), calls=%async_computation.10 | async-start | bytes 1179648 | tf_op jit(solution)/shard_map/all_gather | solution.py:239
  158.7 143.8 %all-reduce.12.cloned.1.call-start = ((), (), s32[]{:S(2)}) async-start(), calls=%async_computation.7 | async-start | bytes 2097152 | tf_op jit(solution)/shard_map/psum | solution.py:280
  199.6 1.1 copy-start.3
  202.3 45.1 %copy-start.14 = (bf16[1024,256]{1,0:T(8,128)(2,1)}, bf16[1024,256]{1,0:T(8,128)(2,1)S(1)}, u32[]{:S(2)}) copy-start(bf16[1024,256]{1,0:T(8,128)(2,1)S(1)} %get-tuple-element.414) | copy-start | bytes 1572868
  242.2 3.2 copy-start
  258.4 6.9 %copy-start.23 = (bf16[2048,1,256]{2,0,1:T(8,128)(2,1)S(1)}, bf16[2048,1,256]{2,0,1:T(8,128)(2,1)}, u32[]{:S(2)}) copy-start(bf16[2048,1,256]{2,0,1:T(8,128)(2,1)} %all-gather.6.cloned.1.call-done) | copy-start | bytes 3145732
  263.3 1.9 copy-start.13
  267.6 44.3 %copy-start.10 = (f32[512,256]{1,0:T(8,128)S(1)}, f32[512,256]{1,0:T(8,128)}, u32[]{:S(2)}) copy-start(f32[512,256]{1,0:T(8,128)} %param.53) | copy-start | bytes 1572868
  267.6 80.9 %all-reduce.14.cloned.1.call-start = ((), (), s32[]{:S(2)}) async-start(), calls=%async_computation.8 | async-start | bytes 2097152 | tf_op jit(solution)/shard_map/psum | solution.py:311
  306.5 1.1 copy-start.12
  309.7 0.8 copy-start.18
  311.8 108.1 %reduce-scatter.2.cloned.1.call-start = ((), (), s32[]{:S(2)}) async-start(), calls=%async_computation.9 | async-start | bytes 2359296 | tf_op jit(solution)/shard_map/reduce_scatter | solution.py:292
  319.1 34.0 %copy-start.17 = (f32[256,256]{1,0:T(8,128)S(1)}, f32[256,256]{1,0:T(8,128)}, u32[]{:S(2)}) copy-start(f32[256,256]{1,0:T(8,128)} %param.41) | copy-start | bytes 786436
  319.1 218.4 %all-reduce.16.cloned.1.call-start = ((), (), s32[]{:S(2)}) async-start(), calls=%async_computation.11 | async-start | bytes 4194304 | tf_op jit(solution)/shard_map/psum | solution.py:336
  352.0 1.1 copy-start.4
  384.7 8.1 %copy-start.5 = (f32[1024,256]{1,0:T(8,128)S(1)}, f32[1024,256]{1,0:T(8,128)}, u32[]{:S(2)}) copy-start(f32[1024,256]{1,0:T(8,128)} %copy-done.4) | copy-start | bytes 3145732
  384.7 8.1 %copy-start.22 = (bf16[2,512,256]{2,1,0:T(8,128)(2,1)S(1)}, bf16[2,512,256]{2,1,0:T(8,128)(2,1)}, u32[]{:S(2)}) copy-start(bf16[2,512,256]{2,1,0:T(8,128)(2,1)} %get-tuple-element.277) | copy-start | bytes 1572868
  384.7 9.1 %copy-start.8 = (bf16[2,512,768]{2,1,0:T(8,128)(2,1)S(1)}, bf16[2,512,768]{2,1,0:T(8,128)(2,1)}, u32[]{:S(2)}) copy-start(bf16[2,512,768]{2,1,0:T(8,128)(2,1)} %get-tuple-element.281) | copy-start | bytes 4718596
  390.6 55.2 %copy-start.28 = (s32[8,1,128]{2,1,0:T(1,128)S(1)}, s32[8,1,128]{2,1,0:T(1,128)}, u32[]{:S(2)}) copy-start(s32[8,1,128]{2,1,0:T(1,128)} %copy-done.27) | copy-start | bytes 12292
  396.4 202.5 %copy-start.31 = (f32[3,256]{1,0:T(4,128)S(1)}, f32[3,256]{1,0:T(4,128)}, u32[]{:S(2)}) copy-start(f32[3,256]{1,0:T(4,128)} %param.50) | copy-start | bytes 9220
  396.4 202.5 %copy-start.33 = (f32[3,256]{1,0:T(4,128)S(1)}, f32[3,256]{1,0:T(4,128)}, u32[]{:S(2)}) copy-start(f32[3,256]{1,0:T(4,128)} %param.51) | copy-start | bytes 9220
  396.4 202.5 %copy-start.34 = (f32[3,256]{1,0:T(4,128)S(1)}, f32[3,256]{1,0:T(4,128)}, u32[]{:S(2)}) copy-start(f32[3,256]{1,0:T(4,128)} %param.52) | copy-start | bytes 9220
  396.4 205.4 %copy-start.11 = (f32[512,256]{1,0:T(8,128)S(1)}, f32[512,256]{1,0:T(8,128)}, u32[]{:S(2)}) copy-start(f32[512,256]{1,0:T(8,128)} %param.53) | copy-start | bytes 1572868
  428.3 176.2 %copy-start.7 = (f32[256,768]{1,0:T(8,128)S(1)}, f32[256,768]{1,0:T(8,128)}, u32[]{:S(2)}) copy-start(f32[256,768]{1,0:T(8,128)} %param.38) | copy-start | bytes 2359300
  431.9 176.1 %copy-start.15 = (f32[784,256]{1,0:T(8,128)S(1)}, f32[784,256]{1,0:T(8,128)}, u32[]{:S(2)}) copy-start(f32[784,256]{1,0:T(8,128)} %param.35) | copy-start | bytes 2408452
  442.3 107.7 %all-to-all-start.3 = ((bf16[8,128,256]{2,1,0:T(8,128)(2,1)}), bf16[8,128,256]{2,1,0:T(8,128)(2,1)S(1)}, u32[]{:S(2)}, u32[]{:S(2)}) async-start(bf16[8,128,256]{2,1,0:T(8,128)(2,1)} %bitcast.241), calls=%async_computation.4 | async-start | bytes 1048576 | tf_op jit(solution)/shard_map/all_to_all | solution.py:330
  476.3 133.6 %copy-start.36 = (f32[5]{0:T(128)}, f32[5]{0:T(128)S(1)}, u32[]{:S(2)}) copy-start(f32[5]{0:T(128)S(1)} %get-tuple-element.379) | copy-start | bytes 64
  550.0 0.8 copy-start.19
  598.9 9.1 %copy-start.25 = (f32[784,256]{1,0:T(8,128)S(1)}, f32[784,256]{1,0:T(8,128)}, u32[]{:S(2)}) copy-start(f32[784,256]{1,0:T(8,128)} %param.36) | copy-start | bytes 2408452
  598.9 9.1 %copy-start.26 = (f32[784,256]{1,0:T(8,128)S(1)}, f32[784,256]{1,0:T(8,128)}, u32[]{:S(2)}) copy-start(f32[784,256]{1,0:T(8,128)} %param.37) | copy-start | bytes 2408452
Sparse Core Ops, SparseCore 0:
  93.3 37.4 all-reduce.7
  158.1 38.3 all-reduce.9
  199.2 40.4 all-gather.5
  267.7 34.7 all-reduce.11
  312.0 36.4 all-reduce.13
  351.8 68.0 reduce-scatter.1
  425.3 112.1 all-reduce.15
where the time goes:
time: 628 us; the launch traced here: 621 us
  waiting for transfers between devices  219 us (35%)
  blocking collectives  126 us (20%)
  local copies, waits for them, and re-layouts  93.9 us (15%)
  other arithmetic  82.5 us (13%)
  matrix products  56.6 us (9%)
  between operations  22.2 us (4%)
  starting transfers between devices  20.4 us (3%)
    psum x1, waiting for transfers between devices, shards(): lax.psum((grad_qkv, grad_out, grad_ffn_in, grad_ffn_back, grad_gains, gra...  59.4 us
    psum x1, blocking collectives, shards(): norm_sq = lax.psum(norm_local, ('dp', 'ffn'))  39.1 us
    psum x1, waiting for transfers between devices, shards(): lax.psum(token_rows.reshape(tokens, 2, width).astype(jnp.bfloat16), 'ffn')  37.4 us
    all_gather x1, waiting for transfers between devices, shards(): lax.all_gather(cand_rows, 'dp', axis=0, tiled=True)  37.4 us
    psum x1, waiting for transfers between devices, shards(): grad_final = lax.psum(grad_part, 'ffn') - valid[:, None] * target_rows  34.9 us
    unnamed x77, local copies, waits for them, and re-layouts  33.6 us
    psum x1, blocking collectives, shards(): stats = lax.psum(stats_local, 'dp')  30.4 us
    psum x1, waiting for transfers between devices, shards(): grad_normed2 = lax.psum(against(grad_pre, in_low), 'ffn')  24.2 us
  transfers between devices with their start and end apart: 11, of which 8 were waited for; matrix products, arithmetic and copies ran while one was open for 19% of the time, Pallas kernels for 0%

commit v1 on v0

v1 whole, which is shorter than its diff:
```python
import functools
import math

import jax
import jax.numpy as jnp
from jax import lax
from jax.experimental import pallas as pl
from jax.experimental.pallas import tpu as pltpu
from jax.sharding import PartitionSpec as P

MESH = pl.DeviceIdType.MESH
LIMIT = 60 * 1024 * 1024


def lowered(value):
    return value.astype(jnp.bfloat16)


def dot(left, right):
    return jnp.dot(left, right, preferred_element_type=jnp.float32)


def against(left, right):
    return lax.dot_general(
        left, right, (((1,), (1,)), ((), ())), preferred_element_type=jnp.float32
    )


def across(left, right):
    return lax.dot_general(
        left, right, (((0,), (0,)), ((), ())), preferred_element_type=jnp.float32
    )


def iota(shape, dim):
    return lax.broadcasted_iota(jnp.int32, shape, dim)


def each(first, last, body):
    if last - first <= 8:
        for k in range(first, last):
            body(k)
    else:

        def step(k, unused):
            body(k)
            return unused

        lax.fori_loop(first, last, step, 0)


class Peers:
    def __init__(self, n_dp):
        self.n_dp = n_dp
        self.d = lax.axis_index("dp")
        self.f = lax.axis_index("ffn")
        near = self.f + 1 - 2 * lax.rem(self.f, 2)
        far = lax.rem(self.f + 2, 4)
        self.member = (self.f, near, far, 3 - self.f)

    def ffn(self, s):
        return (self.d, self.member[s])

    def ahead(self, k):
        return (lax.rem(self.d + k, self.n_dp), self.f)

    def behind(self, k):
        return (lax.rem(self.d + self.n_dp - k, self.n_dp), self.f)

    def greet(self):
        barrier = pltpu.get_barrier_semaphore()
        for s in (1, 2, 3):
            pl.semaphore_signal(barrier, inc=1, device_id=self.ffn(s), device_id_type=MESH)

        def hello(k):
            pl.semaphore_signal(barrier, inc=1, device_id=self.ahead(k), device_id_type=MESH)

        each(1, self.n_dp, hello)
        pl.semaphore_wait(barrier, self.n_dp + 2)


class Wire:
    def __init__(self, send, recv):
        self.send, self.recv = send, recv

    def make(self, src, dst, number, where):
        return pltpu.make_async_remote_copy(
            src_ref=src,
            dst_ref=dst,
            send_sem=self.send.at[number],
            recv_sem=self.recv.at[number],
            device_id=where,
            device_id_type=MESH,
        )


def spread(row, lanes):
    return jnp.broadcast_to(row, (lanes, row.shape[1])).T


def one_hot_rows(row, width):
    column = spread(row, 128)
    lane = iota(column.shape, 1).astype(jnp.float32)
    return jnp.concatenate(
        [
            jnp.where(column == lane + float(128 * b), 1.0, 0.0).astype(jnp.bfloat16)
            for b in range(width // 128)
        ],
        1,
    )


def one_hot_columns(row, height):
    up = iota((height, row.shape[1]), 0).astype(jnp.float32)
    return jnp.where(up == row, 1.0, 0.0)


def lookup_kernel(
    n_dp,
    cap,
    owner_ref,
    row_ref,
    count_ref,
    table_ref,
    in_ref,
    back_ref,
    rows_out,
    bias_out,
    asked_out,
    key_out,
    weights_out,
    hot,
    slot_s,
    table_low,
    req,
    send_rows,
    send_bias,
    found,
    found_bias,
    part,
    part_bias,
    got,
    got_bias,
    ss,
    rs,
):
    here = Peers(n_dp)
    wire = Wire(ss, rs)
    d, f = here.d, here.f
    both = 2 * n_dp
    filled = n_dp * cap
    rows_dev = table_ref.shape[0]
    chunks, span = owner_ref.shape
    quads = chunks // 2
    here.greet()
    weights_out[0, 0] = lowered(in_ref[...])
    weights_out[0, 1] = lowered(back_ref[...])
    w_base = 0
    copies = []
    for s in (1, 2, 3):
        copy = wire.make(weights_out.at[0], weights_out.at[s], w_base + s, here.ffn(s))
        copies.append(copy)
    place = iota((both, span), 0)
    second = (place >= n_dp).astype(jnp.int32)
    ahead = place - second * n_dp + d
    ahead = jnp.where(ahead >= n_dp, ahead - n_dp, ahead)
    named = ahead * 4 + jnp.where(second > 0, here.member[1], f)
    for c in range(chunks):
        hot[c * both : (c + 1) * both, :] = jnp.where(
            owner_ref[c : c + 1, :] == named, 1.0, 0.0
        ).astype(jnp.bfloat16)
    before = jnp.where(iota((span, span), 0) < iota((span, span), 1), 1.0, 0.0)
    ranks = dot(hot[...], before.astype(jnp.bfloat16))
    carry = jnp.zeros((both, 1), jnp.float32)
    place_f = place.astype(jnp.float32)
    asking = jnp.zeros((both, 128), jnp.float32)
    for c in range(chunks):
        ones = hot[c * both : (c + 1) * both, :].astype(jnp.float32)
        slot = jnp.sum(ones * (ranks[c * both : (c + 1) * both, :] + carry), 0, keepdims=True)
        kind = jnp.sum(ones * place_f, 0, keepdims=True)
        present = jnp.sum(ones, 0, keepdims=True)
        carry = carry + jnp.sum(ones, 1, keepdims=True)
        slot_s[c : c + 1, :] = slot
        key_out[c : c + 1, :] = jnp.where(present > 0, kind * cap + slot, -1.0)
        row = row_ref[c : c + 1, :]
        high = (row >> 5).astype(jnp.float32)
        lower = (row & 31).astype(jnp.float32)
        mine = ones[:n_dp]
        spots = lowered(one_hot_columns(slot, 128))
        asking = asking + against(
            lowered(jnp.concatenate([mine * high, mine * lower], 0)), spots
        )
    wanted = (asking[:n_dp] * 32.0 + asking[n_dp:]).astype(jnp.int32)
    for k in range(n_dp):
        req[k, 0:1, :] = wanted[k : k + 1, :]
    q_base = 4

    def ask(k):
        return wire.make(req.at[k], asked_out.at[k], q_base + k, here.ahead(k))

    each(1, n_dp, lambda k: ask(k).start())
    asked_out[0] = req[0]
    for copy in copies:
        copy.start()
    table_low[0:rows_dev, :] = lowered(table_ref[...])
    padded = table_low.shape[0]
    if padded > rows_dev:
        table_low[rows_dev:padded, :] = jnp.zeros((padded - rows_dev, span), jnp.bfloat16)
    counts = lowered(jnp.broadcast_to(count_ref[...], (8, padded)))
    r_base = q_base + n_dp
    b_base = r_base + n_dp

    def at(k):
        return pl.ds(pl.multiple_of(k * cap, cap), cap)

    def reply(k):
        return (
            wire.make(send_rows.at[k], found.at[at(k)], r_base + k, here.behind(k)),
            wire.make(send_bias.at[k], found_bias.at[k], b_base + k, here.behind(k)),
        )

    def fetch(k):
        chosen = one_hot_rows(asked_out[k].astype(jnp.float32), padded)
        return (
            lowered(dot(chosen, table_low[...]))[:cap],
            against(counts, chosen),
        )

    rows, bias = fetch(0)
    found[0:cap, :] = rows
    found_bias[0] = bias

    def serve(k):
        ask(k).wait_recv()
        rows, bias = fetch(k)
        send_rows[k] = rows
        send_bias[k] = bias
        for copy in reply(k):
            copy.start()

    each(1, n_dp, serve)
    e_base = b_base + n_dp
    g_base = e_base + n_dp

    def pass_on(k):
        return (
            wire.make(
                found.at[at(k)],
                found.at[pl.ds(pl.multiple_of(filled + k * cap, cap), cap)],
                e_base + k,
                here.ffn(1),
            ),
            wire.make(found_bias.at[k], found_bias.at[n_dp + k], g_base + k, here.ffn(1)),
        )

    for copy in pass_on(0):
        copy.start()

    def relay(k):
        for copy in reply(k):
            copy.wait_recv()
        for copy in pass_on(k):
            copy.start()

    each(1, n_dp, relay)

    def arrive(k):
        for copy in pass_on(k):
            copy.wait_recv()

    each(0, n_dp, arrive)
    bias_rows = found_bias[:, 0, :].T

    def partial(quarter):
        rows = []
        for column in range(2):
            key = key_out[pl.ds(column * quads + quarter, 1), :]
            chosen = one_hot_rows(key, 2 * filled)
            rows.append(lowered(dot(chosen, found[...])))
        chunk = quads + quarter
        slot = slot_s[pl.ds(chunk, 1), :]
        ones = hot[pl.ds(pl.multiple_of(chunk * both, both), both), :]
        bias = jnp.sum(dot(lowered(bias_rows), ones) * one_hot_columns(slot, 128), 0, keepdims=True)
        return rows, jnp.broadcast_to(bias, (8, span))

    rows, bias = partial(here.member[2])
    x_base = g_base + n_dp
    part[0] = rows[0]
    part[1] = rows[1]
    part_bias[...] = bias
    give = wire.make(part, got, x_base, here.ffn(2))
    give_bias = wire.make(part_bias, got_bias, x_base + 1, here.ffn(2))
    give.start()
    give_bias.start()
    rows, bias = partial(f)
    give.wait_recv()
    give_bias.wait_recv()
    rows_out[0] = rows[0] + got[0]
    other = wire.make(rows_out.at[0], rows_out.at[1], x_base + 2, here.ffn(1))
    other.start()
    rows_out[2] = rows[1] + got[1]
    bias_out[...] = bias + got_bias[...]
    each(1, n_dp, lambda k: ask(k).wait_send())

    def sent(k):
        for copy in reply(k):
            copy.wait_send()

    each(1, n_dp, sent)

    def passed(k):
        for copy in pass_on(k):
            copy.wait_send()

    each(0, n_dp, passed)
    give.wait_send()
    give_bias.wait_send()
    for copy in copies:
        copy.wait()
    other.wait()


def lookup(n_dp, cap, item_owner, item_row, log_count, item_table, ffn_in, ffn_back):
    tokens = item_owner.shape[0]
    rows_dev, width = item_table.shape
    span = tokens // 4
    padded = -(-rows_dev // 128) * 128
    owner = item_owner.T.reshape(8, span)
    row = item_row.T.reshape(8, span)
    count = jnp.pad(log_count.astype(jnp.float32), (0, padded - rows_dev)).reshape(1, padded)
    low, full = jnp.bfloat16, jnp.float32
    vmem = pl.BlockSpec(memory_space=pltpu.VMEM)
    number = 4 + 5 * n_dp + 3
    return pl.pallas_call(
        functools.partial(lookup_kernel, n_dp, cap),
        out_shape=(
            jax.ShapeDtypeStruct((3, span, width), low),
            jax.ShapeDtypeStruct((8, span), full),
            jax.ShapeDtypeStruct((n_dp, 1, 128), jnp.int32),
            jax.ShapeDtypeStruct((8, span), full),
            jax.ShapeDtypeStruct((4, 2, width, width), low),
        ),
        in_specs=[vmem] * 6,
        out_specs=(vmem,) * 5,
        scratch_shapes=[
            pltpu.VMEM((16 * n_dp, span), low),
            pltpu.VMEM((8, span), full),
            pltpu.VMEM((padded, width), low),
            pltpu.VMEM((n_dp, 1, 128), jnp.int32),
            pltpu.VMEM((n_dp, cap, width), low),
            pltpu.VMEM((n_dp, 8, 128), full),
            pltpu.VMEM((2 * n_dp * cap, width), low),
            pltpu.VMEM((2 * n_dp, 8, 128), full),
            pltpu.VMEM((2, span, width), low),
            pltpu.VMEM((8, span), full),
            pltpu.VMEM((2, span, width), low),
            pltpu.VMEM((8, span), full),
            pltpu.SemaphoreType.DMA((number,)),
            pltpu.SemaphoreType.DMA((number,)),
        ],
        compiler_params=pltpu.CompilerParams(
            collective_id=0, has_side_effects=True, vmem_limit_bytes=LIMIT
        ),
        name="lookup",
    )(owner, row, count, item_table, ffn_in, ffn_back)


EPS = 1e-06
NEG = -1e30
HD = 32
ROOT = math.sqrt(2.0 / math.pi)


def factor_of(hidden):
    return lax.rsqrt(jnp.mean(hidden * hidden, -1, keepdims=True) + EPS)


def turned(block):
    return lowered(block.astype(jnp.float32).T)


def rms_back(hidden, gain, upstream):
    factor = factor_of(hidden)
    scaled = upstream * gain
    inner = jnp.mean(scaled * hidden, -1, keepdims=True)
    grad_hidden = factor * scaled - hidden * (factor * factor * factor * inner)
    return grad_hidden, jnp.sum(upstream * hidden * factor, 0, keepdims=True)


def loop(first, last, body):
    def step(k, unused):
        body(k)
        return unused

    lax.fori_loop(first, last, step, 0)


def layer_kernel(
    n_dp,
    rows_ref,
    bias_ref,
    lengths_ref,
    wq_ref,
    wo_ref,
    weights_ref,
    gains_ref,
    positions_ref,
    rowgrad_out,
    gq_out,
    go_out,
    gp_out,
    gf_out,
    sums_out,
    cands,
    cand_bias,
    cand_t,
    cand_col,
    cand_in,
    wq,
    wo,
    h0_s,
    n1_s,
    q_s,
    qt_s,
    k_s,
    v_s,
    kt_s,
    vt_s,
    mask_s,
    p_s,
    p16_s,
    ds16_s,
    stack_s,
    mixt_s,
    h1_s,
    h2_s,
    n2t_s,
    pre_s,
    act_s,
    fin_s,
    fint_s,
    acc_s,
    acc_send,
    acc_got,
    mid_send,
    mid_got,
    tot_s,
    own_s,
    dq_s,
    kv_s,
    kv_send,
    kv_got,
    ss,
    rs,
):
    here = Peers(n_dp)
    wire = Wire(ss, rs)
    f = here.f
    half = lax.rem(f, 2)
    span, width = h0_s.shape
    heads = width // HD
    scale = HD ** (-0.5)
    here.greet()
    length = lengths_ref[f // 2]
    begin = half * span
    lane = iota((1, span), 1)
    valid_lane = jnp.where(lane + begin < length, 1.0, 0.0)
    valid_col = jnp.where(iota((span, 1), 0) + begin < length, 1.0, 0.0)

    cands[0] = rows_ref[2]
    cand_bias[0] = jnp.where(lane + begin < length, -bias_ref[...], NEG)
    c_base, cb_base = 0, n_dp

    def offer(k):
        return (
            wire.make(cands.at[0], cands.at[k], c_base + k, here.ahead(k)),
            wire.make(cand_bias.at[0], cand_bias.at[k], cb_base + k, here.ahead(k)),
        )

    def start_offer(k):
        for copy in offer(k):
            copy.start()

    each(1, n_dp, start_offer)

    wq[...] = lowered(wq_ref[...])
    wo[...] = lowered(wo_ref[...])
    gain1, gain2, gain3 = gains_ref[0:1, :], gains_ref[1:2, :], gains_ref[2:3, :]
    start = pl.multiple_of(begin, span)
    hidden0 = rows_ref[0].astype(jnp.float32) + positions_ref[pl.ds(start, span), :]
    h0_s[...] = hidden0
    normed1 = lowered(hidden0 * factor_of(hidden0) * gain1)
    n1_s[...] = normed1
    q_s[...] = lowered(dot(normed1, wq[:, :width]))
    k_s[0:span, :] = lowered(dot(normed1, wq[:, width : 2 * width]))
    v_s[0:span, :] = lowered(dot(normed1, wq[:, 2 * width :]))
    start = pl.multiple_of(span - begin, span)
    hidden0 = rows_ref[1].astype(jnp.float32) + positions_ref[pl.ds(start, span), :]
    normed1 = lowered(hidden0 * factor_of(hidden0) * gain1)
    k_s[span:, :] = lowered(dot(normed1, wq[:, width : 2 * width]))
    v_s[span:, :] = lowered(dot(normed1, wq[:, 2 * width :]))
    qt_s[...] = turned(q_s[...])
    kt_s[...] = turned(k_s[...])
    vt_s[...] = turned(v_s[...])
    key_at = iota((2 * span, span), 0)
    key_at = jnp.where(key_at < span, key_at + begin, key_at - begin)
    allowed = (key_at <= iota((2 * span, span), 1) + begin) & (key_at < length)
    mask_s[...] = jnp.where(allowed, 0.0, NEG)
    row_head = iota((width, span), 0) // HD
    lane_head = iota((span, width), 1) // HD

    def forward_head(h):
        here_rows = pl.ds(pl.multiple_of(h * HD, HD), HD)
        mine = jnp.where(row_head == h, qt_s[...].astype(jnp.float32), 0.0)
        scores = dot(k_s[...], lowered(mine)) * scale + mask_s[...]
        expo = jnp.exp(scores - jnp.max(scores, 0, keepdims=True))
        probs = expo / jnp.sum(expo, 0, keepdims=True)
        p_s[h] = probs
        low_probs = lowered(probs)
        p16_s[:, pl.ds(pl.multiple_of(h * span, span), span)] = low_probs
        mixt_s[here_rows, :] = lowered(dot(vt_s[here_rows, :], low_probs))

    loop(0, heads, forward_head)
    attn = dot(turned(mixt_s[...]), wo[...])
    hidden1 = h0_s[...] + attn
    h1_s[...] = hidden1
    sum_attn = jnp.sum(valid_col * attn * attn, keepdims=True)
    normed2 = hidden1 * factor_of(hidden1) * gain2
    n2t_s[...] = turned(lowered(normed2))
    normed2 = lowered(normed2)
    for s in range(4):
        pre = dot(normed2, weights_ref[s, 0])
        pre_s[s] = pre
        active = lowered(0.5 * pre * (1.0 + jnp.tanh(ROOT * (pre + 0.044715 * pre * pre * pre))))
        act_s[:, s * span : (s + 1) * span] = active
    branch = dot(act_s[...], jnp.concatenate([weights_ref[s, 1] for s in range(4)], 0))
    hidden2 = h1_s[...] + branch
    h2_s[...] = hidden2
    sum_ffn = jnp.sum(valid_col * branch * branch, keepdims=True)
    sum_hid = jnp.sum(valid_col * hidden2 * hidden2, keepdims=True)
    final = lowered(hidden2 * factor_of(hidden2) * gain3)
    fin_s[0:span, :] = final
    f_base = cb_base + n_dp
    fin = [fin_s.at[pl.ds(s * span, span)] for s in range(4)]
    near = wire.make(fin[0], fin[1], f_base, here.ffn(1))
    far = wire.make(fin[0], fin[2], f_base + 1, here.ffn(2))
    relayed = wire.make(fin[2], fin[3], f_base + 2, here.ffn(1))
    far.start()
    near.start()
    fint_s[:, 0:span] = turned(final)

    def prepare(k):
        cand_t[k] = turned(cands[k])
        cand_col[k] = spread(cand_bias[k, 0:1, :], 128)

    prepare(0)

    def prepare_other(k):
        for copy in offer(k):
            copy.wait_recv()
        prepare(k)

    loop(1, n_dp, prepare_other)
    near.wait_recv()
    fint_s[:, span : 2 * span] = turned(fin_s[span : 2 * span, :])
    acc_s[...] = jnp.zeros_like(acc_s)

    def totals(pair):
        lanes = slice(pair * 2 * span, (pair + 1) * 2 * span)

        def step(b, carry):
            top, total = carry
            column = jnp.concatenate([cand_col[b]] * (2 * span // 128), 1)
            logits = dot(cands[b], fint_s[:, lanes]) + column
            higher = jnp.maximum(top, jnp.max(logits, 0, keepdims=True))
            shrink = jnp.exp(top - higher)
            expo = jnp.exp(logits - higher)
            total = total * shrink + jnp.sum(expo, 0, keepdims=True)
            acc_s[:, lanes] = acc_s[:, lanes] * shrink + dot(cand_t[b], lowered(expo))
            return higher, total

        first = jnp.full((1, 2 * span), NEG, jnp.float32)
        return lax.fori_loop(0, n_dp, step, (first, jnp.zeros((1, 2 * span), jnp.float32)))

    top01, total01 = totals(0)
    far.wait_recv()
    relayed.start()
    fint_s[:, 2 * span : 3 * span] = turned(fin_s[2 * span : 3 * span, :])
    relayed.wait_recv()
    fint_s[:, 3 * span :] = turned(fin_s[3 * span :, :])
    top23, total23 = totals(1)
    stat_row = iota((8, span), 0)

    def packed(top, total):
        return jnp.where(stat_row == 0, top, total)

    acc_send[0] = lowered(acc_s[:, span : 2 * span])
    acc_send[1] = lowered(acc_s[:, 3 * span :])
    mid_send[0] = packed(top01[:, span:], total01[:, span:])
    mid_send[1] = packed(top23[:, span:], total23[:, span:])
    g_base = f_base + 3
    give = wire.make(acc_send.at[pl.ds(0, 2)], acc_got.at[pl.ds(0, 2)], g_base, here.ffn(1))
    give_mid = wire.make(
        mid_send.at[pl.ds(0, 2)], mid_got.at[pl.ds(0, 2)], g_base + 1, here.ffn(1)
    )
    give.start()
    give_mid.start()
    give.wait_recv()
    give_mid.wait_recv()

    def merged(acc, top, total, other, stats):
        other_top, other_total = stats[0:1, :], stats[1:2, :]
        higher = jnp.maximum(top, other_top)
        left, right = jnp.exp(top - higher), jnp.exp(other_top - higher)
        return (
            acc * left + other.astype(jnp.float32) * right,
            higher,
            total * left + other_total * right,
        )

    acc, top, total = merged(
        acc_s[:, 2 * span : 3 * span], top23[:, :span], total23[:, :span], acc_got[1], mid_got[1]
    )
    acc_send[2] = lowered(acc)
    mid_send[2] = packed(top, total)
    give2 = wire.make(acc_send.at[2], acc_got.at[2], g_base + 2, here.ffn(2))
    give2_mid = wire.make(mid_send.at[2], mid_got.at[2], g_base + 3, here.ffn(2))
    give2.start()
    give2_mid.start()
    acc, top, total = merged(
        acc_s[:, :span], top01[:, :span], total01[:, :span], acc_got[0], mid_got[0]
    )
    give2.wait_recv()
    give2_mid.wait_recv()
    acc, top, total = merged(acc, top, total, acc_got[2], mid_got[2])
    log_total = top + jnp.log(total)
    tot_s[0] = jnp.broadcast_to(jnp.where(valid_lane > 0, log_total, -NEG), (8, span))
    t_base = g_base + 4
    tell = [wire.make(tot_s.at[0], tot_s.at[s], t_base + s, here.ffn(s)) for s in (1, 2, 3)]
    for copy in tell:
        copy.start()
    target_t = cand_t[0].astype(jnp.float32)
    positive = (
        jnp.sum(fint_s[:, :span].astype(jnp.float32) * target_t, 0, keepdims=True)
        - bias_ref[0:1, :]
    )
    loss = jnp.sum(valid_lane * (log_total - positive), keepdims=True)
    grad_final = ((acc / total - target_t) * valid_lane).T

    grad_h2, gain_grad3 = rms_back(h2_s[...], gain3, grad_final)
    up = lowered(grad_h2)
    h2_s[...] = grad_h2
    for s in range(4):
        gf_out[s, 1] = across(act_s[:, s * span : (s + 1) * span], up)
        grad_act = against(up, weights_ref[s, 1])
        pre = pre_s[s]
        inner = jnp.tanh(ROOT * (pre + 0.044715 * pre * pre * pre))
        slope = 0.5 * (1.0 + inner) + 0.5 * pre * (1.0 - inner * inner) * (
            ROOT * (1.0 + 3.0 * 0.044715 * pre * pre)
        )
        grad_pre = lowered(grad_act * slope)
        gf_out[s, 0] = dot(n2t_s[...], grad_pre)
        act_s[:, s * span : (s + 1) * span] = grad_pre
    grad_normed2 = against(
        act_s[...], jnp.concatenate([weights_ref[s, 0] for s in range(4)], 1)
    )
    grad_h1_norm, gain_grad2 = rms_back(h1_s[...], gain2, grad_normed2)
    h1_s[...] = h2_s[...] + grad_h1_norm

    for copy in tell:
        copy.wait_recv()
    d_base = t_base + 4

    def hand_back(k):
        return wire.make(cand_t.at[k], cand_in.at[k], d_base + k, here.behind(k))

    def cand_grad(b):
        column = jnp.concatenate([cand_col[b]] * (4 * span // 128), 1)
        level = jnp.concatenate([tot_s[s, 0:1, :] for s in range(4)], 1)
        logits = dot(cands[b], fint_s[...]) + column
        return dot(lowered(jnp.exp(logits - level)), fin_s[...])

    def cand_step(b):
        cand_t[b] = lowered(cand_grad(b))
        hand_back(b).start()

    loop(1, n_dp, cand_step)
    own_s[...] = cand_grad(0)

    grad_h1 = h1_s[...]
    attn_up = lowered(grad_h1)
    go_out[...] = dot(mixt_s[...], attn_up)
    grad_mixed = lowered(against(attn_up, wo[...]))
    grad_mixed_f = grad_mixed.astype(jnp.float32)
    mixt_s[...] = turned(grad_mixed)
    for h in range(heads):
        stack_s[h * span : (h + 1) * span, :] = lowered(
            jnp.where(lane_head == h, grad_mixed_f, 0.0)
        )
    kv_s[...] = dot(p16_s[...], stack_s[...])

    def backward_head(h):
        here_rows = pl.ds(pl.multiple_of(h * HD, HD), HD)
        mine = jnp.where(row_head == h, mixt_s[...].astype(jnp.float32), 0.0)
        grad_probs = dot(v_s[...], lowered(mine))
        probs = p_s[h]
        inner = jnp.sum(probs * grad_probs, 0, keepdims=True)
        grad_scores = lowered(probs * (grad_probs - inner))
        ds16_s[:, pl.ds(pl.multiple_of(h * span, span), span)] = grad_scores
        dq_s[here_rows, :] = dot(kt_s[here_rows, :], grad_scores) * scale

    loop(0, heads, backward_head)
    queries = q_s[...].astype(jnp.float32)
    kv_send[1] = kv_s[span:, :]
    own_v = kv_s[0:span, :]
    for h in range(heads):
        stack_s[h * span : (h + 1) * span, :] = lowered(jnp.where(lane_head == h, queries, 0.0))
    kv_s[...] = dot(ds16_s[...], stack_s[...]) * scale
    kv_send[0] = kv_s[span:, :]
    k_base = d_base + n_dp
    lend = wire.make(kv_send, kv_got, k_base, here.ffn(1))
    lend.start()
    own_k = kv_s[0:span, :]
    grad_q = lowered(dq_s[...].T)
    lend.wait_recv()
    grad_united = jnp.concatenate(
        [grad_q, lowered(own_k + kv_got[0]), lowered(own_v + kv_got[1])], 1
    )
    gq_out[...] = across(n1_s[...], grad_united)
    grad_h0_norm, gain_grad1 = rms_back(h0_s[...], gain1, against(grad_united, wq[...]))
    grad_h0 = h1_s[...] + grad_h0_norm
    gp_out[...] = grad_h0
    rowgrad_out[0] = lowered(grad_h0)
    lane8 = iota((1, width), 1)
    row8 = iota((8, width), 0)
    stats = jnp.where(lane8 == 0, loss, 0.0)
    numbers = (jnp.sum(valid_lane, keepdims=True), sum_hid, sum_attn, sum_ffn)
    for i, number in enumerate(numbers):
        stats = jnp.where(lane8 == i + 1, number, stats)
    sums = jnp.where(row8 == 0, gain_grad1, 0.0)
    sums = jnp.where(row8 == 1, gain_grad2, sums)
    sums = jnp.where(row8 == 2, gain_grad3, sums)
    sums_out[...] = jnp.where(row8 == 3, stats, sums)

    own_s[...] = own_s[...] - valid_col * fin_s[0:span, :].astype(jnp.float32)

    def add_in(k):
        hand_back(k).wait_recv()
        own_s[...] = own_s[...] + cand_in[k].astype(jnp.float32)

    loop(1, n_dp, add_in)
    rowgrad_out[1] = lowered(own_s[...])

    def end(k):
        for copy in offer(k):
            copy.wait_send()
        hand_back(k).wait_send()

    each(1, n_dp, end)
    for copy in (near, far, relayed, give, give_mid, give2, give2_mid, lend, *tell):
        copy.wait_send()


def layer(n_dp, rows, bias, lengths, qkv_weight, out_weight, weights, norm_gains, positions):
    span, width = rows.shape[1:]
    heads = width // HD
    low, full = jnp.bfloat16, jnp.float32
    vmem = pl.BlockSpec(memory_space=pltpu.VMEM)
    smem = pl.BlockSpec(memory_space=pltpu.SMEM)
    square = (span, width)
    number = 4 * n_dp + 16

    def out(shape, kind):
        return jax.ShapeDtypeStruct(shape, kind)

    return pl.pallas_call(
        functools.partial(layer_kernel, n_dp),
        out_shape=(
            out((2,) + square, low),
            out((width, 3 * width), full),
            out((width, width), full),
            out(square, full),
            out((4, 2, width, width), full),
            out((8, width), full),
        ),
        in_specs=[vmem, vmem, smem, vmem, vmem, vmem, vmem, vmem],
        out_specs=(vmem,) * 6,
        scratch_shapes=[
            pltpu.VMEM((n_dp,) + square, low),
            pltpu.VMEM((n_dp, 8, span), full),
            pltpu.VMEM((n_dp, width, span), low),
            pltpu.VMEM((n_dp, span, 128), full),
            pltpu.VMEM((n_dp,) + square, low),
            pltpu.VMEM((width, 3 * width), low),
            pltpu.VMEM((width, width), low),
            pltpu.VMEM(square, full),
            pltpu.VMEM(square, low),
            pltpu.VMEM(square, low),
            pltpu.VMEM((width, span), low),
            pltpu.VMEM((2 * span, width), low),
            pltpu.VMEM((2 * span, width), low),
            pltpu.VMEM((width, 2 * span), low),
            pltpu.VMEM((width, 2 * span), low),
            pltpu.VMEM((2 * span, span), full),
            pltpu.VMEM((heads, 2 * span, span), full),
            pltpu.VMEM((2 * span, heads * span), low),
            pltpu.VMEM((2 * span, heads * span), low),
            pltpu.VMEM((heads * span, width), low),
            pltpu.VMEM((width, span), low),
            pltpu.VMEM(square, full),
            pltpu.VMEM(square, full),
            pltpu.VMEM((width, span), low),
            pltpu.VMEM((4,) + square, full),
            pltpu.VMEM((span, 4 * span), low),
            pltpu.VMEM((4 * span, width), low),
            pltpu.VMEM((width, 4 * span), low),
            pltpu.VMEM((width, 4 * span), full),
            pltpu.VMEM((3, width, span), low),
            pltpu.VMEM((3, width, span), low),
            pltpu.VMEM((4, 8, span), full),
            pltpu.VMEM((4, 8, span), full),
            pltpu.VMEM((4, 8, span), full),
            pltpu.VMEM(square, full),
            pltpu.VMEM((width, span), full),
            pltpu.VMEM((2 * span, width), full),
            pltpu.VMEM((2,) + square, full),
            pltpu.VMEM((2,) + square, full),
            pltpu.SemaphoreType.DMA((number,)),
            pltpu.SemaphoreType.DMA((number,)),
        ],
        compiler_params=pltpu.CompilerParams(
            collective_id=1, has_side_effects=True, vmem_limit_bytes=LIMIT
        ),
        name="layer",
    )(rows, bias, lengths, qkv_weight, out_weight, weights, norm_gains, positions)


LEARN = 0.05
GAIN_LEARN = 0.4
STEP = 5
BETA_ONE = 0.5
BETA_TWO = 0.5
DECAY = 0.01
ADAM_EPS = 1e-08
CLIP = 0.05


def total_of(value):
    return jnp.sum(value, keepdims=True)


def reduce_kernel(
    n_dp,
    cap,
    part,
    rowgrad_ref,
    key_ref,
    asked_ref,
    gq_ref,
    go_ref,
    gp_ref,
    gf_ref,
    sums_ref,
    table_out,
    ffn_out,
    strips_out,
    sums_out,
    rows_s,
    hot_s,
    outgoing,
    incoming,
    near_send,
    near_got,
    far_send,
    far_got,
    own_s,
    piece_send,
    piece_got,
    whole_s,
    small,
    ss,
    rs,
):
    here = Peers(n_dp)
    wire = Wire(ss, rs)
    d, f = here.d, here.f
    half = lax.rem(f, 2)
    span, width = gp_ref.shape
    strip = span // 4
    ffn_rows = 2 * width
    rows_mine = ffn_rows + 6 * strip
    padded = part * n_dp
    block = 2 * span
    if cap < 128:
        incoming[...] = jnp.zeros_like(incoming)
    here.greet()

    def slot(s):
        return rows_s.at[pl.ds(s * block, block)]

    rows_s[0:span, :] = rowgrad_ref[0]
    rows_s[span:block, :] = rowgrad_ref[1]
    base = 0
    far = wire.make(slot(0), slot(2), base, here.ffn(2))
    near = wire.make(slot(0), slot(1), base + 1, here.ffn(1))
    relay = wire.make(slot(2), slot(3), base + 2, here.ffn(1))
    far.start()
    near.start()

    small[0, 0] = sums_ref[...]
    tell = [wire.make(small.at[0, 0], small.at[0, s], base + 2 + s, here.ffn(s)) for s in (1, 2, 3)]
    for copy in tell:
        copy.start()

    halves = (jnp.where(half == 0, 1.0, 0.0), jnp.where(half == 1, 1.0, 0.0))

    def pieces(s):
        first = pl.multiple_of(here.member[s] * strip, strip)
        rows = pl.ds(first, strip)
        yield 0, gf_ref[s, 0]
        yield width, gf_ref[s, 1]
        for j in range(3):
            yield ffn_rows + j * strip, gq_ref[rows, j * width : (j + 1) * width]
        yield ffn_rows + 3 * strip, go_ref[rows, :]
        for u in range(2):
            yield ffn_rows + (4 + u) * strip, gp_ref[rows, :] * halves[u]

    for i, s in enumerate((1, 3)):
        for first, value in pieces(s):
            near_send[i, first : first + value.shape[0], :] = lowered(value)
    base = base + 6
    cross = wire.make(near_send, near_got, base, here.ffn(1))
    cross.start()
    near.wait_recv()
    cross.wait_recv()
    for first, value in pieces(2):
        size = value.shape[0]
        got = near_got[1, first : first + size, :].astype(jnp.float32)
        far_send[first : first + size, :] = lowered(value + got)
    across_chip = wire.make(far_send, far_got, base + 1, here.ffn(2))
    across_chip.start()
    for first, value in pieces(0):
        size = value.shape[0]
        got = near_got[0, first : first + size, :].astype(jnp.float32)
        own_s[first : first + size, :] = value + got
    if padded > rows_mine:
        own_s[rows_mine:padded, :] = jnp.zeros((padded - rows_mine, width), jnp.float32)
    far.wait_recv()
    relay.start()
    relay.wait_recv()

    up = iota((cap, span), 0).astype(jnp.float32)
    r_base = base + 2

    def ship(k):
        return wire.make(
            outgoing.at[k],
            incoming.at[pl.ds(pl.multiple_of(k * 128, 128), cap)],
            r_base + k,
            here.ahead(k),
        )

    def choose(k):
        places = []
        level = up + lax.convert_element_type(k * cap, jnp.float32)
        for s in range(4):
            for column in range(2):
                key = key_ref[pl.ds(column * 4 + here.member[s], 1), :]
                places.append(jnp.where(level == key, 1.0, 0.0).astype(jnp.bfloat16))
        return lowered(dot(jnp.concatenate(places, 1), rows_s[...]))

    def send_rows(k):
        outgoing[k] = choose(k)
        ship(k).start()

    loop(1, n_dp, send_rows)
    incoming[0:cap, :] = choose(0)

    for copy in tell:
        copy.wait_recv()
    small[1, 0] = (small[0, 0] + small[0, 1]) + (small[0, 2] + small[0, 3])
    s_base = r_base + n_dp

    def share(row, k, number):
        return wire.make(
            small.at[row, 0], small.at[row + 1, d], number + k, here.ahead(k)
        )

    each(1, n_dp, lambda k: share(1, k, s_base).start())
    small[2, d] = small[1, 0]

    across_chip.wait_recv()
    own_s[0:rows_mine, :] = own_s[0:rows_mine, :] + far_got[0:rows_mine, :].astype(jnp.float32)
    p_base = s_base + n_dp

    def scatter(k):
        return wire.make(piece_send.at[k], piece_got.at[k], p_base + k, here.ahead(k))

    def part_rows(owner):
        return pl.ds(pl.multiple_of(owner * part, part), part)

    def scatter_step(k):
        owner = lax.rem(d + k, n_dp)
        piece_send[k] = lowered(own_s[part_rows(owner), :])
        scatter(k).start()

    loop(1, n_dp, scatter_step)
    rows_dev = table_out.shape[0]
    for k in range(n_dp):
        hot_s[:, k * 128 : (k + 1) * 128] = lowered(
            one_hot_columns(asked_ref[k].astype(jnp.float32), rows_dev)
        )

    def take_rows(k):
        ship(k).wait_recv()

    each(1, n_dp, take_rows)
    table_grad = dot(hot_s[...], incoming[...])
    table_out[...] = table_grad
    squares = total_of(table_grad * table_grad)
    mine = own_s[part_rows(d), :]
    own_s[0:part, :] = mine

    def add_piece(k):
        scatter(k).wait_recv()
        own_s[0:part, :] = own_s[0:part, :] + piece_got[k].astype(jnp.float32)

    loop(1, n_dp, add_piece)
    summed = own_s[0:part, :]
    squares = squares + total_of(summed * summed)
    whole_s[part_rows(d), :] = lowered(summed)
    a_base = p_base + n_dp

    def gather(k):
        rows = whole_s.at[part_rows(d)]
        return wire.make(rows, rows, a_base + k, here.ahead(k))

    each(1, n_dp, lambda k: gather(k).start())
    n_base = a_base + n_dp
    small[3, 0] = jnp.broadcast_to(squares, small.shape[2:])
    tell_norm = [
        wire.make(small.at[3, 0], small.at[3, s], n_base + s, here.ffn(s)) for s in (1, 2, 3)
    ]
    for copy in tell_norm:
        copy.start()
    each(1, n_dp, lambda k: share(1, k, s_base).wait_recv())
    for copy in tell_norm:
        copy.wait_recv()
    small[4, 0] = (small[3, 0] + small[3, 1]) + (small[3, 2] + small[3, 3])
    m_base = n_base + 4
    each(1, n_dp, lambda k: share(4, k, m_base).start())
    small[5, d] = small[4, 0]

    each(1, n_dp, lambda k: gather(k).wait_recv())
    strip_rows = 6 * strip
    strips_out[f] = whole_s[ffn_rows:rows_mine, :]
    g_base = m_base + n_dp
    mine_at = strips_out.at[f]
    far_at = strips_out.at[here.member[2]]
    far2 = wire.make(mine_at, mine_at, g_base, here.ffn(2))
    near2 = wire.make(mine_at, mine_at, g_base + 1, here.ffn(1))
    relay2 = wire.make(far_at, far_at, g_base + 2, here.ffn(1))
    far2.start()
    near2.start()
    ffn_out[...] = whole_s[0:ffn_rows, :]
    each(1, n_dp, lambda k: share(4, k, m_base).wait_recv())
    totals = small[2, 0]
    for k in range(1, n_dp):
        totals = totals + small[2, k]
    squares = small[5, 0]
    for k in range(1, n_dp):
        squares = squares + small[5, k]
    row8 = iota(totals.shape, 0)
    gains = jnp.where(row8 < 3, totals, 0.0)
    norm = jnp.sqrt(squares + total_of(gains * gains))
    sums_out[...] = jnp.where(row8 == 4, norm, totals)
    far2.wait_recv()
    relay2.start()
    near2.wait_recv()
    relay2.wait_recv()

    def end(k):
        ship(k).wait_send()
        share(1, k, s_base).wait_send()
        scatter(k).wait_send()
        gather(k).wait_send()
        share(4, k, m_base).wait_send()

    each(1, n_dp, end)
    for copy in (far, near, relay, cross, across_chip, far2, near2, relay2, *tell, *tell_norm):
        copy.wait_send()


def reduce_all(n_dp, cap, rows_dev, rowgrad, key, asked, gq, go, gp, gf, sums):
    span, width = gp.shape
    strip_rows = 6 * (span // 4)
    rows_mine = 2 * width + strip_rows
    part = -(-rows_mine // (16 * n_dp)) * 16
    low, full = jnp.bfloat16, jnp.float32
    vmem = pl.BlockSpec(memory_space=pltpu.VMEM)
    number = 7 * n_dp + 20

    def out(shape, kind):
        return jax.ShapeDtypeStruct(shape, kind)

    return pl.pallas_call(
        functools.partial(reduce_kernel, n_dp, cap, part),
        out_shape=(
            out((rows_dev, width), full),
            out((2 * width, width), low),
            out((4, strip_rows, width), low),
            out((8, width), full),
        ),
        in_specs=[vmem] * 8,
        out_specs=(vmem,) * 4,
        scratch_shapes=[
            pltpu.VMEM((8 * span, width), low),
            pltpu.VMEM((rows_dev, n_dp * 128), low),
            pltpu.VMEM((n_dp, cap, width), low),
            pltpu.VMEM((n_dp * 128, width), low),
            pltpu.VMEM((2, rows_mine, width), low),
            pltpu.VMEM((2, rows_mine, width), low),
            pltpu.VMEM((rows_mine, width), low),
            pltpu.VMEM((rows_mine, width), low),
            pltpu.VMEM((part * n_dp, width), full),
            pltpu.VMEM((n_dp, part, width), low),
            pltpu.VMEM((n_dp, part, width), low),
            pltpu.VMEM((part * n_dp, width), low),
            pltpu.VMEM((6, max(n_dp, 4), 8, width), full),
            pltpu.SemaphoreType.DMA((number,)),
            pltpu.SemaphoreType.DMA((number,)),
        ],
        compiler_params=pltpu.CompilerParams(
            collective_id=2, has_side_effects=True, vmem_limit_bytes=LIMIT
        ),
        name="reduce",
    )(rowgrad, key, asked, gq, go, gp, gf, sums)


def update_kernel(
    table_grad,
    ffn_grad,
    strips,
    sums,
    *refs,
):
    ins, outs = refs[:21], refs[21:]
    loss_out, rms_out, norm_out = outs[:3]
    outs = outs[3:]
    norm = sums[4:5, 0:1]
    factor = CLIP / jnp.maximum(norm, CLIP)
    corr_one = 1.0 - BETA_ONE**STEP
    corr_two = 1.0 - BETA_TWO**STEP
    width = sums.shape[1]

    def adam(which, rows, lanes, grad, rate):
        weight, moment, second = (ins[3 * which + i][rows, lanes] for i in range(3))
        clipped = grad.astype(jnp.float32) * factor
        moment = BETA_ONE * moment + (1.0 - BETA_ONE) * clipped
        second = BETA_TWO * second + (1.0 - BETA_TWO) * clipped * clipped
        outs[3 * which][rows, lanes] = weight - rate * (
            moment / corr_one / (jnp.sqrt(second / corr_two) + ADAM_EPS) + DECAY * weight
        )
        outs[3 * which + 1][rows, lanes] = moment
        outs[3 * which + 2][rows, lanes] = second

    every = slice(None)
    rows_dev = table_grad.shape[0]
    for first in range(0, rows_dev, 112):
        rows = slice(first, min(first + 112, rows_dev))
        adam(0, rows, every, table_grad[rows, :], LEARN)
    strip = strips.shape[1] // 6
    for m in range(4):
        rows = slice(m * strip, (m + 1) * strip)
        for j in range(3):
            adam(
                1,
                rows,
                slice(j * width, (j + 1) * width),
                strips[m, j * strip : (j + 1) * strip, :],
                LEARN,
            )
        adam(2, rows, every, strips[m, 3 * strip : 4 * strip, :], LEARN)
        for u in range(2):
            rows = slice((4 * u + m) * strip, (4 * u + m + 1) * strip)
            adam(6, rows, every, strips[m, (4 + u) * strip : (5 + u) * strip, :], LEARN)
    for which in range(2):
        for first in range(0, width, 64):
            rows = slice(first, first + 64)
            start = which * width + first
            adam(3 + which, rows, every, ffn_grad[start : start + 64, :], LEARN)
    adam(5, every, every, sums[0:3, :], GAIN_LEARN)
    stats = sums[3:4, :]
    roots = jnp.sqrt(stats / (stats[:, 1:2] * float(width)))

    def one(row, i):
        return jnp.sum(jnp.where(iota(row.shape, 1) == i, row, 0.0))

    loss_out[0] = one(stats, 0)
    loss_out[1] = one(stats, 1)
    for i in range(3):
        rms_out[i] = one(roots, 2 + i)
    norm_out[0] = one(sums[4:5, :], 0)


def update(table_grad, ffn_grad, strips, sums, states):
    vmem = pl.BlockSpec(memory_space=pltpu.VMEM)
    smem = pl.BlockSpec(memory_space=pltpu.SMEM)
    full = jnp.float32
    return pl.pallas_call(
        update_kernel,
        out_shape=tuple(jax.ShapeDtypeStruct((n,), full) for n in (2, 3, 1))
        + tuple(jax.ShapeDtypeStruct(a.shape, full) for a in states),
        in_specs=[vmem] * (4 + len(states)),
        out_specs=(smem,) * 3 + (vmem,) * len(states),
        compiler_params=pltpu.CompilerParams(vmem_limit_bytes=LIMIT),
        name="update",
    )(table_grad, ffn_grad, strips, sums, *states)


def shards(
    item_owner,
    item_row,
    lengths,
    log_count,
    item_table,
    table_mom,
    table_sec,
    qkv_weight,
    qkv_mom,
    qkv_sec,
    out_weight,
    out_mom,
    out_sec,
    ffn_in,
    ffn_in_mom,
    ffn_in_sec,
    ffn_back,
    ffn_back_mom,
    ffn_back_sec,
    norm_gains,
    gains_mom,
    gains_sec,
    positions,
    positions_mom,
    positions_sec,
):
    n_dp = lax.axis_size("dp")
    tokens = item_owner.shape[0]
    cap = max(2, 4 * tokens // (n_dp * lax.axis_size("ffn")))
    rows, bias, asked, key, weights = lookup(
        n_dp, cap, item_owner, item_row, log_count, item_table, ffn_in, ffn_back
    )
    rowgrad, gq, go, gp, gf, sums = layer(
        n_dp, rows, bias, lengths, qkv_weight, out_weight, weights, norm_gains, positions
    )
    table_grad, ffn_grad, strips, sums = reduce_all(
        n_dp, cap, item_table.shape[0], rowgrad, key, asked, gq, go, gp, gf, sums
    )
    return update(
        table_grad,
        ffn_grad,
        strips,
        sums,
        (
            item_table,
            table_mom,
            table_sec,
            qkv_weight,
            qkv_mom,
            qkv_sec,
            out_weight,
            out_mom,
            out_sec,
            ffn_in,
            ffn_in_mom,
            ffn_in_sec,
            ffn_back,
            ffn_back_mom,
            ffn_back_sec,
            norm_gains,
            gains_mom,
            gains_sec,
            positions,
            positions_mom,
            positions_sec,
        ),
    )


def solution(mesh):
    whole, rows, table = P(), P("dp", None), P(("dp", "ffn"), None)
    wide, tall = P(None, "ffn"), P("ffn", None)
    states = (table,) * 3 + (whole,) * 6 + (wide,) * 3 + (tall,) * 3 + (whole,) * 6
    return jax.shard_map(
        shards,
        mesh=mesh,
        in_specs=(rows, rows, P("dp"), P(("dp", "ffn"))) + states,
        out_specs=(whole,) * 3 + states,
        check_vma=False,
    )
```

time: 628 us -> 185 us (0.29)
  the two profiles are of different devices: /device:TPU:0 before, /device:TPU:29 now
where the time goes in v1:
time: 185 us
  Pallas kernels  180 us (97%)
  local copies, waits for them, and re-layouts  3.2 us (2%)
    pallas_call x1, Pallas kernels, layer(): pl.pallas_call(functools.partial(layer_kernel, n_dp), out_shape=(out((2,)...  74.7 us
    pallas_call x1, Pallas kernels, reduce_all(): pl.pallas_call(functools.partial(reduce_kernel, n_dp, cap, part), out_sha...  65.3 us
    pallas_call x1, Pallas kernels, lookup(): pl.pallas_call(functools.partial(lookup_kernel, n_dp, cap), out_shape=(ja...  30.6 us
    pallas_call x1, Pallas kernels, update(): pl.pallas_call(update_kernel, out_shape=tuple((jax.ShapeDtypeStruct((n,),...  9.64 us

profile of v1, /device:TPU:29, one launch (start us, length us, event | category | flops | bytes accessed | tf_op | source)
XLA Modules:
  0.0 185.0 jit_solution(17559690936791591125)
XLA Ops:
  0.7 0.7 convert_element_type.5
  1.4 0.6 reshape.59.count_ref
  1.9 1.3 reshape.57.owner_ref
  3.2 1.3 reshape.58.row_ref
  4.5 30.6 %lookup.1 = (bf16[3,256,256]{2,1,0:T(8,128)(2,1)}, f32[8,256]{1,0:T(8,128)}, s32[8,1,128]{2,1,0:T(1,128)}, f32[8,256]{1,0:T(8,128)}, bf16[4,2,256,256]{3,2,1,0:T(8,128)(2,1)}) custom-call(s32[8,256]{1,0:T(8,128)} %reshape.57.owner_ref, s32[8,256]{1,0:T(8,128)} %reshape.58.row_ref, f32[1,896]{1,0:T(1,128)} %reshape.59.count_ref, f32[784,256]{1,0:T(8,128)} %refs_0_.1, ...), custom_call_target="tpu_custom_call" | custom-call | tf_op jit(solution)/shard_map/lookup/pallas_call | solution.py:334
  35.2 74.7 %layer.1 = (bf16[2,256,256]{2,1,0:T(8,128)(2,1)}, f32[256,768]{1,0:T(8,128)}, f32[256,256]{1,0:T(8,128)}, f32[256,256]{1,0:T(8,128)}, f32[4,2,256,256]{3,2,1,0:T(8,128)}, /*index=5*/f32[8,256]{1,0:T(8,128)}) custom-call(bf16[3,256,256]{2,1,0:T(8,128)(2,1)} %get-tuple-element.39.rows_ref, f32[8,256]{1,0:T(8,128)} %get-tuple-element.40.bias_ref, ...), custom_call_target="tpu_custom_call" | custom-call | tf_op jit(solution)/shard_map/layer/pallas_call | solution.py:776
  109.9 65.3 %reduce.1 = (f32[784,256]{1,0:T(8,128)}, bf16[512,256]{1,0:T(8,128)(2,1)}, bf16[4,384,256]{2,1,0:T(8,128)(2,1)}, f32[8,256]{1,0:T(8,128)}) custom-call(bf16[2,256,256]{2,1,0:T(8,128)(2,1)} %get-tuple-element.42.rowgrad_ref, f32[8,256]{1,0:T(8,128)} %get-tuple-element.43.key_ref, s32[8,1,128]{2,1,0:T(1,128)} %get-tuple-element.44.asked_ref, ...), custom_call_target="tpu_custom_call" | custom-call | tf_op jit(solution)/shard_map/reduce/pallas_call | solution.py:1106
  175.2 9.6 %update.1 = (f32[2]{0:T(128)}, f32[3]{0:T(128)}, f32[1]{0:T(128)}, f32[784,256]{1,0:T(8,128)}, f32[784,256]{1,0:T(8,128)}, /*index=5*/f32[784,256]{1,0:T(8,128)}...) custom-call(f32[784,256]{1,0:T(8,128)} %get-tuple-element.50.table_g, ...), custom_call_target="tpu_custom_call" | custom-call | tf_op jit(solution)/shard_map/update/pallas_call | solution.py:1210
  (1 shorter events, 0.0 us)

commit v2 on v0

v2 whole, which is shorter than its diff:
```python
import functools
import math
import types

import jax
import jax.numpy as jnp
from jax import lax
from jax.experimental import pallas as pl
from jax.experimental.pallas import tpu as pltpu
from jax.sharding import PartitionSpec as P

MESH = pl.DeviceIdType.MESH
MIB = 1024 * 1024
LOW, FULL = jnp.bfloat16, jnp.float32

EPS = 1e-06
NEG = -1e30
HD = 32
ROOT = math.sqrt(2.0 / math.pi)
LEARN = 0.05
GAIN_LEARN = 0.4
STEP = 5
BETA_ONE = 0.5
BETA_TWO = 0.5
DECAY = 0.01
ADAM_EPS = 1e-08
CLIP = 0.05


def lowered(value):
    return value.astype(LOW)


def raised(value):
    return value.astype(FULL)


def dot(left, right):
    return jnp.dot(left, right, preferred_element_type=FULL)


def against(left, right):
    return lax.dot_general(left, right, (((1,), (1,)), ((), ())), preferred_element_type=FULL)


def across(left, right):
    return lax.dot_general(left, right, (((0,), (0,)), ((), ())), preferred_element_type=FULL)


def iota(shape, dim):
    return lax.broadcasted_iota(jnp.int32, shape, dim)


def loop(first, last, body):
    def step(k, unused):
        body(k)
        return unused

    if last - first == 1:
        body(first)
    elif last > first:
        lax.fori_loop(first, last, step, 0)


def each(first, last, body):
    if last - first <= 8:
        for k in range(first, last):
            body(k)
    else:
        loop(first, last, body)


def at(index, size):
    if isinstance(index, int):
        return pl.ds(index * size, size)
    return pl.ds(pl.multiple_of(index * size, size), size)


def spread(row, lanes):
    return jnp.broadcast_to(row, (lanes, row.shape[1])).T


def turned(block):
    return lowered(raised(block).T)


def total_of(value):
    return jnp.sum(value, keepdims=True)


def one_hot_rows(row, width):
    high = jnp.floor(row * (1.0 / 128.0))
    low = spread(row - high * 128.0, 128)
    base = lowered(jnp.where(low == raised(iota(low.shape, 1)), 1.0, 0.0))
    high = lowered(spread(high, 128))
    zero = jnp.zeros_like(base)
    return jnp.concatenate(
        [jnp.where(high == jnp.asarray(b, LOW), base, zero) for b in range(width // 128)], 1
    )


def one_hot_columns(row, height):
    return jnp.where(raised(iota((height, row.shape[1]), 0)) == row, 1.0, 0.0)


def factor_of(hidden):
    return lax.rsqrt(jnp.mean(hidden * hidden, -1, keepdims=True) + EPS)


def rms_back(hidden, gain, upstream):
    factor = factor_of(hidden)
    scaled = upstream * gain
    inner = jnp.mean(scaled * hidden, -1, keepdims=True)
    grad_hidden = factor * scaled - hidden * (factor * factor * factor * inner)
    return grad_hidden, jnp.sum(upstream * hidden * factor, 0, keepdims=True)


class Peers:
    def __init__(self, n_dp):
        self.n_dp, self.n_z = n_dp, n_dp // 2
        self.d, self.f = lax.axis_index("dp"), lax.axis_index("ffn")
        self.z, self.y = self.d // 2, lax.rem(self.d, 2)
        near = self.f + 1 - 2 * lax.rem(self.f, 2)
        far = lax.rem(self.f + 2, 4)
        self.member = (self.f, near, far, 3 - self.f)

    def ffn(self, s):
        return (self.d, self.member[s])

    def ahead(self, i):
        return self.apart(i // self.n_z, i % self.n_z)

    def behind(self, i):
        return self.apart(i // self.n_z, self.n_z - i % self.n_z)

    def apart(self, ky, kz):
        z = lax.rem(self.z + kz, self.n_z)
        return (z * 2 + self.y + ky - 2 * self.y * ky, self.f)

    def side(self):
        return (self.d + 1 - 2 * self.y, self.f)

    def up(self, k):
        return (lax.rem(self.z + k, self.n_z) * 2 + self.y, self.f)

    def down(self, k):
        return (lax.rem(self.z + self.n_z - k, self.n_z) * 2 + self.y, self.f)

    def greet(self):
        barrier = pltpu.get_barrier_semaphore()

        def hello(where):
            pl.semaphore_signal(barrier, inc=1, device_id=where, device_id_type=MESH)

        for s in (1, 2, 3):
            hello(self.ffn(s))
        each(1, self.n_dp, lambda k: hello(self.ahead(k)))

    def met(self):
        pl.semaphore_wait(pltpu.get_barrier_semaphore(), self.n_dp + 2)


class Wire:
    def __init__(self, send, recv):
        self.send, self.recv, self.used = send, recv, 0

    def take(self, number):
        self.used += number
        return self.used - number

    def make(self, src, dst, number, where):
        return pltpu.make_async_remote_copy(
            src_ref=src,
            dst_ref=dst,
            send_sem=self.send.at[number],
            recv_sem=self.recv.at[number],
            device_id=where,
            device_id_type=MESH,
        )


class Group:
    def __init__(self, *copies):
        self.copies = copies

    def start(self):
        for copy in self.copies:
            copy.start()

    def wait_recv(self):
        for copy in self.copies:
            copy.wait_recv()

    def wait_send(self):
        for copy in self.copies:
            copy.wait_send()


INPUTS = [
    "owner",
    "row",
    "lengths",
    "count",
    "table",
    "wq",
    "wo",
    "w_in",
    "w_back",
    "gains",
    "positions",
]
OUTPUTS = ["table_grad", "ffn_grad", "strips", "sums"]


def plan(n_dp, cap, rows_dev, span, width, heads):
    n_z = n_dp // 2
    filled = n_dp * cap
    padded = -(-rows_dev // 128) * 128
    square = (span, width)
    ffn_part, strip_part = parts(n_dp, span, width)
    return {
        "table_s": (rows_dev, width, FULL),
        "wq_s": (width, 3 * width, FULL),
        "wo_s": (width, width, FULL),
        "positions_s": (2 * span, width, FULL),
        "weights": (4, 2, width, width, LOW),
        "hot": (32 * n_dp, span, LOW),
        "slot_s": (8, span, FULL),
        "kind_s": (8, span, FULL),
        "table_low": (padded, width, LOW),
        "req": (n_dp, 1, 128, jnp.int32),
        "asked": (n_dp, 1, 128, jnp.int32),
        "send_rows": (n_dp, cap, width, LOW),
        "send_bias": (n_dp, 1, 128, FULL),
        "found": (4 * filled, width, LOW),
        "found_bias": (4 * n_dp, 1, 128, FULL),
        "bias_s": (8, span, FULL),
        "cands": (n_dp * span, width, LOW),
        "cand_bias": (n_dp, 8, span, FULL),
        "cand_t": (width, (n_dp if kept(n_dp) else 1) * span, LOW),
        "cand_col": ((n_dp if kept(n_dp) else 1) * span, 128, FULL),
        "logit_s": (6 * span if kept(n_dp) else 2 * span, span, FULL),
        "stat_s": (4, 8, span, FULL),
        "wq16": (width, 3 * width, LOW),
        "wo16": (width, width, LOW),
        "h0_s": square + (FULL,),
        "n1_s": square + (LOW,),
        "q_s": square + (LOW,),
        "qt_s": (width, span, LOW),
        "k_s": (2 * span, width, LOW),
        "v_s": (2 * span, width, LOW),
        "kt_s": (width, 2 * span, LOW),
        "vt_s": (width, 2 * span, LOW),
        "mask_s": (2 * span, span, FULL),
        "p_s": (heads, 2 * span, span, FULL),
        "p16_s": (2 * span, heads * span, LOW),
        "stack_s": (heads * span, width, LOW),
        "mixt_s": (width, span, LOW),
        "h1_s": square + (FULL,),
        "h2_s": square + (FULL,),
        "n2t_s": (width, span, LOW),
        "pre_s": (4 * span, width, FULL),
        "act_s": (span, 4 * span, LOW),
        "fin_s": (4 * span, width, LOW),
        "fint_s": (width, 4 * span, LOW),
        "acc_s": (width, 4 * span, FULL),
        "acc_send": (3, width, span, LOW),
        "acc_got": (3, width, span, LOW),
        "mid_send": (3, 8, span, FULL),
        "mid_got": (3, 8, span, FULL),
        "tot_s": (4, 8, span, FULL),
        "cand_send": (n_z, span, width, LOW),
        "side_got": (n_z, span, width, LOW),
        "line_got": (n_z, span, width, LOW),
        "own_s": square + (FULL,),
        "dq_s": (width, span, FULL),
        "kv_s": (2 * span, width, FULL),
        "kv_got": (2 * span, width, FULL),
        "gf_s": (4, 2, width, width, FULL),
        "fnear_send": (2, 2 * width, width, LOW),
        "fnear_got": (2, 2 * width, width, LOW),
        "ffar_send": (2 * width, width, LOW),
        "ffar_got": (2 * width, width, LOW),
        "snear_send": (2, 6 * span // 4, width, LOW),
        "snear_got": (2, 6 * span // 4, width, LOW),
        "sfar_send": (6 * span // 4, width, LOW),
        "sfar_got": (6 * span // 4, width, LOW),
        "strip_s": (n_dp * strip_part, width, FULL),
        "fside_send": (n_z * ffn_part, width, LOW),
        "fside_got": (n_z * ffn_part, width, LOW),
        "fline_send": (n_z, ffn_part, width, LOW),
        "fline_got": (n_z, ffn_part, width, LOW),
        "sside_send": (n_z * strip_part, width, LOW),
        "sside_got": (n_z * strip_part, width, LOW),
        "sline_send": (n_z, strip_part, width, LOW),
        "sline_got": (n_z, strip_part, width, LOW),
        "whole_f": (n_dp * ffn_part, width, LOW),
        "whole_t": (n_dp * strip_part, width, LOW),
        "incoming": (filled, width, LOW),
        "padded_in": (8 * 128 if cap < 128 else 16, width, LOW),
        "owned": (rows_dev, min(n_dp, 8) * 128, LOW),
        "small": (5, 4, 8, width, FULL),
        "small_dp": (2, n_dp, 8, width, FULL),
    }


def kept(n_dp):
    return n_dp <= 8


def parts(n_dp, span, width):
    return (
        -(-2 * width // (16 * n_dp)) * 16,
        -(-6 * span // (64 * n_dp)) * 16,
    )


def step_kernel(n_dp, cap, names, *refs):
    r = types.SimpleNamespace(**dict(zip(names, refs)))
    here = Peers(n_dp)
    wire = Wire(r.send_sems, r.recv_sems)
    d, f, n_z = here.d, here.f, here.n_z
    me, near, far, cross = here.member
    span, width = r.h0_s.shape
    heads = width // HD
    scale = HD ** (-0.5)
    half = lax.rem(f, 2)
    begin = half * span
    filled = n_dp * cap
    kinds = 4 * n_dp
    rows_dev = r.table_s.shape[0]
    padded = r.table_low.shape[0]
    ended = []

    here.greet()
    loads = [
        pltpu.make_async_copy(src, dst, r.load_sems.at[i])
        for i, (src, dst) in enumerate(
            (
                (r.table, r.table_s),
                (r.wq, r.wq_s),
                (r.wo, r.wo_s),
                (r.positions, r.positions_s),
            )
        )
    ]
    for load in loads:
        load.start()

    place = iota((kinds, span), 0)
    slot_of = jnp.zeros((kinds, span), jnp.int32)
    for s in (1, 2, 3):
        slot_of = slot_of + (place >= s * n_dp).astype(jnp.int32)
    steps = place - slot_of * n_dp
    other_y = (steps >= n_z).astype(jnp.int32)
    steps = steps - other_y * n_z + here.z
    steps = jnp.where(steps >= n_z, steps - n_z, steps)
    ahead = steps * 2 + here.y + other_y * (1 - 2 * here.y)
    named = ahead * 4 + jnp.where(
        slot_of == 0, me, jnp.where(slot_of == 1, near, jnp.where(slot_of == 2, far, cross))
    )

    def chunk_of(ref, c):
        return ref[c // 4 : c // 4 + 1, (c % 4) * span : (c % 4 + 1) * span]

    for c in range(8):
        r.hot[c * kinds : (c + 1) * kinds, :] = lowered(
            jnp.where(chunk_of(r.owner, c) == named, 1.0, 0.0)
        )
    before = lowered(jnp.where(iota((span, span), 0) < iota((span, span), 1), 1.0, 0.0))
    carry = jnp.zeros((kinds, 1), FULL)
    place_f = raised(place)
    asking = jnp.zeros((2 * n_dp, 128), FULL)
    for c in range(8):
        ones = raised(r.hot[c * kinds : (c + 1) * kinds, :])
        ranks = dot(r.hot[c * kinds : (c + 1) * kinds, :], before)
        slot = jnp.sum(ones * (ranks + carry), 0, keepdims=True)
        carry = carry + jnp.sum(ones, 1, keepdims=True)
        r.slot_s[c : c + 1, :] = slot
        r.kind_s[c : c + 1, :] = jnp.sum(ones * place_f, 0, keepdims=True)
        row = chunk_of(r.row, c)
        mine = ones[:n_dp]
        sought = jnp.concatenate([mine * raised(row >> 5), mine * raised(row & 31)], 0)
        asking = asking + against(lowered(sought), lowered(one_hot_columns(slot, 128)))
    wanted = (asking[:n_dp] * 32.0 + asking[n_dp:]).astype(jnp.int32)
    for k in range(n_dp):
        r.req[k, 0:1, :] = wanted[k : k + 1, :]
    r.asked[0] = r.req[0]
    q_base = wire.take(n_dp)

    def ask(k):
        return wire.make(r.req.at[k], r.asked.at[k], q_base + k, here.ahead(k))

    here.met()
    each(1, n_dp, lambda k: ask(k).start())

    r.weights[0, 0] = lowered(r.w_in[...])
    r.weights[0, 1] = lowered(r.w_back[...])
    w_base = wire.take(3)
    w_near = wire.make(r.weights.at[0], r.weights.at[1], w_base, here.ffn(1))
    w_far = wire.make(r.weights.at[0], r.weights.at[2], w_base + 1, here.ffn(2))
    w_relay = wire.make(r.weights.at[2], r.weights.at[3], w_base + 2, here.ffn(1))
    w_far.start()
    w_near.start()
    ended += [w_far, w_near, w_relay]

    loads[0].wait()
    r.table_low[0:rows_dev, :] = lowered(r.table_s[...])
    if padded > rows_dev:
        r.table_low[rows_dev:padded, :] = jnp.zeros((padded - rows_dev, width), LOW)
    counts = lowered(jnp.broadcast_to(raised(r.count[...].reshape(1, rows_dev)), (8, rows_dev)))
    if padded > rows_dev:
        counts = jnp.concatenate([counts, jnp.zeros((8, padded - rows_dev), LOW)], 1)
    r_base, b_base = wire.take(n_dp), wire.take(n_dp)

    def reply(k):
        return Group(
            wire.make(r.send_rows.at[k], r.found.at[at(k, cap)], r_base + k, here.behind(k)),
            wire.make(r.send_bias.at[k], r.found_bias.at[k], b_base + k, here.behind(k)),
        )

    def fetch(k):
        chosen = one_hot_rows(raised(r.asked[k]), padded)
        return lowered(dot(chosen, r.table_low[...]))[:cap], against(counts, chosen)[0:1, :]

    def serve(k):
        ask(k).wait_recv()
        rows, bias = fetch(k)
        r.send_rows[k] = rows
        r.send_bias[k] = bias
        reply(k).start()

    loop(1, n_dp, serve)
    rows, bias = fetch(0)
    r.found[0:cap, :] = rows
    r.found_bias[0] = bias
    passes = [(wire.take(n_dp), wire.take(n_dp)) for i in range(3)]

    def pass_on(k, source, target, number, who):
        first, second = passes[number]
        return Group(
            wire.make(
                r.found.at[at(source * n_dp + k, cap)],
                r.found.at[at(target * n_dp + k, cap)],
                first + k,
                here.ffn(who),
            ),
            wire.make(
                r.found_bias.at[source * n_dp + k],
                r.found_bias.at[target * n_dp + k],
                second + k,
                here.ffn(who),
            ),
        )

    def to_far(k):
        return pass_on(k, 0, 2, 0, 2)

    def to_near(k):
        return pass_on(k, 0, 1, 1, 1)

    def relay(k):
        return pass_on(k, 2, 3, 2, 1)

    def forward(k):
        to_far(k).start()
        to_near(k).start()

    def relay_on(k):
        to_far(k).wait_recv()
        relay(k).start()

    forward(0)
    lag = min(3, n_dp - 1)

    def take_on(k):
        reply(k).wait_recv()
        forward(k)

    each(1, lag, take_on)

    def take_both(k):
        take_on(k)
        relay_on(k - lag)

    each(lag, n_dp, take_both)
    w_far.wait_recv()
    w_relay.start()
    each(n_dp - lag, n_dp, relay_on)
    loads[1].wait()
    loads[2].wait()
    r.wq16[...] = lowered(r.wq_s[...])
    r.wo16[...] = lowered(r.wo_s[...])

    def take_near(k):
        to_near(k).wait_recv()
        relay(k).wait_recv()

    each(0, n_dp, take_near)

    def chosen_rows(column, quarter):
        chunk = pl.ds(column * 4 + quarter, 1)
        key = r.kind_s[chunk, :] * float(cap) + r.slot_s[chunk, :]
        return dot(one_hot_rows(key, 4 * filled), r.found[...])

    r.cands[0:span, :] = lowered(chosen_rows(1, f))
    bias_rows = lowered(r.found_bias[:, 0, :].T)
    lane = iota((1, span), 1)
    length = r.lengths[f // 2]
    valid_lane = jnp.where(lane + begin < length, 1.0, 0.0)
    valid_col = jnp.where(iota((span, 1), 0) + begin < length, 1.0, 0.0)
    chunk = 4 + f
    marks = one_hot_columns(r.slot_s[pl.ds(chunk, 1), :], 128)
    bias = jnp.sum(dot(bias_rows, r.hot[at(chunk, kinds), :]) * marks, 0, keepdims=True)
    r.bias_s[...] = jnp.broadcast_to(bias, (8, span))
    r.cand_bias[0] = jnp.broadcast_to(jnp.where(lane + begin < length, -bias, NEG), (8, span))
    z_base, y_base = wire.take(2 * n_z), wire.take(2 * n_z)

    def slot(k, ky):
        if isinstance(k, int) and k == 0:
            return ky
        return 1 + k + ky * (n_z - 1)

    def offer_line(k):
        i = slot(k, 0)
        return Group(
            wire.make(r.cands.at[at(0, span)], r.cands.at[at(i, span)], z_base + k, here.up(k)),
            wire.make(r.cand_bias.at[0], r.cand_bias.at[i], z_base + n_z + k, here.up(k)),
        )

    def offer_side(k):
        i, j = slot(k, 0), slot(k, 1)
        return Group(
            wire.make(r.cands.at[at(i, span)], r.cands.at[at(j, span)], y_base + k, here.side()),
            wire.make(r.cand_bias.at[i], r.cand_bias.at[j], y_base + n_z + k, here.side()),
        )

    def nearest(j):
        return jnp.where(here.z == 0, n_z - j, j)

    each(1, n_z, lambda k: offer_line(k).start())
    offer_side(0).start()

    def hand_on(j):
        k = nearest(j)
        offer_line(k).wait_recv()
        offer_side(k).start()

    loads[3].wait()
    gain1, gain2, gain3 = r.gains[0:1, :], r.gains[1:2, :], r.gains[2:3, :]
    hidden0 = raised(lowered(chosen_rows(0, f))) + r.positions_s[at(half, span), :]
    r.h0_s[...] = hidden0
    normed1 = lowered(hidden0 * factor_of(hidden0) * gain1)
    r.n1_s[...] = normed1
    r.q_s[...] = lowered(dot(normed1, r.wq16[:, :width]))
    r.k_s[0:span, :] = lowered(dot(normed1, r.wq16[:, width : 2 * width]))
    r.v_s[0:span, :] = lowered(dot(normed1, r.wq16[:, 2 * width :]))
    hidden0 = raised(lowered(chosen_rows(0, near))) + r.positions_s[at(1 - half, span), :]
    normed1 = lowered(hidden0 * factor_of(hidden0) * gain1)
    r.k_s[span:, :] = lowered(dot(normed1, r.wq16[:, width : 2 * width]))
    r.v_s[span:, :] = lowered(dot(normed1, r.wq16[:, 2 * width :]))
    r.qt_s[...] = turned(r.q_s[...])
    r.kt_s[...] = turned(r.k_s[...])
    r.vt_s[...] = turned(r.v_s[...])
    key_at = iota((2 * span, span), 0)
    key_at = jnp.where(key_at < span, key_at + begin, key_at - begin)
    allowed = (key_at <= iota((2 * span, span), 1) + begin) & (key_at < length)
    r.mask_s[...] = jnp.where(allowed, 0.0, NEG)
    row_head = iota((width, span), 0) // HD
    lane_head = iota((span, width), 1) // HD

    def forward_head(h):
        rows = at(h, HD)
        mine = jnp.where(row_head == h, raised(r.qt_s[...]), 0.0)
        scores = dot(r.k_s[...], lowered(mine)) * scale + r.mask_s[...]
        expo = jnp.exp(scores - jnp.max(scores, 0, keepdims=True))
        probs = expo / jnp.sum(expo, 0, keepdims=True)
        r.p_s[h] = probs
        low_probs = lowered(probs)
        r.p16_s[:, at(h, span)] = low_probs
        r.mixt_s[rows, :] = lowered(dot(r.vt_s[rows, :], low_probs))

    loop(0, heads, forward_head)
    hand_on(1)
    attn = dot(turned(r.mixt_s[...]), r.wo16[...])
    hidden1 = r.h0_s[...] + attn
    r.h1_s[...] = hidden1
    sum_attn = total_of(valid_col * attn * attn)
    normed2 = lowered(hidden1 * factor_of(hidden1) * gain2)
    r.n2t_s[...] = turned(normed2)
    w_near.wait_recv()
    w_relay.wait_recv()
    for s in range(4):
        pre = dot(normed2, r.weights[s, 0])
        r.pre_s[s * span : (s + 1) * span, :] = pre
        inner = jnp.tanh(ROOT * (pre + 0.044715 * pre * pre * pre))
        r.act_s[:, s * span : (s + 1) * span] = lowered(0.5 * pre * (1.0 + inner))
    branch = dot(r.act_s[...], jnp.concatenate([r.weights[s, 1] for s in range(4)], 0))
    hidden2 = r.h1_s[...] + branch
    r.h2_s[...] = hidden2
    sum_ffn = total_of(valid_col * branch * branch)
    sum_hid = total_of(valid_col * hidden2 * hidden2)
    final = lowered(hidden2 * factor_of(hidden2) * gain3)
    r.fin_s[0:span, :] = final
    f_base = wire.take(3)
    fin = [r.fin_s.at[at(s, span)] for s in range(4)]
    fin_near = wire.make(fin[0], fin[1], f_base, here.ffn(1))
    fin_far = wire.make(fin[0], fin[2], f_base + 1, here.ffn(2))
    fin_relay = wire.make(fin[2], fin[3], f_base + 2, here.ffn(1))
    fin_far.start()
    fin_near.start()
    ended += [fin_far, fin_near, fin_relay]

    def turn_fin(s):
        r.fint_s[:, s * span : (s + 1) * span] = turned(r.fin_s[s * span : (s + 1) * span, :])

    turn_fin(0)

    def prepare(i):
        if kept(n_dp):
            r.cand_t[:, at(i, span)] = turned(r.cands[at(i, span), :])
            r.cand_col[at(i, span), :] = spread(r.cand_bias[i, 0:1, :], 128)

    def columns(i, number):
        if kept(n_dp):
            return r.cand_col[slots(i, number), :]
        rows = [spread(r.cand_bias[i + j, 0:1, :], 128) for j in range(number)]
        return jnp.concatenate(rows, 0)

    def slots(i, number):
        if isinstance(i, int):
            return pl.ds(i * span, number * span)
        return pl.ds(pl.multiple_of(i * span, span), number * span)

    prepare(0)
    offer_side(0).wait_recv()
    prepare(1)
    r.acc_s[...] = jnp.zeros_like(r.acc_s)
    for s in range(4):
        r.stat_s[s, 0:1, :] = jnp.full((1, span), NEG, FULL)
        r.stat_s[s, 1:2, :] = jnp.zeros((1, span), FULL)

    def count_in(s, i, number):
        lanes = slice(s * span, (s + 1) * span)
        rows = slots(i, number)
        first = s % 2 * 3 * span if kept(n_dp) else 0
        held = slice(first, first + number * span)
        logits = dot(r.cands[rows, :], r.fint_s[:, lanes])
        r.logit_s[held, :] = logits + jnp.concatenate([columns(i, number)] * (span // 128), 1)
        top = r.stat_s[s, 0:1, :]
        higher = jnp.maximum(top, jnp.max(r.logit_s[held, :], 0, keepdims=True))
        shrink = jnp.exp(top - higher)
        expo = jnp.exp(r.logit_s[held, :] - higher)
        r.stat_s[s, 0:1, :] = higher
        r.stat_s[s, 1:2, :] = r.stat_s[s, 1:2, :] * shrink + jnp.sum(expo, 0, keepdims=True)
        if kept(n_dp):
            part = dot(r.cand_t[:, rows], lowered(expo))
        else:
            part = across(r.cands[rows, :], lowered(expo))
        r.acc_s[:, lanes] = r.acc_s[:, lanes] * shrink + part

    def count(s, group):
        first = (0, 2, n_z + 1)[group]
        number = (2, n_z - 1, n_z - 1)[group]
        if number <= 3:
            if number:
                count_in(s, first, number)
        else:
            loop(first, first + number, lambda i: count_in(s, i, 1))

    count(0, 0)
    fin_near.wait_recv()
    turn_fin(1)
    count(1, 0)
    each(2, n_z, hand_on)
    fin_far.wait_recv()
    fin_relay.start()
    turn_fin(2)
    count(2, 0)
    loop(2, n_z + 1, prepare)
    count(2, 1)
    fin_relay.wait_recv()
    turn_fin(3)
    count(3, 0)
    count(3, 1)
    count(0, 1)
    count(1, 1)

    def prepare_side(k):
        offer_side(k).wait_recv()
        prepare(slot(k, 1))

    loop(1, n_z, prepare_side)

    a_base = wire.take(6)

    def give(i, who):
        return Group(
            wire.make(r.acc_send.at[i], r.acc_got.at[i], a_base + 2 * i, here.ffn(who)),
            wire.make(r.mid_send.at[i], r.mid_got.at[i], a_base + 2 * i + 1, here.ffn(who)),
        )

    gives = [give(0, 1), give(1, 1), give(2, 2)]
    ended += gives

    def fill(i, s):
        r.acc_send[i] = lowered(r.acc_s[:, s * span : (s + 1) * span])
        r.mid_send[i] = r.stat_s[s]
        gives[i].start()

    def merge(s, i):
        gives[i].wait_recv()
        lanes = slice(s * span, (s + 1) * span)
        top, other = r.stat_s[s, 0:1, :], r.mid_got[i, 0:1, :]
        higher = jnp.maximum(top, other)
        left, right = jnp.exp(top - higher), jnp.exp(other - higher)
        r.acc_s[:, lanes] = r.acc_s[:, lanes] * left + raised(r.acc_got[i]) * right
        r.stat_s[s, 0:1, :] = higher
        r.stat_s[s, 1:2, :] = r.stat_s[s, 1:2, :] * left + r.mid_got[i, 1:2, :] * right

    count(3, 2)
    fill(0, 3)
    count(2, 2)
    merge(2, 0)
    fill(2, 2)
    count(1, 2)
    fill(1, 1)
    count(0, 2)
    merge(0, 1)
    merge(0, 2)
    total = r.stat_s[0, 1:2, :]
    log_total = r.stat_s[0, 0:1, :] + jnp.log(total)
    r.tot_s[0] = jnp.broadcast_to(jnp.where(valid_lane > 0, log_total, -NEG), (8, span))
    def end_pass(k):
        to_far(k).wait_send()
        to_near(k).wait_send()
        relay(k).wait_send()

    each(0, n_dp, end_pass)

    t_base = wire.take(4)
    tell = Group(
        *[wire.make(r.tot_s.at[0], r.tot_s.at[s], t_base + s, here.ffn(s)) for s in (1, 2, 3)]
    )
    tell.start()
    ended.append(tell)
    if not kept(n_dp):
        r.cand_t[...] = turned(r.cands[0:span, :])
    target_t = raised(r.cand_t[:, 0:span])
    positive = (
        jnp.sum(raised(r.fint_s[:, :span]) * target_t, 0, keepdims=True) - r.bias_s[0:1, :]
    )
    loss = total_of(valid_lane * (log_total - positive))
    grad_final = ((r.acc_s[:, 0:span] / total - target_t) * valid_lane).T

    grad_h2, gain_grad3 = rms_back(r.h2_s[...], gain3, grad_final)
    up = lowered(grad_h2)
    r.h2_s[...] = grad_h2
    for s in (1, 3, 2, 0):
        lanes = slice(s * span, (s + 1) * span)
        r.gf_s[s, 1] = across(r.act_s[:, lanes], up)
        grad_act = against(up, r.weights[s, 1])
        pre = r.pre_s[s * span : (s + 1) * span, :]
        inner = jnp.tanh(ROOT * (pre + 0.044715 * pre * pre * pre))
        slope = 0.5 * (1.0 + inner) + 0.5 * pre * (1.0 - inner * inner) * (
            ROOT * (1.0 + 3.0 * 0.044715 * pre * pre)
        )
        grad_pre = lowered(grad_act * slope)
        r.gf_s[s, 0] = dot(r.n2t_s[...], grad_pre)
        r.act_s[:, lanes] = grad_pre
    for i, s in enumerate((1, 3)):
        for j in range(2):
            r.fnear_send[i, j * width : (j + 1) * width, :] = lowered(r.gf_s[s, j])
    e_base = wire.take(4)
    f_near = wire.make(r.fnear_send, r.fnear_got, e_base, here.ffn(1))
    f_far = wire.make(r.ffar_send, r.ffar_got, e_base + 1, here.ffn(2))
    s_near = wire.make(r.snear_send, r.snear_got, e_base + 2, here.ffn(1))
    s_far = wire.make(r.sfar_send, r.sfar_got, e_base + 3, here.ffn(2))
    ended += [f_near, f_far, s_near, s_far]
    f_near.start()

    tell.wait_recv()
    side_base, line_base = wire.take(n_z), wire.take(n_z)

    def cand_side(k):
        return wire.make(r.cand_send.at[k], r.side_got.at[k], side_base + k, here.side())

    def cand_line(k):
        return wire.make(r.cand_send.at[k], r.line_got.at[k], line_base + k, here.down(k))

    def cand_grad(i):
        column = jnp.concatenate([columns(i, 1)] * (4 * span // 128), 1)
        level = jnp.concatenate([r.tot_s[s, 0:1, :] for s in range(4)], 1)
        logits = dot(r.cands[at(i, span), :], r.fint_s[...]) + column
        return dot(lowered(jnp.exp(logits - level)), r.fin_s[...])

    def slot_at(k, ky):
        return jnp.where(k == 0, ky, 1 + k + ky * (n_z - 1))

    def side_step(k):
        r.cand_send[k] = lowered(cand_grad(slot_at(k, 1)))
        cand_side(k).start()

    def line_step(k):
        grad = cand_grad(slot_at(k, 0))
        cand_side(k).wait_send()
        cand_side(k).wait_recv()
        r.cand_send[k] = lowered(grad + raised(r.side_got[k]))
        cand_line(k).start()

    middle = n_z // 2
    side_step(middle)

    def side_rest(k):
        side_step(lax.rem(k + middle, n_z))

    loop(1, n_z, side_rest)

    grad_normed2 = against(
        r.act_s[...], jnp.concatenate([r.weights[s, 0] for s in range(4)], 1)
    )
    grad_h1_norm, gain_grad2 = rms_back(r.h1_s[...], gain2, grad_normed2)
    grad_h1 = r.h2_s[...] + grad_h1_norm
    r.h1_s[...] = grad_h1
    f_near.wait_recv()
    for j in range(2):
        rows = slice(j * width, (j + 1) * width)
        r.ffar_send[rows, :] = lowered(r.gf_s[2, j] + raised(r.fnear_got[1, rows, :]))
    f_far.start()

    attn_up = lowered(grad_h1)
    r.acc_s[:, 3 * width :] = dot(r.mixt_s[...], attn_up)
    grad_mixed = lowered(against(attn_up, r.wo16[...]))
    grad_mixed_f = raised(grad_mixed)
    r.mixt_s[...] = turned(grad_mixed)
    for h in range(heads):
        r.stack_s[h * span : (h + 1) * span, :] = lowered(
            jnp.where(lane_head == h, grad_mixed_f, 0.0)
        )
    r.kv_s[...] = dot(r.p16_s[...], r.stack_s[...])
    r.logit_s[span : 2 * span, :] = r.kv_s[span:, :]
    r.own_s[...] = r.kv_s[0:span, :]

    def backward_head(h):
        rows = at(h, HD)
        mine = jnp.where(row_head == h, raised(r.mixt_s[...]), 0.0)
        grad_probs = dot(r.v_s[...], lowered(mine))
        probs = r.p_s[h]
        inner = jnp.sum(probs * grad_probs, 0, keepdims=True)
        grad_scores = lowered(probs * (grad_probs - inner))
        r.p16_s[:, at(h, span)] = grad_scores
        r.dq_s[rows, :] = dot(r.kt_s[rows, :], grad_scores) * scale

    loop(0, heads // 2, backward_head)
    if middle:
        line_step(middle)
    loop(heads // 2, heads, backward_head)
    queries = raised(r.q_s[...])
    for h in range(heads):
        r.stack_s[h * span : (h + 1) * span, :] = lowered(jnp.where(lane_head == h, queries, 0.0))
    r.kv_s[...] = dot(r.p16_s[...], r.stack_s[...]) * scale
    r.logit_s[0:span, :] = r.kv_s[span:, :]
    k_base = wire.take(1)
    lend = wire.make(r.logit_s.at[at(0, 2 * span)], r.kv_got, k_base, here.ffn(1))
    ended.append(lend)
    lend.start()
    ffn_part, strip_part = parts(n_dp, span, width)
    f_far.wait_recv()
    for j in range(2):
        rows = slice(j * width, (j + 1) * width)
        r.pre_s[rows, :] = (
            r.gf_s[0, j] + raised(r.fnear_got[0, rows, :]) + raised(r.ffar_got[rows, :])
        )
    if n_dp * ffn_part > 2 * width:
        r.pre_s[2 * width : n_dp * ffn_part, :] = jnp.zeros(
            (n_dp * ffn_part - 2 * width, width), FULL
        )
    m_base = wire.take(2 + 2 * n_z)

    def sum_dp(source, size, side_send, side_got, line_send, line_got, base):
        def rows_of(k, y):
            return at(y * n_z + lax.rem(here.z + k, n_z), size)

        across_y = wire.make(side_send, side_got, base, here.side())

        def along(k):
            return wire.make(line_send.at[k], line_got.at[k], base + 1 + k, here.up(k))

        def begin_side():
            def fill_side(k):
                side_send[at(k, size), :] = lowered(source[rows_of(k, 1 - here.y), :])

            loop(0, n_z, fill_side)
            across_y.start()

        def begin_line():
            across_y.wait_recv()

            def fill_line(k):
                line_send[k] = lowered(
                    source[rows_of(k, here.y), :] + raised(side_got[at(k, size), :])
                )
                along(k).start()

            loop(1, n_z, fill_line)

        def finish():
            value = source[rows_of(0, here.y), :] + raised(side_got[0:size, :])
            for k in range(1, n_z):
                along(k).wait_recv()
                value = value + raised(line_got[k])
            return value

        def end():
            across_y.wait_send()
            each(1, n_z, lambda k: along(k).wait_send())

        return begin_side, begin_line, finish, end

    ffn_side, ffn_line, ffn_finish, ffn_end = sum_dp(
        r.pre_s,
        ffn_part,
        r.fside_send,
        r.fside_got,
        r.fline_send,
        r.fline_got,
        m_base,
    )
    strip_side, strip_line, strip_finish, strip_end = sum_dp(
        r.strip_s,
        strip_part,
        r.sside_send,
        r.sside_got,
        r.sline_send,
        r.sline_got,
        m_base + 1 + n_z,
    )
    ffn_side()


    loop(1, middle, line_step)
    loop(middle + 1, n_z, line_step)
    grad_q = lowered(r.dq_s[...].T)
    lend.wait_recv()
    grad_united = jnp.concatenate(
        [
            grad_q,
            lowered(r.kv_s[0:span, :] + r.kv_got[0:span, :]),
            lowered(r.own_s[...] + r.kv_got[span:, :]),
        ],
        1,
    )
    grad_h0_norm, gain_grad1 = rms_back(r.h0_s[...], gain1, against(grad_united, r.wq16[...]))
    grad_h0 = r.h1_s[...] + grad_h0_norm
    r.h0_s[...] = grad_h0

    r.acc_s[:, : 3 * width] = across(r.n1_s[...], grad_united)

    strip = span // 4
    strip_rows = 6 * strip
    halves = (jnp.where(half == 0, 1.0, 0.0), jnp.where(half == 1, 1.0, 0.0))

    def pieces(s):
        rows = pl.ds(pl.multiple_of(here.member[s] * strip, strip), strip)
        for j in range(3):
            yield j * strip, r.acc_s[rows, j * width : (j + 1) * width]
        yield 3 * strip, r.acc_s[rows, 3 * width :]
        for u in range(2):
            yield (4 + u) * strip, r.h0_s[rows, :] * halves[u]

    for i, s in enumerate((1, 3)):
        for first, value in pieces(s):
            r.snear_send[i, first : first + strip, :] = lowered(value)
    s_near.start()

    o_base = wire.take(6)

    def chunk(s, column):
        return r.found.at[at(2 * s + column, span)]

    def row_copies(column):
        return (
            wire.make(chunk(0, column), chunk(2, column), o_base + 3 * column, here.ffn(2)),
            wire.make(chunk(0, column), chunk(1, column), o_base + 3 * column + 1, here.ffn(1)),
            wire.make(chunk(2, column), chunk(3, column), o_base + 3 * column + 2, here.ffn(1)),
        )

    in_far, in_near, in_relay = row_copies(0)
    out_far, out_near, out_relay = row_copies(1)
    ended += [in_far, in_near, in_relay, out_far, out_near, out_relay]
    r.found[0:span, :] = lowered(grad_h0)
    in_far.start()
    in_near.start()

    lane8 = iota((1, width), 1)
    row8 = iota((8, width), 0)
    stats = jnp.where(lane8 == 0, loss, 0.0)
    for i, number in enumerate((total_of(valid_lane), sum_hid, sum_attn, sum_ffn)):
        stats = jnp.where(lane8 == i + 1, number, stats)
    small = jnp.where(row8 == 0, gain_grad1, 0.0)
    small = jnp.where(row8 == 1, gain_grad2, small)
    small = jnp.where(row8 == 2, gain_grad3, small)
    r.small[0, 0] = jnp.where(row8 == 3, stats, small)
    l_base = wire.take(4)

    def to_members(row, base):
        return Group(
            *[
                wire.make(r.small.at[row, 0], r.small.at[row, s], base + s, here.ffn(s))
                for s in (1, 2, 3)
            ]
        )

    tell_small = to_members(0, l_base)
    tell_small.start()
    ended.append(tell_small)

    grad = cand_grad(0)
    s_near.wait_recv()
    for first, value in pieces(2):
        got = raised(r.snear_got[1, first : first + strip, :])
        r.sfar_send[first : first + strip, :] = lowered(value + got)
    s_far.start()
    ffn_line()
    cand_side(0).wait_send()
    cand_side(0).wait_recv()
    r.own_s[...] = (
        grad + raised(r.side_got[0]) - valid_col * raised(r.fin_s[0:span, :])
    )

    def add_line(k):
        cand_line(k).wait_recv()
        r.own_s[...] = r.own_s[...] + raised(r.line_got[k])

    loop(1, n_z, add_line)
    r.found[span : 2 * span, :] = lowered(r.own_s[...])
    out_far.start()
    out_near.start()

    in_far.wait_recv()
    in_relay.start()

    s_far.wait_recv()
    for first, value in pieces(0):
        rows = slice(first, first + strip)
        r.strip_s[rows, :] = (
            value + raised(r.snear_got[0, rows, :]) + raised(r.sfar_got[rows, :])
        )
    if n_dp * strip_part > strip_rows:
        r.strip_s[strip_rows:, :] = jnp.zeros((n_dp * strip_part - strip_rows, width), FULL)
    strip_side()

    order = here.y * n_z + here.z
    v_base = wire.take(2 * n_z + 2)

    def gather_dp(ref, size, base):
        own_part = ref.at[at(order, size)]
        own_column = ref.at[at(here.y, n_z * size)]

        def line(k):
            return wire.make(own_part, own_part, base + k, here.up(k))

        return line, wire.make(own_column, own_column, base + n_z, here.side())

    ffn_all, ffn_all_side = gather_dp(r.whole_f, ffn_part, v_base)
    strip_all, strip_all_side = gather_dp(r.whole_t, strip_part, v_base + n_z + 1)
    ended += [ffn_all_side, strip_all_side]
    mine = ffn_finish()
    squares = total_of(mine * mine)
    r.whole_f[at(order, ffn_part), :] = lowered(mine)
    each(1, n_z, lambda k: ffn_all(k).start())

    for s in range(4):
        for column in range(2):
            chunk_row = pl.ds(column * 4 + here.member[s], 1)
            r.p16_s[0:cap, (2 * s + column) * span : (2 * s + column + 1) * span] = lowered(
                one_hot_columns(r.slot_s[chunk_row, :], cap)
            )
    where_to = jnp.concatenate(
        [
            r.kind_s[pl.ds(column * 4 + here.member[s], 1), :]
            for s in range(4)
            for column in range(2)
        ],
        1,
    )
    where_to = lowered(jnp.broadcast_to(where_to, (16, 8 * span)))

    tell_small.wait_recv()
    r.small[1, 0] = (r.small[0, 0] + r.small[0, 1]) + (r.small[0, 2] + r.small[0, 3])
    h_base = wire.take(2 * n_dp)

    def share(row, k, number):
        return wire.make(
            r.small.at[row, 0], r.small_dp.at[row // 4, d], number + k, here.ahead(k)
        )

    each(1, n_dp, lambda k: share(1, k, h_base).start())
    r.small_dp[0, d] = r.small[1, 0]

    out_far.wait_recv()
    out_relay.start()

    strip_line()
    each(1, n_z, lambda k: ffn_all(k).wait_recv())
    ffn_all_side.start()

    in_near.wait_recv()
    in_relay.wait_recv()
    out_near.wait_recv()
    out_relay.wait_recv()

    g_base = wire.take(n_dp)

    def outgoing(k):
        return pl.ds(pl.multiple_of(8 * span + k * cap, cap), cap)

    def ship(k):
        return wire.make(
            r.found.at[outgoing(k)], r.incoming.at[at(k, cap)], g_base + k, here.ahead(k)
        )

    zero16 = jnp.zeros((16, 8 * span), LOW)

    def choose(k):
        wanted = where_to == lowered(jnp.full((16, 8 * span), k, FULL))
        picked = jnp.concatenate(
            [
                jnp.where(wanted, r.p16_s[i * 16 : (i + 1) * 16, :], zero16)
                for i in range(cap // 16)
            ],
            0,
        )
        return lowered(dot(picked, r.found[0 : 8 * span, :]))

    def fill_rows(k):
        r.found[outgoing(k), :] = choose(k)

    fill_rows(n_z)
    ship(n_z).start()
    loop(1, n_z, fill_rows)
    loop(n_z + 1, n_dp, fill_rows)

    mine = strip_finish()
    squares = squares + total_of(mine * mine)
    r.whole_t[at(order, strip_part), :] = lowered(mine)
    each(1, n_z, lambda k: strip_all(k).start())
    each(1, n_z, lambda k: ship(k).start())
    each(n_z + 1, n_dp, lambda k: ship(k).start())
    r.incoming[0:cap, :] = choose(0)

    several = min(n_dp, 8)

    def own_marks(g):
        for k in range(several):
            r.owned[:, k * 128 : (k + 1) * 128] = lowered(
                one_hot_columns(raised(r.asked[g * several + k]), rows_dev)
            )

    if n_dp == several:
        own_marks(0)

    each(1, n_z, lambda k: strip_all(k).wait_recv())
    strip_all_side.start()

    ffn_all_side.wait_recv()
    r.ffn_grad[...] = r.whole_f[0 : 2 * width, :]

    strip_all_side.wait_recv()
    r.strips[f] = r.whole_t[0:strip_rows, :]
    c_base = wire.take(3)
    mine_at, far_at = r.strips.at[f], r.strips.at[far]
    strip_far = wire.make(mine_at, mine_at, c_base, here.ffn(2))
    strip_near = wire.make(mine_at, mine_at, c_base + 1, here.ffn(1))
    strip_relay = wire.make(far_at, far_at, c_base + 2, here.ffn(1))
    ended += [strip_far, strip_near, strip_relay]
    strip_far.start()
    strip_near.start()

    each(1, n_dp, lambda k: ship(k).wait_recv())

    if n_dp == several:
        r.table_grad[...] = dot(r.owned[...], r.incoming[...])
    else:
        r.table_grad[...] = jnp.zeros((rows_dev, width), FULL)
        r.padded_in[...] = jnp.zeros_like(r.padded_in)

        def add_rows(g):
            own_marks(g)
            for k in range(several):
                r.padded_in[k * 128 : k * 128 + cap, :] = r.incoming[
                    at(g * several + k, cap), :
                ]
            r.table_grad[...] = r.table_grad[...] + dot(r.owned[...], r.padded_in[...])

        loop(0, n_dp // several, add_rows)
    table_grad = r.table_grad[...]
    squares = squares + total_of(table_grad * table_grad)

    r.small[3, 0] = jnp.broadcast_to(squares, (8, width))
    tell_norm = to_members(3, wire.take(4))
    tell_norm.start()
    ended.append(tell_norm)
    each(1, n_dp, lambda k: share(1, k, h_base).wait_recv())
    tell_norm.wait_recv()
    r.small[4, 0] = (r.small[3, 0] + r.small[3, 1]) + (r.small[3, 2] + r.small[3, 3])

    each(1, n_dp, lambda k: share(4, k, h_base + n_dp).start())
    r.small_dp[1, d] = r.small[4, 0]
    strip_far.wait_recv()
    strip_relay.start()
    each(1, n_dp, lambda k: share(4, k, h_base + n_dp).wait_recv())
    totals, squares = r.small_dp[0, 0], r.small_dp[1, 0]
    for k in range(1, n_dp):
        totals = totals + r.small_dp[0, k]
        squares = squares + r.small_dp[1, k]
    gains = jnp.where(row8 < 3, totals, 0.0)
    norm = jnp.sqrt(squares + total_of(gains * gains))
    r.sums[...] = jnp.where(row8 == 4, norm, totals)

    def end_dp(k):
        ask(k).wait_send()
        reply(k).wait_send()
        ship(k).wait_send()
        share(1, k, h_base).wait_send()
        share(4, k, h_base + n_dp).wait_send()

    each(1, n_dp, end_dp)

    def end_side(k):
        offer_side(k).wait_send()

    each(0, n_z, end_side)

    def end_line(k):
        offer_line(k).wait_send()
        cand_line(k).wait_send()
        ffn_all(k).wait_send()
        strip_all(k).wait_send()

    each(1, n_z, end_line)
    ffn_end()
    strip_end()
    strip_near.wait_recv()
    strip_relay.wait_recv()
    for copy in ended:
        copy.wait_send()


def step(n_dp, cap, owner, row, lengths, count, table, wq, wo, w_in, w_back, gains, positions):
    rows_dev, width = table.shape
    span = owner.shape[1] // 4
    heads = width // HD
    shapes = plan(n_dp, cap, rows_dev, span, width, heads)
    names = INPUTS + OUTPUTS + list(shapes) + ["load_sems", "send_sems", "recv_sems"]
    vmem = pl.BlockSpec(memory_space=pltpu.VMEM)
    smem = pl.BlockSpec(memory_space=pltpu.SMEM)
    rest = pl.BlockSpec(memory_space=pl.ANY)
    number = 20 * n_dp + 80

    def out(kind, *shape):
        return jax.ShapeDtypeStruct(shape, kind)

    return pl.pallas_call(
        functools.partial(step_kernel, n_dp, cap, names),
        out_shape=(
            out(FULL, rows_dev, width),
            out(LOW, 2 * width, width),
            out(LOW, 4, 6 * span // 4, width),
            out(FULL, 8, width),
        ),
        in_specs=[vmem, vmem, smem, vmem, rest, rest, rest, vmem, vmem, vmem, rest],
        out_specs=(vmem,) * 4,
        scratch_shapes=[pltpu.VMEM(shape[:-1], shape[-1]) for shape in shapes.values()]
        + [
            pltpu.SemaphoreType.DMA((4,)),
            pltpu.SemaphoreType.DMA((number,)),
            pltpu.SemaphoreType.DMA((number,)),
        ],
        compiler_params=pltpu.CompilerParams(
            collective_id=0,
            has_side_effects=True,
            vmem_limit_bytes=63 * MIB,
        ),
        name="step",
    )(owner, row, lengths, count, table, wq, wo, w_in, w_back, gains, positions)


STATES = 21
GAINS = 5


def jobs(rows_dev, width):
    quarter = -(-rows_dev // 32) * 8
    result = []
    for first in range(0, rows_dev, quarter):
        result.append((0, first, min(quarter, rows_dev - first)))
    return result + [(3, 0, width), (4, 0, width), (1, 0, width), (6, 0, 2 * width), (2, 0, width)]


def update_kernel(rows_dev, table_grad, ffn_grad, strips, sums, *refs):
    ins, refs = refs[:STATES], refs[STATES:]
    loss_out, rms_out, norm_out = refs[:3]
    outs, refs = refs[3 : 3 + STATES], refs[3 + STATES :]
    held, made, refs = refs[:18], refs[18:36], refs[36:]
    table_s, ffn_s, strips_s, grad_sems, in_sems, out_sems = refs
    width = sums.shape[1]
    work = jobs(rows_dev, width)

    def kept_at(which, i):
        return 3 * (which if which < GAINS else which - 1) + i

    def moves(number):
        which, first, rows = work[number]
        part = pl.ds(first, rows)
        here = [kept_at(which, i) for i in range(3)]
        return (
            [
                pltpu.make_async_copy(
                    ins[3 * which + i].at[part],
                    held[here[i]].at[part],
                    in_sems.at[number, i],
                )
                for i in range(3)
            ],
            [
                pltpu.make_async_copy(
                    made[here[i]].at[part],
                    outs[3 * which + i].at[part],
                    out_sems.at[number, i],
                )
                for i in range(3)
            ],
        )

    grads = [
        pltpu.make_async_copy(table_grad, table_s, grad_sems.at[0]),
        pltpu.make_async_copy(ffn_grad, ffn_s, grad_sems.at[1]),
        pltpu.make_async_copy(strips, strips_s, grad_sems.at[2]),
    ]
    grads[0].start()
    for number in range(len(work)):
        for copy in moves(number)[0]:
            copy.start()
        if number == 1:
            grads[1].start()
            grads[2].start()
    norm = sums[4:5, 0:1]
    factor = CLIP / jnp.maximum(norm, CLIP)
    corr_one = 1.0 - BETA_ONE**STEP
    corr_two = 1.0 - BETA_TWO**STEP

    def adam(which, rows, lanes, grad, rate):
        if which == GAINS:
            source, target = ins[3 * which : 3 * which + 3], outs[3 * which : 3 * which + 3]
        else:
            first = kept_at(which, 0)
            source, target = held[first : first + 3], made[first : first + 3]
        weight, moment, second = (ref[rows, lanes] for ref in source)
        clipped = raised(grad) * factor
        moment = BETA_ONE * moment + (1.0 - BETA_ONE) * clipped
        second = BETA_TWO * second + (1.0 - BETA_TWO) * clipped * clipped
        target[0][rows, lanes] = weight - rate * (
            moment / corr_one / (jnp.sqrt(second / corr_two) + ADAM_EPS) + DECAY * weight
        )
        target[1][rows, lanes] = moment
        target[2][rows, lanes] = second

    every = slice(None)
    strip = strips_s.shape[1] // 6
    waited = set()

    def need(i):
        if i not in waited:
            waited.add(i)
            grads[i].wait()

    for number, (which, first, rows) in enumerate(work):
        copies_in, copies_out = moves(number)
        need(0 if which == 0 else 1 if which in (3, 4) else 2)
        for copy in copies_in:
            copy.wait()
        if which == 0:
            part = slice(first, first + rows)
            adam(0, part, every, table_s[part, :], LEARN)
        elif which in (3, 4):
            start = (which - 3) * width
            adam(which, every, every, ffn_s[start : start + width, :], LEARN)
        for m in range(4):
            at_rows = slice(m * strip, (m + 1) * strip)
            if which == 1:
                for j in range(3):
                    lanes = slice(j * width, (j + 1) * width)
                    grad = strips_s[m, j * strip : (j + 1) * strip, :]
                    adam(1, at_rows, lanes, grad, LEARN)
            elif which == 2:
                adam(2, at_rows, every, strips_s[m, 3 * strip : 4 * strip, :], LEARN)
            elif which == 6:
                for u in range(2):
                    at_rows = slice((4 * u + m) * strip, (4 * u + m + 1) * strip)
                    grad = strips_s[m, (4 + u) * strip : (5 + u) * strip, :]
                    adam(6, at_rows, every, grad, LEARN)
        for copy in copies_out:
            copy.start()
    adam(GAINS, every, every, sums[0:3, :], GAIN_LEARN)
    stats = sums[3:4, :]
    roots = jnp.sqrt(stats / (stats[:, 1:2] * float(width)))

    def one(row, i):
        return jnp.sum(jnp.where(iota(row.shape, 1) == i, row, 0.0))

    loss_out[0] = one(stats, 0)
    loss_out[1] = one(stats, 1)
    for i in range(3):
        rms_out[i] = one(roots, 2 + i)
    norm_out[0] = one(sums[4:5, :], 0)
    for number in range(len(work)):
        for copy in moves(number)[1]:
            copy.wait()


def update(table_grad, ffn_grad, strips, sums, states):
    vmem = pl.BlockSpec(memory_space=pltpu.VMEM)
    smem = pl.BlockSpec(memory_space=pltpu.SMEM)
    rest = pl.BlockSpec(memory_space=pl.ANY)
    places = [vmem if i // 3 == GAINS else rest for i in range(STATES)]
    room = [pltpu.VMEM(a.shape, FULL) for i, a in enumerate(states) if i // 3 != GAINS]
    rows_dev, width = table_grad.shape
    number = len(jobs(rows_dev, width))
    return pl.pallas_call(
        functools.partial(update_kernel, rows_dev),
        out_shape=tuple(jax.ShapeDtypeStruct((n,), FULL) for n in (2, 3, 1))
        + tuple(jax.ShapeDtypeStruct(a.shape, FULL) for a in states),
        in_specs=[rest] * 3 + [vmem] + places,
        out_specs=[smem] * 3 + places,
        scratch_shapes=room
        + room
        + [pltpu.VMEM(a.shape, a.dtype) for a in (table_grad, ffn_grad, strips)]
        + [
            pltpu.SemaphoreType.DMA((3,)),
            pltpu.SemaphoreType.DMA((number, 3)),
            pltpu.SemaphoreType.DMA((number, 3)),
        ],
        compiler_params=pltpu.CompilerParams(vmem_limit_bytes=63 * MIB),
        name="update",
    )(table_grad, ffn_grad, strips, sums, *states)


def shards(
    item_owner,
    item_row,
    lengths,
    log_count,
    item_table,
    table_mom,
    table_sec,
    qkv_weight,
    qkv_mom,
    qkv_sec,
    out_weight,
    out_mom,
    out_sec,
    ffn_in,
    ffn_in_mom,
    ffn_in_sec,
    ffn_back,
    ffn_back_mom,
    ffn_back_sec,
    norm_gains,
    gains_mom,
    gains_sec,
    positions,
    positions_mom,
    positions_sec,
):
    n_dp = lax.axis_size("dp")
    tokens = item_owner.shape[0]
    cap = max(2, 4 * tokens // (n_dp * lax.axis_size("ffn")))
    table_grad, ffn_grad, strips, sums = step(
        n_dp,
        cap,
        item_owner.T,
        item_row.T,
        lengths,
        log_count,
        item_table,
        qkv_weight,
        out_weight,
        ffn_in,
        ffn_back,
        norm_gains,
        positions,
    )
    return update(
        table_grad,
        ffn_grad,
        strips,
        sums,
        (
            item_table,
            table_mom,
            table_sec,
            qkv_weight,
            qkv_mom,
            qkv_sec,
            out_weight,
            out_mom,
            out_sec,
            ffn_in,
            ffn_in_mom,
            ffn_in_sec,
            ffn_back,
            ffn_back_mom,
            ffn_back_sec,
            norm_gains,
            gains_mom,
            gains_sec,
            positions,
            positions_mom,
            positions_sec,
        ),
    )


def solution(mesh):
    whole, rows, table = P(), P("dp", None), P(("dp", "ffn"), None)
    wide, tall = P(None, "ffn"), P("ffn", None)
    states = (table,) * 3 + (whole,) * 6 + (wide,) * 3 + (tall,) * 3 + (whole,) * 6
    return jax.shard_map(
        shards,
        mesh=mesh,
        in_specs=(rows, rows, P("dp"), P(("dp", "ffn"))) + states,
        out_specs=(whole,) * 3 + states,
        check_vma=False,
    )
```

time: 628 us -> 131 us (0.21); the launches traced: 621 us -> 131 us
  waiting for transfers between devices: 219 us -> 0 us
  Pallas kernels: 0 us -> 130 us
  blocking collectives: 126 us -> 0 us
  local copies, waits for them, and re-layouts: 93.9 us -> 0 us
  other arithmetic: 82.5 us -> 0 us
  matrix products: 56.6 us -> 0 us
  between operations: 22.2 us -> 0.85 us
  starting transfers between devices: 20.4 us -> 0 us
    psum x5 -> x0, waiting for transfers between devices: 156 us -> none  [the longest x1 59.4 us: shards(): lax.psum((grad_qkv, grad_out, grad_ffn_in, grad_ffn_back, grad_gains, gra...]
    pallas_call x0 -> x2, Pallas kernels: none -> 130 us  [the longest x1 121 us: step(): pl.pallas_call(functools.partial(step_kernel, n_dp, cap, names), out_shap...]
    psum x3 -> x0, blocking collectives: 87.6 us -> none  [the longest x1 39.1 us: shards(): norm_sq = lax.psum(norm_local, ('dp', 'ffn'))]
    dot_general x29 -> x0, matrix products: 56.6 us -> none  [the longest x5 13.6 us: across(): lax.dot_general(left, right, (((0,), (0,)), ((), ())), preferred_element_...]
    gather x6 -> x0, local copies, waits for them, and re-layouts: 40.8 us -> none  [the longest x2 16.7 us: shards(): found_bias[dest, picked]]
    all_gather x4 -> x0, blocking collectives: 38.5 us -> none  [the longest x1 20.5 us: shards(): lax.all_gather(cand_bias, 'dp', axis=0, tiled=True)]
    all_gather x1 -> x0, waiting for transfers between devices: 37.4 us -> none  [shards(): lax.all_gather(cand_rows, 'dp', axis=0, tiled=True)]
    unnamed x77 -> x0, local copies, waits for them, and re-layouts: 33.6 us -> none
  transfers between devices with their start and end apart: 11 -> 0, of which waited for: 8 -> 0; matrix products, arithmetic and copies ran while one was open for 19% -> 0% of each run, Pallas kernels for 0% -> 0%
where the time goes in v2:
time: 131 us
  Pallas kernels  130 us (99%)
    pallas_call x1, Pallas kernels, step(): pl.pallas_call(functools.partial(step_kernel, n_dp, cap, names), out_shap...  121 us
    pallas_call x1, Pallas kernels, update(): pl.pallas_call(functools.partial(update_kernel, rows_dev), out_shape=tupl...  9.55 us

profile of v2, /device:TPU:0, one launch (start us, length us, event | category | flops | bytes accessed | tf_op | source)
XLA Modules:
  0.0 131.1 jit_solution(5571553498465148961)
XLA Ops:
  0.7 120.7 %step.1 = (f32[784,256]{1,0:T(8,128)}, bf16[512,256]{1,0:T(8,128)(2,1)}, bf16[4,384,256]{2,1,0:T(8,128)(2,1)}, f32[8,256]{1,0:T(8,128)}) custom-call(s32[2,1024]{1,0:T(2,128)} %bitcast.2, s32[2,1024]{1,0:T(2,128)} %bitcast.3, s32[2]{0:T(128)} %refs_2_.2, s32[784]{0:T(1024)} %refs_3_.2, f32[784,256]{1,0:T(8,128)} %refs_0_.1, f32[256,768]{1,0:T(8,128)} %refs_3_.3, ...), custom_call_target="tpu_custom_call" | custom-call | tf_op jit(solution)/shard_map/step/pallas_call | solution.py:1264
  121.4 9.5 %update.1 = (f32[2]{0:T(128)}, f32[3]{0:T(128)}, f32[1]{0:T(128)}, f32[784,256]{1,0:T(8,128)}, f32[784,256]{1,0:T(8,128)}, /*index=5*/f32[784,256]{1,0:T(8,128)}...) custom-call(f32[784,256]{1,0:T(8,128)} %get-tuple-element.28.table_g, ...), custom_call_target="tpu_custom_call" | custom-call | tf_op jit(solution)/shard_map/update/pallas_call | solution.py:1430

commit v3 on v2

--- a/solution.py
+++ b/solution.py
@@ -160,23 +160,53 @@
         pl.semaphore_wait(pltpu.get_barrier_semaphore(), self.n_dp + 2)
 
 
+class Number:
+    def __init__(self, leave, arrive, shared=False):
+        self.leave, self.arrive, self.shared = leave, arrive, shared
+
+    def __add__(self, k):
+        return Number(self.leave if self.shared else self.leave + k, self.arrive + k, self.shared)
+
+
 class Wire:
     def __init__(self, send, recv):
-        self.send, self.recv, self.used = send, recv, 0
-
-    def take(self, number):
-        self.used += number
-        return self.used - number
-
-    def make(self, src, dst, number, where):
+        self.send, self.recv = send, recv
+        self.left, self.arrived, self.most = 0, 0, 0
+
+    def take(self, number, arrivals=None, shared=False):
+        result = Number(self.left, self.arrived, shared)
+        self.left += 1 if shared else number
+        self.arrived += number if arrivals is None else arrivals
+        self.most = max(self.most, self.left)
+        return result
+
+    def renew(self):
+        self.left = 0
+
+    def make(self, src, dst, number, where, landing=None):
         return pltpu.make_async_remote_copy(
             src_ref=src,
             dst_ref=dst,
-            send_sem=self.send.at[number],
-            recv_sem=self.recv.at[number],
+            send_sem=self.send.at[number.leave],
+            recv_sem=self.recv.at[(landing or number).arrive],
             device_id=where,
             device_id_type=MESH,
         )
+
+
+class Joined:
+    def __init__(self, copies, all_of_them):
+        self.copies, self.all = copies, all_of_them
+
+    def start(self):
+        for copy in self.copies:
+            copy.start()
+
+    def wait_recv(self):
+        self.all.wait_recv()
+
+    def wait_send(self):
+        self.all.wait_send()
 
 
 class Group:
@@ -209,7 +239,7 @@
     "gains",
     "positions",
 ]
-OUTPUTS = ["table_grad", "ffn_grad", "strips", "sums"]
+OUTPUTS = ["table_out", "ffn_out", "strips_out", "sums"]
 
 
 def plan(n_dp, cap, rows_dev, span, width, heads):
@@ -223,6 +253,7 @@
         "wq_s": (width, 3 * width, FULL),
         "wo_s": (width, width, FULL),
         "positions_s": (2 * span, width, FULL),
+        "w_s": (2, width, width, FULL),
         "weights": (4, 2, width, width, LOW),
         "hot": (32 * n_dp, span, LOW),
         "slot_s": (8, span, FULL),
@@ -241,6 +272,8 @@
         "cand_col": ((n_dp if kept(n_dp) else 1) * span, 128, FULL),
         "logit_s": (6 * span if kept(n_dp) else 2 * span, span, FULL),
         "stat_s": (4, 8, span, FULL),
+        "scale_s": (8, 4 * span, FULL),
+        "expo_s": (n_dp * span if kept(n_dp) else 16, 4 * span, LOW),
         "wq16": (width, 3 * width, LOW),
         "wo16": (width, width, LOW),
         "h0_s": square + (FULL,),
@@ -281,10 +314,15 @@
         "fnear_got": (2, 2 * width, width, LOW),
         "ffar_send": (2 * width, width, LOW),
         "ffar_got": (2 * width, width, LOW),
-        "snear_send": (2, 6 * span // 4, width, LOW),
-        "snear_got": (2, 6 * span // 4, width, LOW),
-        "sfar_send": (6 * span // 4, width, LOW),
-        "sfar_got": (6 * span // 4, width, LOW),
+        "enear_send": (2, span // 2, width, LOW),
+        "enear_got": (2, span // 2, width, LOW),
+        "efar_send": (span // 2, width, LOW),
+        "efar_got": (span // 2, width, LOW),
+        "snear_send": (2, span, width, LOW),
+        "snear_got": (2, span, width, LOW),
+        "sfar_send": (span, width, LOW),
+        "sfar_got": (span, width, LOW),
+        "gv_s": square + (LOW,),
         "strip_s": (n_dp * strip_part, width, FULL),
         "fside_send": (n_z * ffn_part, width, LOW),
         "fside_got": (n_z * ffn_part, width, LOW),
@@ -297,8 +335,13 @@
         "whole_f": (n_dp * ffn_part, width, LOW),
         "whole_t": (n_dp * strip_part, width, LOW),
         "incoming": (filled, width, LOW),
+        "place_s": (3 * span if kept(n_dp) else 16, 4 * filled if kept(n_dp) else 128, LOW),
+        "placed_s": (3 * span if kept(n_dp) else 16, width, LOW),
+        "pick_s": (filled if kept(n_dp) else 16, 8 * span, LOW),
         "padded_in": (8 * 128 if cap < 128 else 16, width, LOW),
         "owned": (rows_dev, min(n_dp, 8) * 128, LOW),
+        "table_grad": (rows_dev, width, FULL),
+        "strips": (4, 6 * span // 4, width, LOW),
         "small": (5, 4, 8, width, FULL),
         "small_dp": (2, n_dp, 8, width, FULL),
     }
@@ -310,8 +353,8 @@
 
 def parts(n_dp, span, width):
     return (
-        -(-2 * width // (16 * n_dp)) * 16,
-        -(-6 * span // (64 * n_dp)) * 16,
+        -(-(2 * width + span // 2) // (16 * n_dp)) * 16,
+        -(-span // (16 * n_dp)) * 16,
     )
 
 
@@ -341,11 +384,13 @@
                 (r.wq, r.wq_s),
                 (r.wo, r.wo_s),
                 (r.positions, r.positions_s),
+                (r.w_in, r.w_s.at[0]),
+                (r.w_back, r.w_s.at[1]),
             )
         )
     ]
-    for load in loads:
-        load.start()
+    for i in (4, 5, 0, 1, 2, 3):
+        loads[i].start()
 
     place = iota((kinds, span), 0)
     slot_of = jnp.zeros((kinds, span), jnp.int32)
@@ -386,7 +431,7 @@
     for k in range(n_dp):
         r.req[k, 0:1, :] = wanted[k : k + 1, :]
     r.asked[0] = r.req[0]
-    q_base = wire.take(n_dp)
+    q_base = wire.take(n_dp, shared=True)
 
     def ask(k):
         return wire.make(r.req.at[k], r.asked.at[k], q_base + k, here.ahead(k))
@@ -394,15 +439,59 @@
     here.met()
     each(1, n_dp, lambda k: ask(k).start())
 
-    r.weights[0, 0] = lowered(r.w_in[...])
-    r.weights[0, 1] = lowered(r.w_back[...])
+    loads[4].wait()
+    loads[5].wait()
+    r.weights[0] = lowered(r.w_s[...])
     w_base = wire.take(3)
     w_near = wire.make(r.weights.at[0], r.weights.at[1], w_base, here.ffn(1))
     w_far = wire.make(r.weights.at[0], r.weights.at[2], w_base + 1, here.ffn(2))
     w_relay = wire.make(r.weights.at[2], r.weights.at[3], w_base + 2, here.ffn(1))
     w_far.start()
     w_near.start()
-    ended += [w_far, w_near, w_relay]
+
+    def build_marks():
+        for s in range(4):
+            for column in range(2):
+                chunk_row = pl.ds(column * 4 + here.member[s], 1)
+                r.p16_s[0:cap, (2 * s + column) * span : (2 * s + column + 1) * span] = lowered(
+                    one_hot_columns(r.slot_s[chunk_row, :], cap)
+                )
+        where_to = jnp.concatenate(
+            [
+                r.kind_s[pl.ds(column * 4 + here.member[s], 1), :]
+                for s in range(4)
+                for column in range(2)
+            ],
+            1,
+        )
+        where_to = lowered(jnp.broadcast_to(where_to, (16, 8 * span)))
+        return where_to
+
+    zero16 = jnp.zeros((16, 8 * span), LOW)
+
+    def picks(where_to, k):
+        wanted = where_to == lowered(jnp.full((16, 8 * span), k, FULL))
+        return jnp.concatenate(
+            [
+                jnp.where(wanted, r.p16_s[i * 16 : (i + 1) * 16, :], zero16)
+                for i in range(cap // 16)
+            ],
+            0,
+        )
+
+    def key_of(column, quarter):
+        chunk = pl.ds(column * 4 + quarter, 1)
+        return r.kind_s[chunk, :] * float(cap) + r.slot_s[chunk, :]
+
+    if kept(n_dp):
+        marks_to = build_marks()
+
+        def keep_picks(k):
+            r.pick_s[at(k, cap), :] = picks(marks_to, k)
+
+        loop(0, n_dp, keep_picks)
+        for i, (column, quarter) in enumerate(((1, f), (0, f), (0, near))):
+            r.place_s[at(i, span), :] = one_hot_rows(key_of(column, quarter), 4 * filled)
 
     loads[0].wait()
     r.table_low[0:rows_dev, :] = lowered(r.table_s[...])
@@ -411,13 +500,21 @@
     counts = lowered(jnp.broadcast_to(raised(r.count[...].reshape(1, rows_dev)), (8, rows_dev)))
     if padded > rows_dev:
         counts = jnp.concatenate([counts, jnp.zeros((8, padded - rows_dev), LOW)], 1)
-    r_base, b_base = wire.take(n_dp), wire.take(n_dp)
+    r_base, b_base = wire.take(n_dp, shared=True), wire.take(1)
+    others = pl.ds(1, n_dp - 1)
 
     def reply(k):
-        return Group(
-            wire.make(r.send_rows.at[k], r.found.at[at(k, cap)], r_base + k, here.behind(k)),
-            wire.make(r.send_bias.at[k], r.found_bias.at[k], b_base + k, here.behind(k)),
-        )
+        return wire.make(r.send_rows.at[k], r.found.at[at(k, cap)], r_base + k, here.behind(k))
+
+    def reply_bias(k):
+        return wire.make(r.send_bias.at[k], r.found_bias.at[k], b_base, here.behind(k))
+
+    def all_replies():
+        rest = r.found.at[pl.ds(cap, filled - cap)]
+        return wire.make(r.send_rows.at[others], rest, r_base, here.side())
+
+    def all_biases():
+        return wire.make(r.send_bias.at[others], r.found_bias.at[others], b_base, here.side())
 
     def fetch(k):
         chosen = one_hot_rows(raised(r.asked[k]), padded)
@@ -429,81 +526,83 @@
         r.send_rows[k] = rows
         r.send_bias[k] = bias
         reply(k).start()
+        reply_bias(k).start()
 
     loop(1, n_dp, serve)
     rows, bias = fetch(0)
     r.found[0:cap, :] = rows
     r.found_bias[0] = bias
-    passes = [(wire.take(n_dp), wire.take(n_dp)) for i in range(3)]
-
-    def pass_on(k, source, target, number, who):
-        first, second = passes[number]
-        return Group(
-            wire.make(
-                r.found.at[at(source * n_dp + k, cap)],
-                r.found.at[at(target * n_dp + k, cap)],
-                first + k,
-                here.ffn(who),
-            ),
-            wire.make(
-                r.found_bias.at[source * n_dp + k],
-                r.found_bias.at[target * n_dp + k],
-                second + k,
-                here.ffn(who),
-            ),
-        )
-
-    def to_far(k):
-        return pass_on(k, 0, 2, 0, 2)
-
-    def to_near(k):
-        return pass_on(k, 0, 1, 1, 1)
-
-    def relay(k):
-        return pass_on(k, 2, 3, 2, 1)
-
-    def forward(k):
-        to_far(k).start()
-        to_near(k).start()
-
-    def relay_on(k):
-        to_far(k).wait_recv()
-        relay(k).start()
-
-    forward(0)
-    lag = min(3, n_dp - 1)
-
-    def take_on(k):
-        reply(k).wait_recv()
-        forward(k)
-
-    each(1, lag, take_on)
-
-    def take_both(k):
-        take_on(k)
-        relay_on(k - lag)
-
-    each(lag, n_dp, take_both)
+    cuts = [(k, 1) for k in range(n_dp)]
+    passes = [wire.take(len(cuts), shared=True) for i in range(3)]
+    bias_passes = [wire.take(1) for i in range(3)]
+
+    def pass_on(i, source, target, number, who):
+        sem = bias_passes[number] if i == len(cuts) else passes[number] + i
+        if i == len(cuts):
+            src, dst = (r.found_bias.at[at(slot, n_dp)] for slot in (source, target))
+        else:
+            first, several = cuts[i]
+            src, dst = (
+                r.found.at[pl.ds((slot * n_dp + first) * cap, several * cap)]
+                for slot in (source, target)
+            )
+        return wire.make(src, dst, sem, here.ffn(who))
+
+    def all_passes(source, number):
+        rows = r.found.at[at(source, filled)]
+        return wire.make(rows, rows, passes[number], here.side())
+
+    def to_far(i):
+        return pass_on(i, 0, 2, 0, 2)
+
+    def to_near(i):
+        return pass_on(i, 0, 1, 1, 1)
+
+    def relay(i):
+        return pass_on(i, 2, 3, 2, 1)
+
+    def take_on(i):
+        first, several = cuts[i]
+        for k in range(max(first, 1), first + several):
+            reply(k).wait_recv()
+        to_far(i).start()
+        to_near(i).start()
+
+    def relay_on(i):
+        to_far(i).wait_recv()
+        relay(i).start()
+
+    for i in range(len(cuts)):
+        take_on(i)
+        if i > 1:
+            relay_on(i - 2)
+    all_biases().wait_recv()
+    to_far(len(cuts)).start()
+    to_near(len(cuts)).start()
     w_far.wait_recv()
     w_relay.start()
-    each(n_dp - lag, n_dp, relay_on)
+    for i in range(len(cuts) - 2, len(cuts) + 1):
+        relay_on(i)
     loads[1].wait()
     loads[2].wait()
     r.wq16[...] = lowered(r.wq_s[...])
     r.wo16[...] = lowered(r.wo_s[...])
-
-    def take_near(k):
-        to_near(k).wait_recv()
-        relay(k).wait_recv()
-
-    each(0, n_dp, take_near)
-
-    def chosen_rows(column, quarter):
-        chunk = pl.ds(column * 4 + quarter, 1)
-        key = r.kind_s[chunk, :] * float(cap) + r.slot_s[chunk, :]
-        return dot(one_hot_rows(key, 4 * filled), r.found[...])
-
-    r.cands[0:span, :] = lowered(chosen_rows(1, f))
+    for i in range(len(cuts)):
+        to_near(i).wait_recv()
+        relay(i).wait_recv()
+
+    if kept(n_dp):
+        r.placed_s[...] = lowered(dot(r.place_s[...], r.found[...]))
+
+    def chosen_rows(i):
+        if kept(n_dp):
+            return r.placed_s[at(i, span), :]
+        column, quarter = ((1, f), (0, f), (0, near))[i]
+        return lowered(dot(one_hot_rows(key_of(column, quarter), 4 * filled), r.found[...]))
+
+    r.cands[0:span, :] = chosen_rows(0)
+    to_near(len(cuts)).wait_recv()
+    relay(len(cuts)).wait_recv()
     bias_rows = lowered(r.found_bias[:, 0, :].T)
     lane = iota((1, span), 1)
     length = r.lengths[f // 2]
@@ -514,19 +613,36 @@
     bias = jnp.sum(dot(bias_rows, r.hot[at(chunk, kinds), :]) * marks, 0, keepdims=True)
     r.bias_s[...] = jnp.broadcast_to(bias, (8, span))
     r.cand_bias[0] = jnp.broadcast_to(jnp.where(lane + begin < length, -bias, NEG), (8, span))
-    z_base, y_base = wire.take(2 * n_z), wire.take(2 * n_z)
+    z_base, y_base = wire.take(0, 2 * n_z), wire.take(2 * n_z)
+    u_base = wire.take(4 * n_z, 0)
+    has_up, has_down = here.z + 1 < n_z, here.z > 0
 
     def slot(k, ky):
         if isinstance(k, int) and k == 0:
             return ky
         return 1 + k + ky * (n_z - 1)
 
-    def offer_line(k):
-        i = slot(k, 0)
+    def offer_line(source, target, number, where):
+        i, j = slot(source, 0), slot(target, 0)
         return Group(
-            wire.make(r.cands.at[at(0, span)], r.cands.at[at(i, span)], z_base + k, here.up(k)),
-            wire.make(r.cand_bias.at[0], r.cand_bias.at[i], z_base + n_z + k, here.up(k)),
-        )
+            wire.make(
+                r.cands.at[at(i, span)], r.cands.at[at(j, span)], number, where, z_base + target
+            ),
+            wire.make(
+                r.cand_bias.at[i],
+                r.cand_bias.at[j],
+                number + 2 * n_z,
+                where,
+                z_base + n_z + target,
+            ),
+        )
+
+    def send_up(a):
+        return offer_line(a, a + 1, u_base + a, here.up(1))
+
+    def send_down(b):
+        source = b if isinstance(b, int) and b == 0 else n_z - b
+        return offer_line(source, n_z - 1 - b, u_base + n_z + b, here.down(1))
 
     def offer_side(k):
         i, j = slot(k, 0), slot(k, 1)
@@ -535,27 +651,33 @@
             wire.make(r.cand_bias.at[i], r.cand_bias.at[j], y_base + n_z + k, here.side()),
         )
 
-    def nearest(j):
-        return jnp.where(here.z == 0, n_z - j, j)
-
-    each(1, n_z, lambda k: offer_line(k).start())
     offer_side(0).start()
+    pl.when(has_up)(lambda: send_up(0).start())
+    pl.when(has_down)(lambda: send_down(0).start())
 
     def hand_on(j):
-        k = nearest(j)
-        offer_line(k).wait_recv()
-        offer_side(k).start()
+        @pl.when(here.z >= j)
+        def from_below():
+            offer_line(0, j, u_base, here.up(1)).wait_recv()
+            pl.when(has_up)(lambda: send_up(j).start())
+            offer_side(j).start()
+
+        @pl.when(here.z + j < n_z)
+        def from_above():
+            offer_line(0, n_z - j, u_base, here.up(1)).wait_recv()
+            pl.when(has_down)(lambda: send_down(j).start())
+            offer_side(n_z - j).start()
 
     loads[3].wait()
     gain1, gain2, gain3 = r.gains[0:1, :], r.gains[1:2, :], r.gains[2:3, :]
-    hidden0 = raised(lowered(chosen_rows(0, f))) + r.positions_s[at(half, span), :]
+    hidden0 = raised(chosen_rows(1)) + r.positions_s[at(half, span), :]
     r.h0_s[...] = hidden0
     normed1 = lowered(hidden0 * factor_of(hidden0) * gain1)
     r.n1_s[...] = normed1
     r.q_s[...] = lowered(dot(normed1, r.wq16[:, :width]))
     r.k_s[0:span, :] = lowered(dot(normed1, r.wq16[:, width : 2 * width]))
     r.v_s[0:span, :] = lowered(dot(normed1, r.wq16[:, 2 * width :]))
-    hidden0 = raised(lowered(chosen_rows(0, near))) + r.positions_s[at(1 - half, span), :]
+    hidden0 = raised(chosen_rows(2)) + r.positions_s[at(1 - half, span), :]
     normed1 = lowered(hidden0 * factor_of(hidden0) * gain1)
     r.k_s[span:, :] = lowered(dot(normed1, r.wq16[:, width : 2 * width]))
     r.v_s[span:, :] = lowered(dot(normed1, r.wq16[:, 2 * width :]))
@@ -580,8 +702,9 @@
         r.p16_s[:, at(h, span)] = low_probs
         r.mixt_s[rows, :] = lowered(dot(r.vt_s[rows, :], low_probs))
 
-    loop(0, heads, forward_head)
+    loop(0, heads * 3 // 4, forward_head)
     hand_on(1)
+    loop(heads * 3 // 4, heads, forward_head)
     attn = dot(turned(r.mixt_s[...]), r.wo16[...])
     hidden1 = r.h0_s[...] + attn
     r.h1_s[...] = hidden1
@@ -615,6 +738,8 @@
         r.fint_s[:, s * span : (s + 1) * span] = turned(r.fin_s[s * span : (s + 1) * span, :])
 
     turn_fin(0)
+    if n_z > 2:
+        hand_on(2)
 
     def prepare(i):
         if kept(n_dp):
@@ -640,7 +765,7 @@
         r.stat_s[s, 0:1, :] = jnp.full((1, span), NEG, FULL)
         r.stat_s[s, 1:2, :] = jnp.zeros((1, span), FULL)
 
-    def count_in(s, i, number):
+    def count_in(s, i, number, group):
         lanes = slice(s * span, (s + 1) * span)
         rows = slots(i, number)
         first = s % 2 * 3 * span if kept(n_dp) else 0
@@ -654,7 +779,10 @@
         r.stat_s[s, 0:1, :] = higher
         r.stat_s[s, 1:2, :] = r.stat_s[s, 1:2, :] * shrink + jnp.sum(expo, 0, keepdims=True)
         if kept(n_dp):
-            part = dot(r.cand_t[:, rows], lowered(expo))
+            low_expo = lowered(expo)
+            r.expo_s[rows, lanes] = low_expo
+            r.stat_s[s, 2 + group : 3 + group, :] = higher
+            part = dot(r.cand_t[:, rows], low_expo)
         else:
             part = across(r.cands[rows, :], lowered(expo))
         r.acc_s[:, lanes] = r.acc_s[:, lanes] * shrink + part
@@ -664,25 +792,25 @@
         number = (2, n_z - 1, n_z - 1)[group]
         if number <= 3:
             if number:
-                count_in(s, first, number)
+                count_in(s, first, number, group)
         else:
-            loop(first, first + number, lambda i: count_in(s, i, 1))
+            loop(first, first + number, lambda i: count_in(s, i, 1, group))
 
     count(0, 0)
     fin_near.wait_recv()
     turn_fin(1)
     count(1, 0)
-    each(2, n_z, hand_on)
     fin_far.wait_recv()
     fin_relay.start()
     turn_fin(2)
     count(2, 0)
-    loop(2, n_z + 1, prepare)
-    count(2, 1)
     fin_relay.wait_recv()
     turn_fin(3)
     count(3, 0)
+    loop(3, n_z, hand_on)
+    loop(2, n_z + 1, prepare)
     count(3, 1)
+    count(2, 1)
     count(0, 1)
     count(1, 1)
 
@@ -731,17 +859,26 @@
     total = r.stat_s[0, 1:2, :]
     log_total = r.stat_s[0, 0:1, :] + jnp.log(total)
     r.tot_s[0] = jnp.broadcast_to(jnp.where(valid_lane > 0, log_total, -NEG), (8, span))
-    def end_pass(k):
-        to_far(k).wait_send()
-        to_near(k).wait_send()
-        relay(k).wait_send()
-
-    each(0, n_dp, end_pass)
-
-    t_base = wire.take(4)
-    tell = Group(
-        *[wire.make(r.tot_s.at[0], r.tot_s.at[s], t_base + s, here.ffn(s)) for s in (1, 2, 3)]
-    )
+    for copy in (
+        all_passes(0, 0),
+        all_passes(0, 1),
+        all_passes(2, 2),
+        to_far(len(cuts)),
+        to_near(len(cuts)),
+        relay(len(cuts)),
+    ):
+        copy.wait_send()
+
+    t_base = wire.take(1)
+
+    def to_members(ref, number):
+        three = ref.at[pl.ds(1, 3)]
+        return Joined(
+            [wire.make(ref.at[0], ref.at[s], number, here.ffn(s)) for s in (1, 2, 3)],
+            wire.make(three, three, number, here.side()),
+        )
+
+    tell = to_members(r.tot_s, t_base)
     tell.start()
     ended.append(tell)
     if not kept(n_dp):
@@ -771,15 +908,35 @@
     for i, s in enumerate((1, 3)):
         for j in range(2):
             r.fnear_send[i, j * width : (j + 1) * width, :] = lowered(r.gf_s[s, j])
-    e_base = wire.take(4)
+    all_asks = wire.make(r.req.at[others], r.req.at[others], q_base, here.side())
+    for copy in (all_asks, all_replies(), all_biases(), w_far, w_near, w_relay):
+        copy.wait_send()
+    def end_offers(j):
+        pl.when(has_up & (here.z >= j))(lambda: send_up(j).wait_send())
+        pl.when(has_down & (here.z + j < n_z))(lambda: send_down(j).wait_send())
+
+    each(0, n_z, end_offers)
+    each(0, n_z, lambda k: offer_side(k).wait_send())
+    for copy in ended:
+        copy.wait_send()
+    ended.clear()
+    wire.renew()
+    e_base = wire.take(6)
     f_near = wire.make(r.fnear_send, r.fnear_got, e_base, here.ffn(1))
     f_far = wire.make(r.ffar_send, r.ffar_got, e_base + 1, here.ffn(2))
     s_near = wire.make(r.snear_send, r.snear_got, e_base + 2, here.ffn(1))
     s_far = wire.make(r.sfar_send, r.sfar_got, e_base + 3, here.ffn(2))
-    ended += [f_near, f_far, s_near, s_far]
+    e_near = wire.make(r.enear_send, r.enear_got, e_base + 4, here.ffn(1))
+    e_far = wire.make(r.efar_send, r.efar_got, e_base + 5, here.ffn(2))
+    ended += [f_near, f_far, s_near, s_far, e_near, e_far]
     f_near.start()
 
     tell.wait_recv()
+    if kept(n_dp):
+        for s in range(4):
+            for group in range(3):
+                level = r.stat_s[s, 2 + group : 3 + group, :] - r.tot_s[s, 0:1, :]
+                r.scale_s[group : group + 1, s * span : (s + 1) * span] = jnp.exp(level)
     side_base, line_base = wire.take(n_z), wire.take(n_z)
 
     def cand_side(k):
@@ -789,6 +946,11 @@
         return wire.make(r.cand_send.at[k], r.line_got.at[k], line_base + k, here.down(k))
 
     def cand_grad(i):
+        if kept(n_dp):
+            group = jnp.where(i < 2, 0, jnp.where(i <= n_z, 1, 2))
+            share_of = r.scale_s[pl.ds(group, 1), :]
+            weights = raised(r.expo_s[at(i, span), :]) * share_of
+            return dot(lowered(weights), r.fin_s[...])
         column = jnp.concatenate([columns(i, 1)] * (4 * span // 128), 1)
         level = jnp.concatenate([r.tot_s[s, 0:1, :] for s in range(4)], 1)
         logits = dot(r.cands[at(i, span), :], r.fint_s[...]) + column
@@ -810,11 +972,10 @@
 
     middle = n_z // 2
     side_step(middle)
-
-    def side_rest(k):
-        side_step(lax.rem(k + middle, n_z))
-
-    loop(1, n_z, side_rest)
+    loop(1, middle, side_step)
+    loop(middle + 1, n_z, side_step)
+    if middle:
+        side_step(0)
 
     grad_normed2 = against(
         r.act_s[...], jnp.concatenate([r.weights[s, 0] for s in range(4)], 1)
@@ -840,6 +1001,15 @@
     r.kv_s[...] = dot(r.p16_s[...], r.stack_s[...])
     r.logit_s[span : 2 * span, :] = r.kv_s[span:, :]
     r.own_s[...] = r.kv_s[0:span, :]
+    k_base = wire.take(2)
+
+    def lend(i):
+        rows = at(i, span)
+        return wire.make(r.logit_s.at[rows], r.kv_got.at[rows], k_base + i, here.ffn(1))
+
+    lend_k, lend_v = lend(0), lend(1)
+    ended += [lend_k, lend_v]
+    lend_v.start()
 
     def backward_head(h):
         rows = at(h, HD)
@@ -854,16 +1024,44 @@
     loop(0, heads // 2, backward_head)
     if middle:
         line_step(middle)
+    strip = span // 4
+    halves = (jnp.where(half == 0, 1.0, 0.0), jnp.where(half == 1, 1.0, 0.0))
+
+    def strip_at(s):
+        return pl.ds(pl.multiple_of(here.member[s] * strip, strip), strip)
+
+    def early_pieces(s):
+        yield 0, r.acc_s[strip_at(s), 3 * width :]
+        yield strip, r.acc_s[strip_at(s), 2 * width : 3 * width]
+
+    def pieces(s):
+        for j in range(2):
+            yield j * strip, r.acc_s[strip_at(s), j * width : (j + 1) * width]
+        for u in range(2):
+            yield (2 + u) * strip, r.h0_s[strip_at(s), :] * halves[u]
+
+    lend_v.wait_recv()
+    r.gv_s[...] = lowered(r.own_s[...] + r.kv_got[span:, :])
+    r.acc_s[:, 2 * width : 3 * width] = across(r.n1_s[...], r.gv_s[...])
+    for i, s in enumerate((1, 3)):
+        for first, value in early_pieces(s):
+            r.enear_send[i, first : first + strip, :] = lowered(value)
+    e_near.start()
     loop(heads // 2, heads, backward_head)
+    loop(1, middle, line_step)
+    e_near.wait_recv()
+    for first, value in early_pieces(2):
+        got = raised(r.enear_got[1, first : first + strip, :])
+        r.efar_send[first : first + strip, :] = lowered(value + got)
+    e_far.start()
     queries = raised(r.q_s[...])
     for h in range(heads):
         r.stack_s[h * span : (h + 1) * span, :] = lowered(jnp.where(lane_head == h, queries, 0.0))
     r.kv_s[...] = dot(r.p16_s[...], r.stack_s[...]) * scale
     r.logit_s[0:span, :] = r.kv_s[span:, :]
-    k_base = wire.take(1)
-    lend = wire.make(r.logit_s.at[at(0, 2 * span)], r.kv_got, k_base, here.ffn(1))
-    ended.append(lend)
-    lend.start()
+    lend_k.start()
+    loop(middle + 1, n_z, line_step)
+    r.h2_s[...] = cand_grad(0)
     ffn_part, strip_part = parts(n_dp, span, width)
     f_far.wait_recv()
     for j in range(2):
@@ -871,9 +1069,16 @@
         r.pre_s[rows, :] = (
             r.gf_s[0, j] + raised(r.fnear_got[0, rows, :]) + raised(r.ffar_got[rows, :])
         )
-    if n_dp * ffn_part > 2 * width:
-        r.pre_s[2 * width : n_dp * ffn_part, :] = jnp.zeros(
-            (n_dp * ffn_part - 2 * width, width), FULL
+    e_far.wait_recv()
+    early_rows = 2 * width + 2 * strip
+    for first, value in early_pieces(0):
+        rows = slice(first, first + strip)
+        r.pre_s[2 * width + first : 2 * width + first + strip, :] = (
+            value + raised(r.enear_got[0, rows, :]) + raised(r.efar_got[rows, :])
+        )
+    if n_dp * ffn_part > early_rows:
+        r.pre_s[early_rows : n_dp * ffn_part, :] = jnp.zeros(
+            (n_dp * ffn_part - early_rows, width), FULL
         )
     m_base = wire.take(2 + 2 * n_z)
 
@@ -938,35 +1143,18 @@
     ffn_side()
 
 
-    loop(1, middle, line_step)
-    loop(middle + 1, n_z, line_step)
     grad_q = lowered(r.dq_s[...].T)
-    lend.wait_recv()
-    grad_united = jnp.concatenate(
-        [
-            grad_q,
-            lowered(r.kv_s[0:span, :] + r.kv_got[0:span, :]),
-            lowered(r.own_s[...] + r.kv_got[span:, :]),
-        ],
+    lend_k.wait_recv()
+    grad_qk = jnp.concatenate(
+        [grad_q, lowered(r.kv_s[0:span, :] + r.kv_got[0:span, :])],
         1,
     )
+    grad_united = jnp.concatenate([grad_qk, r.gv_s[...]], 1)
     grad_h0_norm, gain_grad1 = rms_back(r.h0_s[...], gain1, against(grad_united, r.wq16[...]))
     grad_h0 = r.h1_s[...] + grad_h0_norm
     r.h0_s[...] = grad_h0
 
-    r.acc_s[:, : 3 * width] = across(r.n1_s[...], grad_united)
-
-    strip = span // 4
-    strip_rows = 6 * strip
-    halves = (jnp.where(half == 0, 1.0, 0.0), jnp.where(half == 1, 1.0, 0.0))
-
-    def pieces(s):
-        rows = pl.ds(pl.multiple_of(here.member[s] * strip, strip), strip)
-        for j in range(3):
-            yield j * strip, r.acc_s[rows, j * width : (j + 1) * width]
-        yield 3 * strip, r.acc_s[rows, 3 * width :]
-        for u in range(2):
-            yield (4 + u) * strip, r.h0_s[rows, :] * halves[u]
+    r.acc_s[:, : 2 * width] = across(r.n1_s[...], grad_qk)
 
     for i, s in enumerate((1, 3)):
         for first, value in pieces(s):
@@ -1001,31 +1189,21 @@
     small = jnp.where(row8 == 1, gain_grad2, small)
     small = jnp.where(row8 == 2, gain_grad3, small)
     r.small[0, 0] = jnp.where(row8 == 3, stats, small)
-    l_base = wire.take(4)
-
-    def to_members(row, base):
-        return Group(
-            *[
-                wire.make(r.small.at[row, 0], r.small.at[row, s], base + s, here.ffn(s))
-                for s in (1, 2, 3)
-            ]
-        )
-
-    tell_small = to_members(0, l_base)
+    l_base = wire.take(1)
+
+    tell_small = to_members(r.small.at[0], l_base)
     tell_small.start()
     ended.append(tell_small)
 
-    grad = cand_grad(0)
     s_near.wait_recv()
     for first, value in pieces(2):
         got = raised(r.snear_got[1, first : first + strip, :])
         r.sfar_send[first : first + strip, :] = lowered(value + got)
     s_far.start()
-    ffn_line()
     cand_side(0).wait_send()
     cand_side(0).wait_recv()
     r.own_s[...] = (
-        grad + raised(r.side_got[0]) - valid_col * raised(r.fin_s[0:span, :])
+        r.h2_s[...] + raised(r.side_got[0]) - valid_col * raised(r.fin_s[0:span, :])
     )
 
     def add_line(k):
@@ -1036,6 +1214,8 @@
     r.found[span : 2 * span, :] = lowered(r.own_s[...])
     out_far.start()
     out_near.start()
+
+    ffn_line()
 
     in_far.wait_recv()
     in_relay.start()
@@ -1046,54 +1226,44 @@
         r.strip_s[rows, :] = (
             value + raised(r.snear_got[0, rows, :]) + raised(r.sfar_got[rows, :])
         )
-    if n_dp * strip_part > strip_rows:
-        r.strip_s[strip_rows:, :] = jnp.zeros((n_dp * strip_part - strip_rows, width), FULL)
+    late_rows = 4 * strip
+    if n_dp * strip_part > late_rows:
+        r.strip_s[late_rows:, :] = jnp.zeros((n_dp * strip_part - late_rows, width), FULL)
     strip_side()
 
     order = here.y * n_z + here.z
-    v_base = wire.take(2 * n_z + 2)
+    v_base = wire.take(4)
 
     def gather_dp(ref, size, base):
         own_part = ref.at[at(order, size)]
         own_column = ref.at[at(here.y, n_z * size)]
 
         def line(k):
-            return wire.make(own_part, own_part, base + k, here.up(k))
-
-        return line, wire.make(own_column, own_column, base + n_z, here.side())
+            return wire.make(own_part, own_part, base, here.up(k))
+
+        others = ref.at[pl.ds(0, (n_z - 1) * size)]
+        lines = Joined(
+            [line(k) for k in range(1, n_z)], wire.make(others, others, base, here.side())
+        )
+        return lines, wire.make(own_column, own_column, base + 1, here.side())
 
     ffn_all, ffn_all_side = gather_dp(r.whole_f, ffn_part, v_base)
-    strip_all, strip_all_side = gather_dp(r.whole_t, strip_part, v_base + n_z + 1)
-    ended += [ffn_all_side, strip_all_side]
+    strip_all, strip_all_side = gather_dp(r.whole_t, strip_part, v_base + 2)
+    ended += [ffn_all, strip_all, ffn_all_side, strip_all_side]
     mine = ffn_finish()
     squares = total_of(mine * mine)
     r.whole_f[at(order, ffn_part), :] = lowered(mine)
-    each(1, n_z, lambda k: ffn_all(k).start())
-
-    for s in range(4):
-        for column in range(2):
-            chunk_row = pl.ds(column * 4 + here.member[s], 1)
-            r.p16_s[0:cap, (2 * s + column) * span : (2 * s + column + 1) * span] = lowered(
-                one_hot_columns(r.slot_s[chunk_row, :], cap)
-            )
-    where_to = jnp.concatenate(
-        [
-            r.kind_s[pl.ds(column * 4 + here.member[s], 1), :]
-            for s in range(4)
-            for column in range(2)
-        ],
-        1,
-    )
-    where_to = lowered(jnp.broadcast_to(where_to, (16, 8 * span)))
-
+    ffn_all.start()
     tell_small.wait_recv()
     r.small[1, 0] = (r.small[0, 0] + r.small[0, 1]) + (r.small[0, 2] + r.small[0, 3])
-    h_base = wire.take(2 * n_dp)
+    h_base = wire.take(2)
 
     def share(row, k, number):
-        return wire.make(
-            r.small.at[row, 0], r.small_dp.at[row // 4, d], number + k, here.ahead(k)
-        )
+        return wire.make(r.small.at[row, 0], r.small_dp.at[row // 4, d], number, here.ahead(k))
+
+    def all_shares(row, number):
+        others = r.small_dp.at[row // 4, pl.ds(0, n_dp - 1)]
+        return wire.make(others, others, number, here.side())
 
     each(1, n_dp, lambda k: share(1, k, h_base).start())
     r.small_dp[0, d] = r.small[1, 0]
@@ -1102,52 +1272,47 @@
     out_relay.start()
 
     strip_line()
-    each(1, n_z, lambda k: ffn_all(k).wait_recv())
-    ffn_all_side.start()
 
     in_near.wait_recv()
     in_relay.wait_recv()
     out_near.wait_recv()
     out_relay.wait_recv()
 
-    g_base = wire.take(n_dp)
+    g_base = wire.take(1)
 
     def outgoing(k):
         return pl.ds(pl.multiple_of(8 * span + k * cap, cap), cap)
 
     def ship(k):
         return wire.make(
-            r.found.at[outgoing(k)], r.incoming.at[at(k, cap)], g_base + k, here.ahead(k)
-        )
-
-    zero16 = jnp.zeros((16, 8 * span), LOW)
-
-    def choose(k):
-        wanted = where_to == lowered(jnp.full((16, 8 * span), k, FULL))
-        picked = jnp.concatenate(
-            [
-                jnp.where(wanted, r.p16_s[i * 16 : (i + 1) * 16, :], zero16)
-                for i in range(cap // 16)
-            ],
-            0,
-        )
-        return lowered(dot(picked, r.found[0 : 8 * span, :]))
-
-    def fill_rows(k):
-        r.found[outgoing(k), :] = choose(k)
-
-    fill_rows(n_z)
+            r.found.at[outgoing(k)], r.incoming.at[at(k, cap)], g_base, here.ahead(k)
+        )
+
+    def all_rows():
+        rows = pl.ds(8 * span + cap, (n_dp - 1) * cap)
+        landed = r.incoming.at[pl.ds(cap, (n_dp - 1) * cap)]
+        return wire.make(r.found.at[rows], landed, g_base, here.side())
+
+    places = pl.ds(8 * span, filled)
+    if kept(n_dp):
+        r.found[places, :] = lowered(dot(r.pick_s[...], r.found[0 : 8 * span, :]))
+    else:
+        marks_to = build_marks()
+
+        def choose(k):
+            chosen = picks(marks_to, k)
+            r.found[outgoing(k), :] = lowered(dot(chosen, r.found[0 : 8 * span, :]))
+
+        loop(0, n_dp, choose)
     ship(n_z).start()
-    loop(1, n_z, fill_rows)
-    loop(n_z + 1, n_dp, fill_rows)
+    r.incoming[0:cap, :] = r.found[outgoing(0), :]
 
     mine = strip_finish()
     squares = squares + total_of(mine * mine)
     r.whole_t[at(order, strip_part), :] = lowered(mine)
-    each(1, n_z, lambda k: strip_all(k).start())
+    strip_all.start()
     each(1, n_z, lambda k: ship(k).start())
     each(n_z + 1, n_dp, lambda k: ship(k).start())
-    r.incoming[0:cap, :] = choose(0)
 
     several = min(n_dp, 8)
 
@@ -1160,24 +1325,54 @@
     if n_dp == several:
         own_marks(0)
 
-    each(1, n_z, lambda k: strip_all(k).wait_recv())
+    ffn_all.wait_recv()
+    ffn_all_side.start()
+
+    strip_all.wait_recv()
     strip_all_side.start()
 
-    ffn_all_side.wait_recv()
-    r.ffn_grad[...] = r.whole_f[0 : 2 * width, :]
-
     strip_all_side.wait_recv()
-    r.strips[f] = r.whole_t[0:strip_rows, :]
-    c_base = wire.take(3)
-    mine_at, far_at = r.strips.at[f], r.strips.at[far]
-    strip_far = wire.make(mine_at, mine_at, c_base, here.ffn(2))
-    strip_near = wire.make(mine_at, mine_at, c_base + 1, here.ffn(1))
-    strip_relay = wire.make(far_at, far_at, c_base + 2, here.ffn(1))
-    ended += [strip_far, strip_near, strip_relay]
+    c_base = wire.take(6)
+
+    def spread_strips(first, rows, base):
+        part = pl.ds(first, rows)
+        mine_at, far_at = r.strips.at[f, part], r.strips.at[far, part]
+        copies = (
+            wire.make(mine_at, mine_at, base, here.ffn(2)),
+            wire.make(mine_at, mine_at, base + 1, here.ffn(1)),
+            wire.make(far_at, far_at, base + 2, here.ffn(1)),
+        )
+        ended.extend(copies)
+        return copies
+
+    r.strips[f, 2 * strip :, :] = r.whole_t[0:late_rows, :]
+    strip_far, strip_near, strip_relay = spread_strips(2 * strip, late_rows, c_base + 3)
     strip_far.start()
     strip_near.start()
-
-    each(1, n_dp, lambda k: ship(k).wait_recv())
+    ffn_all_side.wait_recv()
+    outs = [
+        pltpu.make_async_copy(src, dst, r.load_sems.at[i])
+        for i, (src, dst) in enumerate(
+            (
+                (r.whole_f.at[pl.ds(0, 2 * width)], r.ffn_out),
+                (r.table_grad, r.table_out),
+            )
+        )
+    ]
+
+    def strip_out(s):
+        place = here.member[s]
+        return pltpu.make_async_copy(
+            r.strips.at[place], r.strips_out.at[place], r.load_sems.at[2 + s]
+        )
+
+    outs[0].start()
+    r.strips[f, 0 : 2 * strip, :] = r.whole_f[2 * width : early_rows, :]
+    early_far, early_near, early_relay = spread_strips(0, 2 * strip, c_base)
+    early_far.start()
+    early_near.start()
+
+    all_rows().wait_recv()
 
     if n_dp == several:
         r.table_grad[...] = dot(r.owned[...], r.incoming[...])
@@ -1194,22 +1389,30 @@
             r.table_grad[...] = r.table_grad[...] + dot(r.owned[...], r.padded_in[...])
 
         loop(0, n_dp // several, add_rows)
+    outs[1].start()
     table_grad = r.table_grad[...]
     squares = squares + total_of(table_grad * table_grad)
 
     r.small[3, 0] = jnp.broadcast_to(squares, (8, width))
-    tell_norm = to_members(3, wire.take(4))
+    tell_norm = to_members(r.small.at[3], wire.take(1))
     tell_norm.start()
     ended.append(tell_norm)
-    each(1, n_dp, lambda k: share(1, k, h_base).wait_recv())
+    all_shares(1, h_base).wait_recv()
     tell_norm.wait_recv()
     r.small[4, 0] = (r.small[3, 0] + r.small[3, 1]) + (r.small[3, 2] + r.small[3, 3])
 
-    each(1, n_dp, lambda k: share(4, k, h_base + n_dp).start())
+    each(1, n_dp, lambda k: share(4, k, h_base + 1).start())
     r.small_dp[1, d] = r.small[4, 0]
+    early_far.wait_recv()
+    early_relay.start()
+    early_near.wait_recv()
+    strip_near.wait_recv()
+    strip_out(0).start()
+    strip_out(1).start()
     strip_far.wait_recv()
     strip_relay.start()
-    each(1, n_dp, lambda k: share(4, k, h_base + n_dp).wait_recv())
+    strip_out(2).start()
+    all_shares(4, h_base + 1).wait_recv()
     totals, squares = r.small_dp[0, 0], r.small_dp[1, 0]
     for k in range(1, n_dp):
         totals = totals + r.small_dp[0, k]
@@ -1218,45 +1421,39 @@
     norm = jnp.sqrt(squares + total_of(gains * gains))
     r.sums[...] = jnp.where(row8 == 4, norm, totals)
 
-    def end_dp(k):
-        ask(k).wait_send()
-        reply(k).wait_send()
-        ship(k).wait_send()
-        share(1, k, h_base).wait_send()
-        share(4, k, h_base + n_dp).wait_send()
-
-    each(1, n_dp, end_dp)
-
-    def end_side(k):
-        offer_side(k).wait_send()
-
-    each(0, n_z, end_side)
+    all_rows().wait_send()
+    all_shares(1, h_base).wait_send()
+    all_shares(4, h_base + 1).wait_send()
+
 
     def end_line(k):
-        offer_line(k).wait_send()
         cand_line(k).wait_send()
-        ffn_all(k).wait_send()
-        strip_all(k).wait_send()
 
     each(1, n_z, end_line)
+
     ffn_end()
     strip_end()
-    strip_near.wait_recv()
+    early_relay.wait_recv()
     strip_relay.wait_recv()
+    strip_out(3).start()
+    for copy in outs + [strip_out(s) for s in range(4)]:
+        copy.wait()
     for copy in ended:
         copy.wait_send()
+    assert wire.arrived <= r.recv_sems.shape[0]
+    assert wire.most <= r.send_sems.shape[0]
 
 
 def step(n_dp, cap, owner, row, lengths, count, table, wq, wo, w_in, w_back, gains, positions):
     rows_dev, width = table.shape
     span = owner.shape[1] // 4
-    heads = width // HD
+    heads, n_z = width // HD, n_dp // 2
     shapes = plan(n_dp, cap, rows_dev, span, width, heads)
     names = INPUTS + OUTPUTS + list(shapes) + ["load_sems", "send_sems", "recv_sems"]
     vmem = pl.BlockSpec(memory_space=pltpu.VMEM)
     smem = pl.BlockSpec(memory_space=pltpu.SMEM)
     rest = pl.BlockSpec(memory_space=pl.ANY)
-    number = 20 * n_dp + 80
+    sends, arrivals = 6 * n_z + 23, 18 * n_z + 48
 
     def out(kind, *shape):
         return jax.ShapeDtypeStruct(shape, kind)
@@ -1269,13 +1466,13 @@
             out(LOW, 4, 6 * span // 4, width),
             out(FULL, 8, width),
         ),
-        in_specs=[vmem, vmem, smem, vmem, rest, rest, rest, vmem, vmem, vmem, rest],
-        out_specs=(vmem,) * 4,
+        in_specs=[vmem, vmem, smem, vmem, rest, rest, rest, rest, rest, vmem, rest],
+        out_specs=(rest, rest, rest, vmem),
         scratch_shapes=[pltpu.VMEM(shape[:-1], shape[-1]) for shape in shapes.values()]
         + [
-            pltpu.SemaphoreType.DMA((4,)),
-            pltpu.SemaphoreType.DMA((number,)),
-            pltpu.SemaphoreType.DMA((number,)),
+            pltpu.SemaphoreType.DMA((6,)),
+            pltpu.SemaphoreType.DMA((sends,)),
+            pltpu.SemaphoreType.DMA((arrivals,)),
         ],
         compiler_params=pltpu.CompilerParams(
             collective_id=0,
@@ -1340,8 +1537,8 @@
     ]
     grads[0].start()
     for number in range(len(work)):
-        for copy in moves(number)[0]:
-            copy.start()
+        for i, copy in enumerate(moves(number)[0]):
+            copy.start(priority=(number + i) % 2)
         if number == 1:
             grads[1].start()
             grads[2].start()
@@ -1389,12 +1586,12 @@
         for m in range(4):
             at_rows = slice(m * strip, (m + 1) * strip)
             if which == 1:
-                for j in range(3):
+                for j, i in enumerate((2, 3, 1)):
                     lanes = slice(j * width, (j + 1) * width)
-                    grad = strips_s[m, j * strip : (j + 1) * strip, :]
+                    grad = strips_s[m, i * strip : (i + 1) * strip, :]
                     adam(1, at_rows, lanes, grad, LEARN)
             elif which == 2:
-                adam(2, at_rows, every, strips_s[m, 3 * strip : 4 * strip, :], LEARN)
+                adam(2, at_rows, every, strips_s[m, 0:strip, :], LEARN)
             elif which == 6:
                 for u in range(2):
                     at_rows = slice((4 * u + m) * strip, (4 * u + m + 1) * strip)

time: 131 us -> 125 us (0.954)
  Pallas kernels: 130 us -> 124 us
    pallas_call x1, Pallas kernels: 121 us -> 115 us  [step(): pl.pallas_call(functools.partial(step_kernel, n_dp, cap, names), out_shap...]
where the time goes in v3:
time: 125 us
  Pallas kernels  124 us (99%)
    pallas_call x1, Pallas kernels, step(): pl.pallas_call(functools.partial(step_kernel, n_dp, cap, names), out_shap...  115 us
    pallas_call x1, Pallas kernels, update(): pl.pallas_call(functools.partial(update_kernel, rows_dev), out_shape=tupl...  8.9 us

profile of v3, /device:TPU:0, one launch (start us, length us, event | category | flops | bytes accessed | tf_op | source)
XLA Modules:
  0.0 124.6 jit_solution(10123997250341020146)
XLA Ops:
  0.7 114.8 %step.1 = (f32[784,256]{1,0:T(8,128)}, bf16[512,256]{1,0:T(8,128)(2,1)}, bf16[4,384,256]{2,1,0:T(8,128)(2,1)}, f32[8,256]{1,0:T(8,128)}) custom-call(s32[2,1024]{1,0:T(2,128)} %bitcast.2, s32[2,1024]{1,0:T(2,128)} %bitcast.3, s32[2]{0:T(128)} %refs_2_.2, s32[784]{0:T(1024)} %refs_3_.2, f32[784,256]{1,0:T(8,128)} %refs_0_.1, f32[256,768]{1,0:T(8,128)} %refs_3_.3, ...), custom_call_target="tpu_custom_call" | custom-call | tf_op jit(solution)/shard_map/step/pallas_call | solution.py:1461
  115.5 8.9 %update.1 = (f32[2]{0:T(128)}, f32[3]{0:T(128)}, f32[1]{0:T(128)}, f32[784,256]{1,0:T(8,128)}, f32[784,256]{1,0:T(8,128)}, /*index=5*/f32[784,256]{1,0:T(8,128)}...) custom-call(f32[784,256]{1,0:T(8,128)} %get-tuple-element.28.table_g, ...), custom_call_target="tpu_custom_call" | custom-call | tf_op jit(solution)/shard_map/update/pallas_call | solution.py:1627

commit v4 on v3

--- a/solution.py
+++ b/solution.py
@@ -336,6 +336,7 @@
         "whole_t": (n_dp * strip_part, width, LOW),
         "incoming": (filled, width, LOW),
         "place_s": (3 * span if kept(n_dp) else 16, 4 * filled if kept(n_dp) else 128, LOW),
+        "placing_s": (3 * span if kept(n_dp) else 16, width, FULL),
         "placed_s": (3 * span if kept(n_dp) else 16, width, LOW),
         "pick_s": (filled if kept(n_dp) else 16, 8 * span, LOW),
         "padded_in": (8 * 128 if cap < 128 else 16, width, LOW),
@@ -581,18 +582,23 @@
     to_near(len(cuts)).start()
     w_far.wait_recv()
     w_relay.start()
-    for i in range(len(cuts) - 2, len(cuts) + 1):
-        relay_on(i)
+    relay_on(len(cuts) - 2)
+    for i in range(len(cuts)):
+        to_near(i).wait_recv()
+    if kept(n_dp):
+        r.placing_s[...] = dot(r.place_s[:, : 2 * filled], r.found[0 : 2 * filled, :])
+    relay_on(len(cuts) - 1)
+    relay_on(len(cuts))
     loads[1].wait()
     loads[2].wait()
     r.wq16[...] = lowered(r.wq_s[...])
     r.wo16[...] = lowered(r.wo_s[...])
     for i in range(len(cuts)):
-        to_near(i).wait_recv()
         relay(i).wait_recv()
 
     if kept(n_dp):
-        r.placed_s[...] = lowered(dot(r.place_s[...], r.found[...]))
+        far_rows = dot(r.place_s[:, 2 * filled :], r.found[2 * filled :, :])
+        r.placed_s[...] = lowered(r.placing_s[...] + far_rows)
 
     def chosen_rows(i):
         if kept(n_dp):
@@ -613,8 +619,8 @@
     bias = jnp.sum(dot(bias_rows, r.hot[at(chunk, kinds), :]) * marks, 0, keepdims=True)
     r.bias_s[...] = jnp.broadcast_to(bias, (8, span))
     r.cand_bias[0] = jnp.broadcast_to(jnp.where(lane + begin < length, -bias, NEG), (8, span))
-    z_base, y_base = wire.take(0, 2 * n_z), wire.take(2 * n_z)
-    u_base = wire.take(4 * n_z, 0)
+    z_base, y_base = wire.take(0, 3 * n_z), wire.take(3 * n_z)
+    u_base = wire.take(6 * n_z, 0)
     has_up, has_down = here.z + 1 < n_z, here.z > 0
 
     def slot(k, ky):
@@ -622,51 +628,73 @@
             return ky
         return 1 + k + ky * (n_z - 1)
 
+    half_rows = span // 2
+
+    def half_of(i, h):
+        first = i * span + h * half_rows
+        if not isinstance(first, int):
+            first = pl.multiple_of(first, half_rows)
+        return r.cands.at[pl.ds(first, half_rows)]
+
     def offer_line(source, target, number, where):
         i, j = slot(source, 0), slot(target, 0)
-        return Group(
+        first, second = (
             wire.make(
-                r.cands.at[at(i, span)], r.cands.at[at(j, span)], number, where, z_base + target
-            ),
-            wire.make(
-                r.cand_bias.at[i],
-                r.cand_bias.at[j],
-                number + 2 * n_z,
+                half_of(i, h),
+                half_of(j, h),
+                number + 2 * n_z * h,
                 where,
-                z_base + n_z + target,
-            ),
-        )
+                z_base + (n_z * h + target),
+            )
+            for h in range(2)
+        )
+        bias = wire.make(
+            r.cand_bias.at[i],
+            r.cand_bias.at[j],
+            number + 4 * n_z,
+            where,
+            z_base + (2 * n_z + target),
+        )
+        return first, Group(second, bias)
 
     def send_up(a):
         return offer_line(a, a + 1, u_base + a, here.up(1))
 
     def send_down(b):
         source = b if isinstance(b, int) and b == 0 else n_z - b
-        return offer_line(source, n_z - 1 - b, u_base + n_z + b, here.down(1))
+        return offer_line(source, n_z - 1 - b, u_base + (n_z + b), here.down(1))
 
     def offer_side(k):
         i, j = slot(k, 0), slot(k, 1)
-        return Group(
-            wire.make(r.cands.at[at(i, span)], r.cands.at[at(j, span)], y_base + k, here.side()),
-            wire.make(r.cand_bias.at[i], r.cand_bias.at[j], y_base + n_z + k, here.side()),
-        )
-
-    offer_side(0).start()
-    pl.when(has_up)(lambda: send_up(0).start())
-    pl.when(has_down)(lambda: send_down(0).start())
+        first, second = (
+            wire.make(half_of(i, h), half_of(j, h), y_base + (n_z * h + k), here.side())
+            for h in range(2)
+        )
+        bias = wire.make(
+            r.cand_bias.at[i], r.cand_bias.at[j], y_base + (2 * n_z + k), here.side()
+        )
+        return first, Group(second, bias)
+
+    for h in range(2):
+        pl.when(has_up)(lambda: send_up(0)[h].start())
+        pl.when(has_down)(lambda: send_down(0)[h].start())
+    for h in range(2):
+        offer_side(0)[h].start()
 
     def hand_on(j):
         @pl.when(here.z >= j)
         def from_below():
-            offer_line(0, j, u_base, here.up(1)).wait_recv()
-            pl.when(has_up)(lambda: send_up(j).start())
-            offer_side(j).start()
+            for h in range(2):
+                offer_line(0, j, u_base, here.up(1))[h].wait_recv()
+                pl.when(has_up)(lambda: send_up(j)[h].start())
+                offer_side(j)[h].start()
 
         @pl.when(here.z + j < n_z)
         def from_above():
-            offer_line(0, n_z - j, u_base, here.up(1)).wait_recv()
-            pl.when(has_down)(lambda: send_down(j).start())
-            offer_side(n_z - j).start()
+            for h in range(2):
+                offer_line(0, n_z - j, u_base, here.up(1))[h].wait_recv()
+                pl.when(has_down)(lambda: send_down(j)[h].start())
+                offer_side(n_z - j)[h].start()
 
     loads[3].wait()
     gain1, gain2, gain3 = r.gains[0:1, :], r.gains[1:2, :], r.gains[2:3, :]
@@ -758,7 +786,8 @@
         return pl.ds(pl.multiple_of(i * span, span), number * span)
 
     prepare(0)
-    offer_side(0).wait_recv()
+    for copy in offer_side(0):
+        copy.wait_recv()
     prepare(1)
     r.acc_s[...] = jnp.zeros_like(r.acc_s)
     for s in range(4):
@@ -803,11 +832,11 @@
     fin_far.wait_recv()
     fin_relay.start()
     turn_fin(2)
+    loop(3, n_z, hand_on)
     count(2, 0)
     fin_relay.wait_recv()
     turn_fin(3)
     count(3, 0)
-    loop(3, n_z, hand_on)
     loop(2, n_z + 1, prepare)
     count(3, 1)
     count(2, 1)
@@ -815,7 +844,8 @@
     count(1, 1)
 
     def prepare_side(k):
-        offer_side(k).wait_recv()
+        for copy in offer_side(k):
+            copy.wait_recv()
         prepare(slot(k, 1))
 
     loop(1, n_z, prepare_side)
@@ -912,11 +942,12 @@
     for copy in (all_asks, all_replies(), all_biases(), w_far, w_near, w_relay):
         copy.wait_send()
     def end_offers(j):
-        pl.when(has_up & (here.z >= j))(lambda: send_up(j).wait_send())
-        pl.when(has_down & (here.z + j < n_z))(lambda: send_down(j).wait_send())
+        for h in range(2):
+            pl.when(has_up & (here.z >= j))(lambda: send_up(j)[h].wait_send())
+            pl.when(has_down & (here.z + j < n_z))(lambda: send_down(j)[h].wait_send())
+            offer_side(j)[h].wait_send()
 
     each(0, n_z, end_offers)
-    each(0, n_z, lambda k: offer_side(k).wait_send())
     for copy in ended:
         copy.wait_send()
     ended.clear()
@@ -1453,7 +1484,7 @@
     vmem = pl.BlockSpec(memory_space=pltpu.VMEM)
     smem = pl.BlockSpec(memory_space=pltpu.SMEM)
     rest = pl.BlockSpec(memory_space=pl.ANY)
-    sends, arrivals = 6 * n_z + 23, 18 * n_z + 48
+    sends, arrivals = 9 * n_z + 23, 20 * n_z + 48
 
     def out(kind, *shape):
         return jax.ShapeDtypeStruct(shape, kind)

time: 125 us -> 124 us (level)
  Pallas kernels: 124 us -> 122 us
    pallas_call x1, Pallas kernels: 115 us -> 114 us  [step(): pl.pallas_call(functools.partial(step_kernel, n_dp, cap, names), out_shap...]
where the time goes in v4:
time: 124 us; the launch traced here: 123 us
  Pallas kernels  122 us (98%)
    pallas_call x1, Pallas kernels, step(): pl.pallas_call(functools.partial(step_kernel, n_dp, cap, names), out_shap...  114 us
    pallas_call x1, Pallas kernels, update(): pl.pallas_call(functools.partial(update_kernel, rows_dev), out_shape=tupl...  8.9 us

profile of v4, /device:TPU:0, one launch (start us, length us, event | category | flops | bytes accessed | tf_op | source)
XLA Modules:
  0.0 123.3 jit_solution(10535894038721322143)
XLA Ops:
  0.7 113.5 %step.1 = (f32[784,256]{1,0:T(8,128)}, bf16[512,256]{1,0:T(8,128)(2,1)}, bf16[4,384,256]{2,1,0:T(8,128)(2,1)}, f32[8,256]{1,0:T(8,128)}) custom-call(s32[2,1024]{1,0:T(2,128)} %bitcast.2, s32[2,1024]{1,0:T(2,128)} %bitcast.3, s32[2]{0:T(128)} %refs_2_.2, s32[784]{0:T(1024)} %refs_3_.2, f32[784,256]{1,0:T(8,128)} %refs_0_.1, f32[256,768]{1,0:T(8,128)} %refs_3_.3, ...), custom_call_target="tpu_custom_call" | custom-call | tf_op jit(solution)/shard_map/step/pallas_call | solution.py:1492
  114.2 8.9 %update.1 = (f32[2]{0:T(128)}, f32[3]{0:T(128)}, f32[1]{0:T(128)}, f32[784,256]{1,0:T(8,128)}, f32[784,256]{1,0:T(8,128)}, /*index=5*/f32[784,256]{1,0:T(8,128)}...) custom-call(f32[784,256]{1,0:T(8,128)} %get-tuple-element.28.table_g, ...), custom_call_target="tpu_custom_call" | custom-call | tf_op jit(solution)/shard_map/update/pallas_call | solution.py:1658

commit v5 on v4

--- a/solution.py
+++ b/solution.py
@@ -885,6 +885,13 @@
     fill(1, 1)
     count(0, 2)
     merge(0, 1)
+    for s in range(4):
+        rows = slice(s * span, (s + 1) * span)
+        pre = r.pre_s[rows, :]
+        inner = jnp.tanh(ROOT * (pre + 0.044715 * pre * pre * pre))
+        r.pre_s[rows, :] = 0.5 * (1.0 + inner) + 0.5 * pre * (1.0 - inner * inner) * (
+            ROOT * (1.0 + 3.0 * 0.044715 * pre * pre)
+        )
     merge(0, 2)
     total = r.stat_s[0, 1:2, :]
     log_total = r.stat_s[0, 0:1, :] + jnp.log(total)
@@ -927,12 +934,7 @@
         lanes = slice(s * span, (s + 1) * span)
         r.gf_s[s, 1] = across(r.act_s[:, lanes], up)
         grad_act = against(up, r.weights[s, 1])
-        pre = r.pre_s[s * span : (s + 1) * span, :]
-        inner = jnp.tanh(ROOT * (pre + 0.044715 * pre * pre * pre))
-        slope = 0.5 * (1.0 + inner) + 0.5 * pre * (1.0 - inner * inner) * (
-            ROOT * (1.0 + 3.0 * 0.044715 * pre * pre)
-        )
-        grad_pre = lowered(grad_act * slope)
+        grad_pre = lowered(grad_act * r.pre_s[s * span : (s + 1) * span, :])
         r.gf_s[s, 0] = dot(r.n2t_s[...], grad_pre)
         r.act_s[:, lanes] = grad_pre
     for i, s in enumerate((1, 3)):
@@ -962,6 +964,12 @@
     ended += [f_near, f_far, s_near, s_far, e_near, e_far]
     f_near.start()
 
+    grad_normed2 = against(
+        r.act_s[...], jnp.concatenate([r.weights[s, 0] for s in range(4)], 1)
+    )
+    grad_h1_norm, gain_grad2 = rms_back(r.h1_s[...], gain2, grad_normed2)
+    grad_h1 = r.h2_s[...] + grad_h1_norm
+    r.h1_s[...] = grad_h1
     tell.wait_recv()
     if kept(n_dp):
         for s in range(4):
@@ -1008,12 +1016,6 @@
     if middle:
         side_step(0)
 
-    grad_normed2 = against(
-        r.act_s[...], jnp.concatenate([r.weights[s, 0] for s in range(4)], 1)
-    )
-    grad_h1_norm, gain_grad2 = rms_back(r.h1_s[...], gain2, grad_normed2)
-    grad_h1 = r.h2_s[...] + grad_h1_norm
-    r.h1_s[...] = grad_h1
     f_near.wait_recv()
     for j in range(2):
         rows = slice(j * width, (j + 1) * width)
@@ -1361,6 +1363,17 @@
 
     strip_all.wait_recv()
     strip_all_side.start()
+    for copy in ended:
+        copy.wait_send()
+    ended.clear()
+
+    def end_line(k):
+        cand_line(k).wait_send()
+
+    each(1, n_z, end_line)
+
+    ffn_end()
+    strip_end()
 
     strip_all_side.wait_recv()
     c_base = wire.take(6)
@@ -1406,7 +1419,11 @@
     all_rows().wait_recv()
 
     if n_dp == several:
-        r.table_grad[...] = dot(r.owned[...], r.incoming[...])
+        for first in range(0, rows_dev, 208):
+            rows = slice(first, min(first + 208, rows_dev))
+            value = dot(r.owned[rows, :], r.incoming[...])
+            r.table_grad[rows, :] = value
+            squares = squares + total_of(value * value)
     else:
         r.table_grad[...] = jnp.zeros((rows_dev, width), FULL)
         r.padded_in[...] = jnp.zeros_like(r.padded_in)
@@ -1420,9 +1437,9 @@
             r.table_grad[...] = r.table_grad[...] + dot(r.owned[...], r.padded_in[...])
 
         loop(0, n_dp // several, add_rows)
+        table_grad = r.table_grad[...]
+        squares = squares + total_of(table_grad * table_grad)
     outs[1].start()
-    table_grad = r.table_grad[...]
-    squares = squares + total_of(table_grad * table_grad)
 
     r.small[3, 0] = jnp.broadcast_to(squares, (8, width))
     tell_norm = to_members(r.small.at[3], wire.take(1))
@@ -1457,13 +1474,6 @@
     all_shares(4, h_base + 1).wait_send()
 
 
-    def end_line(k):
-        cand_line(k).wait_send()
-
-    each(1, n_z, end_line)
-
-    ffn_end()
-    strip_end()
     early_relay.wait_recv()
     strip_relay.wait_recv()
     strip_out(3).start()

time: 124 us -> 124 us (level)
  no operation moved by 1% of the time
where the time goes in v5:
time: 124 us; the launch traced here: 123 us
  Pallas kernels  123 us (99%)
    pallas_call x1, Pallas kernels, step(): pl.pallas_call(functools.partial(step_kernel, n_dp, cap, names), out_shap...  114 us
    pallas_call x1, Pallas kernels, update(): pl.pallas_call(functools.partial(update_kernel, rows_dev), out_shape=tupl...  8.9 us

profile of v5, /device:TPU:0, one launch (start us, length us, event | category | flops | bytes accessed | tf_op | source)
XLA Modules:
  0.0 123.4 jit_solution(16604245954075207556)
XLA Ops:
  0.7 113.7 %step.1 = (f32[784,256]{1,0:T(8,128)}, bf16[512,256]{1,0:T(8,128)(2,1)}, bf16[4,384,256]{2,1,0:T(8,128)(2,1)}, f32[8,256]{1,0:T(8,128)}) custom-call(s32[2,1024]{1,0:T(2,128)} %bitcast.2, s32[2,1024]{1,0:T(2,128)} %bitcast.3, s32[2]{0:T(128)} %refs_2_.2, s32[784]{0:T(1024)} %refs_3_.2, f32[784,256]{1,0:T(8,128)} %refs_0_.1, f32[256,768]{1,0:T(8,128)} %refs_3_.3, ...), custom_call_target="tpu_custom_call" | custom-call | tf_op jit(solution)/shard_map/step/pallas_call | solution.py:1502
  114.3 8.9 %update.1 = (f32[2]{0:T(128)}, f32[3]{0:T(128)}, f32[1]{0:T(128)}, f32[784,256]{1,0:T(8,128)}, f32[784,256]{1,0:T(8,128)}, /*index=5*/f32[784,256]{1,0:T(8,128)}...) custom-call(f32[784,256]{1,0:T(8,128)} %get-tuple-element.28.table_g, ...), custom_call_target="tpu_custom_call" | custom-call | tf_op jit(solution)/shard_map/update/pallas_call | solution.py:1668

commit v6 on v5

--- a/solution.py
+++ b/solution.py
@@ -1638,8 +1638,8 @@
                     at_rows = slice((4 * u + m) * strip, (4 * u + m + 1) * strip)
                     grad = strips_s[m, (4 + u) * strip : (5 + u) * strip, :]
                     adam(6, at_rows, every, grad, LEARN)
-        for copy in copies_out:
-            copy.start()
+        for i, copy in enumerate(copies_out):
+            copy.start(priority=(number + i) % 2)
     adam(GAINS, every, every, sums[0:3, :], GAIN_LEARN)
     stats = sums[3:4, :]
     roots = jnp.sqrt(stats / (stats[:, 1:2] * float(width)))

time: 124 us -> 124 us (level)
  no operation moved by 1% of the time
where the time goes in v6:
time: 124 us; the launch traced here: 123 us
  Pallas kernels  123 us (99%)
    pallas_call x1, Pallas kernels, step(): pl.pallas_call(functools.partial(step_kernel, n_dp, cap, names), out_shap...  114 us
    pallas_call x1, Pallas kernels, update(): pl.pallas_call(functools.partial(update_kernel, rows_dev), out_shape=tupl...  8.91 us

profile of v6, /device:TPU:0, one launch (start us, length us, event | category | flops | bytes accessed | tf_op | source)
XLA Modules:
  0.0 123.4 jit_solution(9518029729733145819)
XLA Ops:
  0.7 113.7 %step.1 = (f32[784,256]{1,0:T(8,128)}, bf16[512,256]{1,0:T(8,128)(2,1)}, bf16[4,384,256]{2,1,0:T(8,128)(2,1)}, f32[8,256]{1,0:T(8,128)}) custom-call(s32[2,1024]{1,0:T(2,128)} %bitcast.2, s32[2,1024]{1,0:T(2,128)} %bitcast.3, s32[2]{0:T(128)} %refs_2_.2, s32[784]{0:T(1024)} %refs_3_.2, f32[784,256]{1,0:T(8,128)} %refs_0_.1, f32[256,768]{1,0:T(8,128)} %refs_3_.3, ...), custom_call_target="tpu_custom_call" | custom-call | tf_op jit(solution)/shard_map/step/pallas_call | solution.py:1502
  114.3 8.9 %update.1 = (f32[2]{0:T(128)}, f32[3]{0:T(128)}, f32[1]{0:T(128)}, f32[784,256]{1,0:T(8,128)}, f32[784,256]{1,0:T(8,128)}, /*index=5*/f32[784,256]{1,0:T(8,128)}...) custom-call(f32[784,256]{1,0:T(8,128)} %get-tuple-element.28.table_g, ...), custom_call_target="tpu_custom_call" | custom-call | tf_op jit(solution)/shard_map/update/pallas_call | solution.py:1668
